TPU v7x, 32 devices: a whole 2x2x4 slice. The times are simulated.
32 devices in a mesh: clouds: 16 (over z, y, x), points: 2 (over core).
Axes of the slice: x: 2, y: 2, z: 4, core: 2. Of those that a mesh axis runs over, the one named last changes fastest.
Arguments:
- features: float32 [64, 32768], P(None, ('clouds', 'points')), may hold values from -24 to 24
- lengths: int32 [64], P('clouds'), may hold values from 128 to 1664, as said below
- mask: int32 [32768], P(('clouds', 'points')), may hold values from 0 to 1, as said below
- neighbours: int32 [20, 32768], P(None, ('clouds', 'points')), may hold values from 0 to 2047, as said below
- first_layer_weight: float32 [128, 128], replicated, may hold values from -0.5 to 0.5
- first_norm_gain: float32 [128], replicated, may hold values from 0.5 to 1.5
- first_norm_bias: float32 [128], replicated, may hold values from -2.5 to 2.5
- second_layer_weight: float32 [256, 256], replicated, may hold values from -0.375 to 0.375
- second_norm_gain: float32 [256], replicated, may hold values from 0.5 to 1.5
- second_norm_bias: float32 [256], replicated, may hold values from -2.5 to 2.5
- pooled_grad: float32 [64, 512], P('clouds'), may hold values from -6 to 6
Outputs:
- pooled: float32 [64, 512], P('clouds')
- grad_features: float32 [64, 32768], P(None, ('clouds', 'points'))
- grad_weight_one: float32 [128, 128], replicated
- grad_gamma_one: float32 [128], replicated
- grad_beta_one: float32 [128], replicated
- grad_weight_two: float32 [256, 256], replicated
- grad_gamma_two: float32 [256], replicated
- grad_beta_two: float32 [256], replicated
Inputs may be any that keep to these rules, and one draw needn't show every extreme that they name: The 4 lengths of each cloud group sum to 2048; a group holds either four clouds of 384 to 768 points, or one cloud of exactly 1664 points and three of 128; at least one group is of the second kind. `neighbours`: each entry names a point of the same cloud as the point it belongs to, by its index within the cloud group. Every 1024-th point, beginning with the first, has mask 1.
All inputs are finite; a program needn't handle non-finite values.
Results may differ from a plain program's by a relative error of at most 0.0003.
Values sent between devices are 32-bit elements; how exact they have to be, the bound alone decides.
A program may use at most 128 MiB of HBM per device.

v0:
```python
import math

import jax
import jax.numpy as jnp
from jax import lax
from jax.sharding import PartitionSpec as P

EPSILON = 1e-05
FULL_ACCURACY = lax.Precision.HIGHEST


def combined_all(value, axis, join):
    pieces = jax.tree.map(lambda part: lax.all_gather(part, axis), value)
    head = jax.tree.map(lambda part: part[0], pieces)
    tail = jax.tree.map(lambda part: part[1:], pieces)
    total, _ = lax.scan(lambda total, piece: (join(total, piece), None), head, tail)
    return total


def product(left, right):
    return jnp.dot(left, right, precision=FULL_ACCURACY)


def gather_columns(table, neighbours):
    return jnp.take(table, neighbours, axis=1)


def scatter_columns(values, neighbours, group_size):
    start = jnp.zeros((values.shape[0], group_size), jnp.float32)
    return start.at[:, neighbours].add(values)


def edgeconv_forward(input_points, neighbours, active_mask, layer_weight, norm_gain, norm_bias):
    width = input_points.shape[0]
    depth = neighbours.shape[0]
    direct = layer_weight[:, :width]
    relative = layer_weight[:, width:]
    whole = lax.all_gather(input_points, "points", axis=1, tiled=True)
    spread = gather_columns(whole, neighbours) - input_points[:, None, :]
    edge_value_rows = product(direct, input_points)[:, None, :] + jnp.einsum(
        "cd,dkp->ckp", relative, spread, precision=FULL_ACCURACY
    )
    active_flag = active_mask[None, None, :]
    first, element_count = lax.psum(
        (jnp.sum(edge_value_rows * active_flag, axis=(1, 2)), jnp.sum(active_mask)),
        ("clouds", "points"),
    )
    total = element_count * depth
    channel_means = first / total
    centred = edge_value_rows - channel_means[:, None, None]
    channel_variance = (
        lax.psum(jnp.sum(centred * centred * active_flag, axis=(1, 2)), ("clouds", "points"))
        / total
    )
    scale = lax.rsqrt(channel_variance + EPSILON)
    normed = centred * scale[:, None, None]
    shifted = norm_gain[:, None, None] * normed + norm_bias[:, None, None]
    active = 0.2 * shifted + 0.8 * jax.nn.softplus(shifted)
    outputs = jax.nn.logsumexp(active, axis=1) - math.log(depth)
    return (outputs, (spread, normed, shifted, active, outputs, scale, total))


def edgeconv_backward(
    output_gradient, input_points, neighbours, active_mask, layer_weight, norm_gain, saved_residuals
):
    kept, normed, shifted, active, outputs, scale, total = saved_residuals
    depth = neighbours.shape[0]
    width = input_points.shape[0]
    direct = layer_weight[:, :width]
    relative = layer_weight[:, width:]
    group_size = input_points.shape[1] * lax.axis_size("points")
    shares = jnp.exp(active - (outputs + math.log(depth))[:, None, :])
    grad_shift = output_gradient[:, None, :] * shares * (0.2 + 0.8 * jax.nn.sigmoid(shifted))
    grad_beta, grad_gamma = lax.psum(
        (jnp.sum(grad_shift, axis=(1, 2)), jnp.sum(grad_shift * normed, axis=(1, 2))),
        ("clouds", "points"),
    )
    correction = (
        active_mask[None, None, :]
        * (grad_beta[:, None, None] + normed * grad_gamma[:, None, None])
        / total
    )
    grad_values = (norm_gain * scale)[:, None, None] * (grad_shift - correction)
    summed = jnp.sum(grad_values, axis=1)
    grad_direct = product(summed, input_points.T)
    grad_relative = jnp.einsum("ckp,dkp->cd", grad_values, kept, precision=FULL_ACCURACY)
    pushed = jnp.einsum("cd,ckp->dkp", relative, grad_values, precision=FULL_ACCURACY)
    scattered = scatter_columns(pushed, neighbours, group_size)
    arrived = lax.psum_scatter(scattered, "points", scatter_dimension=1, tiled=True)
    grad_inputs = product((direct - relative).T, summed) + arrived
    grad_weight = jnp.concatenate([grad_direct, grad_relative], axis=1)
    return (grad_inputs, grad_weight, grad_gamma, grad_beta)


def combine(first, second):
    top = jnp.maximum(first[0], second[0])
    mass = first[1] * jnp.exp(first[0] - top) + second[1] * jnp.exp(second[0] - top)
    return (top, mass, first[2] + second[2])


def on_device(
    features,
    lengths,
    mask,
    neighbours,
    first_layer_weight,
    first_norm_gain,
    first_norm_bias,
    second_layer_weight,
    second_norm_gain,
    second_norm_bias,
    pooled_grad,
):
    active_mask = mask.astype(jnp.float32)
    hidden_features, first_residuals = edgeconv_forward(
        features, neighbours, active_mask, first_layer_weight, first_norm_gain, first_norm_bias
    )
    final_output, second_residuals = edgeconv_forward(
        hidden_features,
        neighbours,
        active_mask,
        second_layer_weight,
        second_norm_gain,
        second_norm_bias,
    )
    share = features.shape[1]
    channels = final_output.shape[0]
    position = lax.axis_index("points") * share + jnp.arange(share, dtype=jnp.int32)
    ends = jnp.cumsum(lengths)
    starts = ends - lengths
    group_member = (position[None, :] >= starts[:, None]) & (position[None, :] < ends[:, None])
    membership = group_member.astype(jnp.float32)
    masked = jnp.where(group_member[:, None, :], final_output[None, :, :], -1e30)
    peaks = jnp.max(masked, axis=2)
    sums = jnp.sum(membership[:, None, :] * jnp.exp(masked - peaks[:, :, None]), axis=2)
    group_totals = product(membership, final_output.T)
    peak, mass, total_sum = combined_all((peaks, sums, group_totals), "points", combine)
    sizes = lengths.astype(jnp.float32)
    level = peak + jnp.log(mass)
    pooled = jnp.concatenate([level - jnp.log(sizes)[:, None], total_sum / sizes[:, None]], axis=1)
    grad_level = pooled_grad[:, :channels]
    grad_mean = pooled_grad[:, channels:] / sizes[:, None]
    pool_shares = membership[:, None, :] * jnp.exp(masked - level[:, :, None])
    final_output_gradient = jnp.einsum(
        "qc,qcp->cp", grad_level, pool_shares, precision=FULL_ACCURACY
    ) + product(grad_mean.T, membership)
    hidden_gradient, grad_weight_two, grad_gamma_two, grad_beta_two = edgeconv_backward(
        final_output_gradient,
        hidden_features,
        neighbours,
        active_mask,
        second_layer_weight,
        second_norm_gain,
        second_residuals,
    )
    grad_features, grad_weight_one, grad_gamma_one, grad_beta_one = edgeconv_backward(
        hidden_gradient,
        features,
        neighbours,
        active_mask,
        first_layer_weight,
        first_norm_gain,
        first_residuals,
    )
    grad_weight_one, grad_weight_two = lax.psum(
        (grad_weight_one, grad_weight_two), ("clouds", "points")
    )
    return (
        pooled,
        grad_features,
        grad_weight_one,
        grad_gamma_one,
        grad_beta_one,
        grad_weight_two,
        grad_gamma_two,
        grad_beta_two,
    )


def solution(mesh):
    in_specs = (
        P(None, ("clouds", "points")),
        P("clouds"),
        P(("clouds", "points")),
        P(None, ("clouds", "points")),
        P(),
        P(),
        P(),
        P(),
        P(),
        P(),
        P("clouds", None),
    )
    out_specs = (P("clouds", None), P(None, ("clouds", "points")), P(), P(), P(), P(), P(), P())
    return jax.shard_map(
        on_device, mesh=mesh, in_specs=in_specs, out_specs=out_specs, check_vma=False
    )
```

profile of v0, /device:TPU:0, one launch (start us, length us, event | category | flops | bytes accessed | tf_op | source)
XLA Modules:
  0.0 960.5 jit_solution(5840556544919661238)
XLA Ops:
  9.7 1.3 convert_reduce_fusion
  12.2 2.0 fusion.65
  14.2 2.6 all_gather.24
  16.9 68.0 %gather_fusion = f32[20480,64]{1,0:T(8,128)} fusion(f32[64,2048]{0,1:T(8,128)S(1)} %all_gather.24, s32[20480]{0:T(1024)S(1)} %broadcast_clamp_fusion), kind=kCustom, calls=%fused_computation | custom fusion | bytes 10567680 | tf_op jit(solution)/shard_map/jit(_take)/gather | solution.py:25
  84.8 9.1 copy.80
  94.0 21.2 %multiply_reduce_fusion.5 = (f32[128]{0:T(128)S(1)}, f32[20,1024,128]{2,1,0:T(8,128)}) fusion(f32[1024]{0:T(1024)S(1)} %convert_element_type.13, f32[128,1024]{0,1:T(8,128)S(1)} %fusion.65, f32[128,128]{1,0:T(8,128)S(1)} %copy-done.8, f32[20,1024,64]{1,2,0:T(8,128)} %copy.80, f32[64,1024]{1,0:T(8,128)S(1)} %copy-done.6, ...), kind=kOutput, calls=%fused_computation.28 | convolution fusion | flops 2023751552 | bytes 16605696 | tf_op jit(solution)/shard_map/cd,dkp->ckp/dot_general | solution.py:40
  115.1 42.3 %all-reduce.2 = (f32[128]{0:T(128)S(1)}, f32[]{:T(128)}) all-reduce(f32[128]{0:T(128)S(1)} %get-tuple-element.95, f32[]{:T(128)} %convert_reduce_fusion), channel_id=1, replica_groups=mesh['clouds'=16,'points'=2] {'clouds','points'}, use_global_device_ids=true, to_apply=%region_2.3 | all-reduce | flops 129 | bytes 1032 | tf_op jit(solution)/shard_map/psum | solution.py:44
  158.1 6.8 multiply_reduce_fusion.4
  164.9 40.3 %psum.82 = f32[128]{0:T(128)S(1)} all-reduce(f32[128]{0:T(128)S(1)} %multiply_reduce_fusion.4), channel_id=1, replica_groups=mesh['clouds'=16,'points'=2] {'clouds','points'}, use_global_device_ids=true, to_apply=%region_6.7 | all-reduce | flops 128 | bytes 1024 | tf_op jit(solution)/shard_map/psum | solution.py:52
  205.2 10.6 %fusion.70 = f32[128,1024]{0,1:T(8,128)S(1)} fusion(f32[128]{0:T(128)S(1)} %copy-done.16, f32[128]{0:T(128)S(1)} %get-tuple-element.76, f32[128]{0:T(128)S(1)} %broadcast_divide_fusion.1, f32[20,1024,128]{2,1,0:T(8,128)} %get-tuple-element.96, f32[128,1024]{0,1:T(8,128)S(1)} %fusion.65, f32[128]{0:T(128)S(1)} %copy-done.14), kind=kLoop, calls=%fused_computation.131 | loop fusion | flops 39190528 | bytes 11536384 | tf_op jit(solution)/shard_map/reduce_max | solution.py:59
  215.9 11.7 %exponential_reduce_fusion.1 = f32[128,1024]{0,1:T(8,128)S(1)} fusion(f32[128,1024]{0,1:T(8,128)S(1)} %is-finite_select_fusion.1, f32[128]{0:T(128)S(1)} %copy-done.16, f32[128]{0:T(128)S(1)} %get-tuple-element.76, f32[128]{0:T(128)S(1)} %broadcast_divide_fusion.1, f32[20,1024,128]{2,1,0:T(8,128)} %get-tuple-element.96, f32[128,1024]{0,1:T(8,128)S(1)} %fusion.65, ...), kind=kLoop, calls=%fused_computation.25 | loop fusion | flops 41811968 | bytes 12060672 | tf_op jit(solution)/shard_map/reduce_sum | solution.py:59
  228.8 1.2 copy.83
  232.2 6.2 all-gather.8.cloned.1.call-done
  238.4 69.2 %gather_fusion.1 = f32[20480,128]{1,0:T(8,128)} fusion(f32[128,2048]{0,1:T(8,128)} %all-gather.8.cloned.1.call-done, s32[20480]{0:T(1024)S(1)} %broadcast_clamp_fusion), kind=kCustom, calls=%fused_computation.1 | custom fusion | bytes 21053440 | tf_op jit(solution)/shard_map/jit(_take)/gather | solution.py:25
  307.6 11.4 %copy.82 = f32[20,1024,128]{1,2,0:T(8,128)} copy(f32[20,1024,128]{2,1,0:T(8,128)} %bitcast.150) | data formatting | bytes 20971520 | tf_op jit(solution)/shard_map/jit(_take)/gather | solution.py:25
  319.0 24.6 %multiply_reduce_fusion.2 = (f32[256]{0:T(256)S(1)}, f32[20,1024,256]{2,1,0:T(8,128)}) fusion(f32[1024]{0:T(1024)S(1)} %convert_element_type.13, f32[256,1024]{0,1:T(8,128)S(1)} %convolution_bitcast_fusion, f32[256,256]{1,0:T(8,128)S(1)} %copy-done.10, f32[20,1024,128]{1,2,0:T(8,128)} %copy.82, f32[128,1024]{1,0:T(8,128)S(1)} %copy.83, ...), kind=kOutput, calls=%fused_computation.15 | convolution fusion | flops 8074035200 | bytes 33190912 | tf_op jit(solution)/shard_map/cd,dkp->ckp/dot_general | solution.py:40
  343.6 40.5 %psum.83 = f32[256]{0:T(256)S(1)} all-reduce(f32[256]{0:T(256)S(1)} %get-tuple-element.97), channel_id=1, replica_groups=mesh['clouds'=16,'points'=2] {'clouds','points'}, use_global_device_ids=true, to_apply=%region_10.11 | all-reduce | flops 256 | bytes 2048 | tf_op jit(solution)/shard_map/psum | solution.py:44
  384.1 9.5 multiply_reduce_fusion.1
  393.6 40.5 %psum.84 = f32[256]{0:T(256)S(1)} all-reduce(f32[256]{0:T(256)S(1)} %multiply_reduce_fusion.1), channel_id=1, replica_groups=mesh['clouds'=16,'points'=2] {'clouds','points'}, use_global_device_ids=true, to_apply=%region_12.13 | all-reduce | flops 256 | bytes 2048 | tf_op jit(solution)/shard_map/psum | solution.py:52
  434.0 20.4 %fusion.71 = f32[256,1024]{0,1:T(8,128)S(1)} fusion(f32[256]{0:T(256)S(1)} %copy-done.15, f32[256]{0:T(256)S(1)} %get-tuple-element.81, f32[256]{0:T(256)S(1)} %broadcast_divide_fusion, f32[20,1024,256]{2,1,0:T(8,128)} %get-tuple-element.98, f32[256,1024]{0,1:T(8,128)S(1)} %convolution_bitcast_fusion, f32[256]{0:T(256)S(1)} %copy-done.12), kind=kLoop, calls=%fused_computation.132 | loop fusion | flops 78381056 | bytes 23072768 | tf_op jit(solution)/shard_map/reduce_max | solution.py:59
  454.5 19.3 %exponential_reduce_fusion = f32[256,1024]{0,1:T(8,128)S(1)} fusion(f32[256,1024]{0,1:T(8,128)S(1)} %is-finite_select_fusion, f32[256]{0:T(256)S(1)} %copy-done.15, f32[256]{0:T(256)S(1)} %get-tuple-element.81, f32[256]{0:T(256)S(1)} %broadcast_divide_fusion, f32[20,1024,256]{2,1,0:T(8,128)S(1)} %copy-done, f32[256,1024]{0,1:T(8,128)S(1)} %convolution_bitcast_fusion, ...), kind=kLoop, calls=%fused_computation.12 | loop fusion | flops 83623936 | bytes 24121344 | tf_op jit(solution)/shard_map/reduce_sum | solution.py:59
  473.8 1.6 broadcast_add_fusion
  475.4 1.6 copy.85
  478.5 1.8 all-gather.4
  480.3 2.0 all-gather.3
  483.2 9.7 %fusion.23 = f32[256,1,1024]{2,1,0:T(1,128)S(1)} fusion(f32[4,256,1]{0,2,1:T(1,128)} %copy.100, f32[4,256,1024]{2,1,0:T(8,128)S(1)} %fusion.22), kind=kOutput, calls=%fused_computation.50 | convolution fusion | flops 12582912 | bytes 5246976 | tf_op jit(solution)/shard_map/qc,qcp->cp/dot_general | solution.py:144
  492.9 1.8 convolution_add_fusion
  494.7 1.6 copy.86
  496.3 29.5 %fusion.72 = (f32[256]{0:T(256)S(1)}, f32[256]{0:T(256)S(1)}, f32[256,20,1024]{0,2,1:T(8,128)}) fusion(f32[256]{0:T(256)S(1)} %get-tuple-element.81, f32[256]{0:T(256)S(1)} %broadcast_divide_fusion, f32[20,1024,256]{2,1,0:T(8,128)} %get-tuple-element.98, f32[256,1024]{0,1:T(8,128)S(1)} %convolution_bitcast_fusion, f32[256,1024]{0,1:T(8,128)} %get-tuple-element.88, ...), kind=kLoop, calls=%fused_computation.133 | loop fusion | flops 131071488 | bytes 45094912 | tf_op jit(solution)/shard_map/reduce_sum | solution.py:75
  525.8 40.3 %all-reduce.1 = (f32[256]{0:T(256)S(1)}, f32[256]{0:T(256)S(1)}) all-reduce(f32[256]{0:T(256)S(1)} %get-tuple-element.62, f32[256]{0:T(256)S(1)} %get-tuple-element.61), channel_id=1, replica_groups=mesh['clouds'=16,'points'=2] {'clouds','points'}, use_global_device_ids=true, to_apply=%region_20.21 | all-reduce | flops 512 | bytes 4096 | tf_op jit(solution)/shard_map/psum | solution.py:74
  566.1 15.6 %fusion.76 = (f32[256,1024]{0,1:T(8,128)S(1)}, f32[256,20,1024]{0,2,1:T(8,128)S(1)}) fusion(f32[256,20,1024]{0,2,1:T(8,128)} %get-tuple-element.82, f32[]{:T(128)S(6)} %mul.204, f32[256]{0:T(256)S(1)} %get-tuple-element.67, f32[256]{0:T(256)S(1)} %get-tuple-element.81, f32[256]{0:T(256)S(1)} %broadcast_divide_fusion, ...), kind=kLoop, calls=%fused_computation.137 | loop fusion | flops 52166656 | bytes 65020932 | tf_op jit(solution)/shard_map/reduce_sum | solution.py:84
  581.7 18.7 %fusion.37 = f32[20,1024,128]{2,1,0:T(8,128)} fusion(f32[256,20,1024]{0,2,1:T(8,128)S(1)} %get-tuple-element.79, f32[256,256]{1,0:T(8,128)S(1)} %copy-done.10), kind=kOutput, calls=%fused_computation.77 | convolution fusion | flops 8053063680 | bytes 31588352 | tf_op jit(solution)/shard_map/cd,ckp->dkp/dot_general | solution.py:87
  600.5 110.2 %scatter_custom_fusion = f32[128,2048]{0,1:T(8,128)} fusion(s32[20480]{0:T(1024)} %copy-done.11, f32[20480,128]{1,0:T(8,128)} %bitcast.155, f32[]{:T(128)} %constant.38.clone.1), kind=kCustom, calls=%fused_computation.70 | custom fusion | flops 2621440 | bytes 1049088 | tf_op jit(solution)/shard_map/scatter-add | solution.py:30
  710.7 2.5 copy.87
  714.8 16.4 %fusion.31 = f32[256,128]{0,1:T(8,128)S(1)} fusion(f32[256,20,1024]{0,2,1:T(8,128)} %copy-done.1, f32[20,1024,128]{1,2,0:T(8,128)} %copy.82, f32[128,1024]{1,0:T(8,128)S(1)} %copy-done.5, pred[20,1024]{1,0:T(8,128)(4,1)S(1)} %compare_and_fusion), kind=kOutput, calls=%fused_computation.64 | convolution fusion | flops 8058306560 | bytes 32133120 | tf_op jit(solution)/shard_map/ckp,dkp->cd/dot_general | solution.py:86
  731.9 2.3 convolution_add_fusion.1
  734.4 16.4 %fusion.73 = (f32[128]{0:T(128)S(1)}, f32[128]{0:T(128)S(1)}, f32[128,20,1024]{0,2,1:T(8,128)}) fusion(f32[128]{0:T(128)S(1)} %get-tuple-element.76, f32[128]{0:T(128)S(1)} %broadcast_divide_fusion.1, f32[20,1024,128]{2,1,0:T(8,128)} %get-tuple-element.96, f32[128,1024]{0,1:T(8,128)S(1)} %fusion.65, f32[128,1024]{0,1:T(8,128)S(1)} %get-tuple-element.90, ...), kind=kLoop, calls=%fused_computation.134 | loop fusion | flops 65535744 | bytes 22547456 | tf_op jit(solution)/shard_map/reduce_sum | solution.py:75
  750.8 40.2 %all-reduce = (f32[128]{0:T(128)S(1)}, f32[128]{0:T(128)S(1)}) all-reduce(f32[128]{0:T(128)S(1)} %get-tuple-element.64, f32[128]{0:T(128)S(1)} %get-tuple-element.63), channel_id=1, replica_groups=mesh['clouds'=16,'points'=2] {'clouds','points'}, use_global_device_ids=true, to_apply=%region_27.28 | all-reduce | flops 256 | bytes 2048 | tf_op jit(solution)/shard_map/psum | solution.py:74
  791.0 10.0 %fusion.74 = (f32[128,1024]{0,1:T(8,128)S(1)}, f32[128,20,1024]{0,2,1:T(8,128)S(1)}) fusion(f32[128,20,1024]{0,2,1:T(8,128)} %get-tuple-element.77, f32[]{:T(128)S(6)} %mul.204, f32[128]{0:T(128)S(1)} %get-tuple-element.65, f32[128]{0:T(128)S(1)} %get-tuple-element.76, f32[128]{0:T(128)S(1)} %broadcast_divide_fusion.1, ...), kind=kLoop, calls=%fused_computation.135 | loop fusion | flops 26083328 | bytes 32512516 | tf_op jit(solution)/shard_map/reduce_sum | solution.py:84
  801.1 4.0 copy-done.2
  805.0 7.5 fusion.32
  813.9 13.0 %fusion.46 = f32[20,1024,64]{2,1,0:T(8,128)} fusion(f32[128,20,1024]{0,2,1:T(8,128)} %copy-done.2, f32[128,128]{1,0:T(8,128)S(1)} %copy-done.9), kind=kOutput, calls=%fused_computation.88 | convolution fusion | flops 2013265920 | bytes 15794176 | tf_op jit(solution)/shard_map/cd,ckp->dkp/dot_general | solution.py:87
  826.9 109.5 %scatter_custom_fusion.1 = f32[64,2048]{0,1:T(8,128)S(1)} fusion(s32[20480]{0:T(1024)} %copy-done.11, f32[20480,64]{1,0:T(8,128)} %bitcast.153, f32[]{:T(128)} %constant.38.clone.1), kind=kCustom, calls=%fused_computation.68 | custom fusion | flops 1310720 | bytes 524800 | tf_op jit(solution)/shard_map/scatter-add | solution.py:30
  938.3 1.8 all-gather.5
  940.7 1.6 copy.95
  942.3 1.8 copy.96
  944.1 7.3 reduce-scatter.5.cloned.1.call-done
  951.4 2.3 convolution_add_fusion.2
  (95 shorter events, 16.1 us)
Async XLA Ops:
  7.2 231.2 %all-gather.8.cloned.1.call-start = ((), (), s32[]{:S(2)}) async-start(), calls=%async_computation.2 | async-start | bytes 1572864 | tf_op jit(solution)/shard_map/all_gather | solution.py:38
  16.8 68.0 %copy-start.11 = (s32[20480]{0:T(1024)}, s32[20480]{0:T(1024)S(1)}, u32[]{:S(2)}) copy-start(s32[20480]{0:T(1024)S(1)} %reshape.238) | copy-start | bytes 245764
  84.8 9.1 copy-start.6
  84.8 9.1 copy-start.8
  94.0 111.2 %copy-start.14 = (f32[128]{0:T(128)S(1)}, f32[128]{0:T(128)}, u32[]{:S(2)}) copy-start(f32[128]{0:T(128)} %param.16) | copy-start | bytes 1540
  94.0 111.3 %copy-start.16 = (f32[128]{0:T(128)S(1)}, f32[128]{0:T(128)}, u32[]{:S(2)}) copy-start(f32[128]{0:T(128)} %param.17) | copy-start | bytes 1540
  215.9 14.2 %copy-start.13 = (f32[4,512]{1,0:T(4,128)S(1)}, f32[4,512]{1,0:T(4,128)}, u32[]{:S(2)}) copy-start(f32[4,512]{1,0:T(4,128)} %param.21) | copy-start | bytes 24580
  215.9 15.1 %copy-start.19 = (s32[4]{0:T(128)S(1)}, s32[4]{0:T(128)}, u32[]{:S(2)}) copy-start(s32[4]{0:T(128)} %param.12) | copy-start | bytes 52
  215.9 15.4 %copy-start.10 = (f32[256,256]{1,0:T(8,128)S(1)}, f32[256,256]{1,0:T(8,128)}, u32[]{:S(2)}) copy-start(f32[256,256]{1,0:T(8,128)} %param.18) | copy-start | bytes 786436
  228.6 503.3 %reduce-scatter.3.cloned.1.call-start = ((), (), s32[]{:S(2)}) async-start(), calls=%async_computation.3 | async-start | bytes 1572864 | tf_op jit(solution)/shard_map/reduce_scatter | solution.py:89
  230.1 88.9 %copy-start.4 = (f32[128,1024]{1,0:T(8,128)}, f32[128,1024]{1,0:T(8,128)S(1)}, u32[]{:S(2)}) copy-start(f32[128,1024]{1,0:T(8,128)S(1)} %copy.83) | copy-start | bytes 1572868
  384.1 50.0 %copy-start.12 = (f32[256]{0:T(256)S(1)}, f32[256]{0:T(256)}, u32[]{:S(2)}) copy-start(f32[256]{0:T(256)} %param.19) | copy-start | bytes 3076
  384.1 50.0 %copy-start.15 = (f32[256]{0:T(256)S(1)}, f32[256]{0:T(256)}, u32[]{:S(2)}) copy-start(f32[256]{0:T(256)} %param.20) | copy-start | bytes 3076
  434.0 20.5 %copy-start = (f32[20,1024,256]{2,1,0:T(8,128)S(1)}, f32[20,1024,256]{2,1,0:T(8,128)}, u32[]{:S(2)}) copy-start(f32[20,1024,256]{2,1,0:T(8,128)} %get-tuple-element.98) | copy-start | bytes 62914564
  566.1 15.6 %copy-start.17 = (f32[256]{0:T(256)}, f32[256]{0:T(256)S(1)}, u32[]{:S(2)}) copy-start(f32[256]{0:T(256)S(1)} %get-tuple-element.67) | copy-start | bytes 3076
  566.1 15.7 %copy-start.18 = (f32[256]{0:T(256)}, f32[256]{0:T(256)S(1)}, u32[]{:S(2)}) copy-start(f32[256]{0:T(256)S(1)} %get-tuple-element.68) | copy-start | bytes 3076
  581.7 18.7 %copy-start.1 = (f32[256,20,1024]{0,2,1:T(8,128)}, f32[256,20,1024]{0,2,1:T(8,128)S(1)}, u32[]{:S(2)}) copy-start(f32[256,20,1024]{0,2,1:T(8,128)S(1)} %get-tuple-element.79) | copy-start | bytes 62914564
  581.7 133.1 %copy-start.5 = (f32[128,1024]{1,0:T(8,128)S(1)}, f32[128,1024]{1,0:T(8,128)}, u32[]{:S(2)}) copy-start(f32[128,1024]{1,0:T(8,128)} %copy-done.4) | copy-start | bytes 1572868
  713.2 227.5 %all-reduce.6.cloned.1.call-start = ((), (), s32[]{:S(2)}) async-start(), calls=%async_computation.5 | async-start | bytes 655360 | tf_op jit(solution)/shard_map/psum | solution.py:165
  734.4 70.6 %slice-start = ((s8[5242880]{0:T(1024)(128)(4,1)}), s8[1048576]{0:T(1024)(128)(4,1)S(1)}, s32[]{:S(2)}) async-start(s8[5242880]{0:T(1024)(128)(4,1)} %bitcast.151), calls=%async_computation.6 | async-start | bytes 2097152
  791.0 10.0 %copy-start.20 = (f32[128]{0:T(128)}, f32[128]{0:T(128)S(1)}, u32[]{:S(2)}) copy-start(f32[128]{0:T(128)S(1)} %get-tuple-element.65) | copy-start | bytes 1540
  791.0 10.0 %copy-start.21 = (f32[128]{0:T(128)}, f32[128]{0:T(128)S(1)}, u32[]{:S(2)}) copy-start(f32[128]{0:T(128)S(1)} %get-tuple-element.66) | copy-start | bytes 1540
  791.0 14.0 %slice-start.1 = ((s8[5242880]{0:T(1024)(128)(4,1)}), s8[4194304]{0:T(1024)(128)(4,1)S(1)}, s32[]{:S(2)}) async-start(s8[5242880]{0:T(1024)(128)(4,1)} %bitcast.151), calls=%async_computation.7 | async-start | bytes 8388608
  791.0 14.0 %copy-start.7 = (f32[64,1024]{1,0:T(8,128)S(1)}, f32[64,1024]{1,0:T(8,128)}, u32[]{:S(2)}) copy-start(f32[64,1024]{1,0:T(8,128)} %param.11) | copy-start | bytes 786436
  801.0 4.0 copy-start.2
  801.0 12.8 %copy-start.9 = (f32[128,128]{1,0:T(8,128)S(1)}, f32[128,128]{1,0:T(8,128)}, u32[]{:S(2)}) copy-start(f32[128,128]{1,0:T(8,128)} %param.15) | copy-start | bytes 196612
  813.6 124.2 %copy-start.3 = (f32[256,1024]{0,1:T(8,128)S(1)}, f32[256,1024]{0,1:T(8,128)}, u32[]{:S(2)}) copy-start(f32[256,1024]{0,1:T(8,128)} %get-tuple-element.88) | copy-start | bytes 3145732
  813.6 137.8 %reduce-scatter.5.cloned.1.call-start = ((), (), s32[]{:S(2)}) async-start(), calls=%async_computation.4 | async-start | bytes 786432 | tf_op jit(solution)/shard_map/reduce_scatter | solution.py:89
Sparse Core Ops, SparseCore 0:
  228.7 9.6 all-gather.7
  713.4 8.3 reduce-scatter.2
  813.7 126.5 all-reduce.5
  942.5 8.9 reduce-scatter.4
where the time goes:
time: 970 us; the launch traced here: 961 us
  other arithmetic  381 us (39%)
  blocking collectives  252 us (26%)
  local copies, waits for them, and re-layouts  175 us (18%)
  matrix products  122 us (13%)
  between operations  15.1 us (2%)
  waiting for transfers between devices  13.5 us (1%)
    scatter-add x2, other arithmetic, scatter_columns(): return start.at[:, neighbours].add(values)  220 us
    gather x4, local copies, waits for them, and re-layouts, gather_columns(): return jnp.take(table, neighbours, axis=1)  158 us
    psum x2, blocking collectives, edgeconv_forward(): lax.psum((jnp.sum(edge_value_rows * active_flag, axis=(1, 2)), jnp.sum(ac...  82.8 us
    psum x2, blocking collectives, edgeconv_forward(): lax.psum(jnp.sum(centred * centred * active_flag, axis=(1, 2)), ('clouds'...  80.8 us
    psum x2, blocking collectives, edgeconv_backward(): lax.psum((jnp.sum(grad_shift, axis=(1, 2)), jnp.sum(grad_shift * normed,...  80.5 us
    reduce_sum x2, other arithmetic, edgeconv_backward(): jnp.sum(grad_shift, axis=(1, 2))  45.9 us
    dot_general x2, matrix products, edgeconv_forward(): jnp.einsum('cd,dkp->ckp', relative, spread, precision=FULL_ACCURACY)  45.8 us
    dot_general x2, matrix products, edgeconv_backward(): jnp.einsum('cd,ckp->dkp', relative, grad_values, precision=FULL_ACCURACY)  31.7 us
  transfers between devices with their start and end apart: 4, of which 2 were waited for; matrix products, arithmetic and copies ran while one was open for 16% of the time, Pallas kernels for 0%

commit v1 on v0

v1 whole, which is shorter than its diff:
```python
import functools
import math

import jax
import jax.numpy as jnp
from jax import lax
from jax.experimental import pallas as pl
from jax.experimental.pallas import tpu as pltpu
from jax.sharding import PartitionSpec as P

EPSILON = 1e-05
LOG2E = math.log2(math.e)
LN2 = math.log(2.0)
MESH = pl.DeviceIdType.MESH
F32 = jnp.float32
BF16 = jnp.bfloat16
LANES = 128
SUBLANES = 8
CHUNK = 256
MEMORY = 60 * 2**20
VMEM = pl.BlockSpec(memory_space=pltpu.VMEM)
SMEM = pl.BlockSpec(memory_space=pltpu.SMEM)


def dot(left, right, dims):
    return lax.dot_general(
        left,
        right,
        (dims, ((), ())),
        precision=lax.Precision.HIGHEST,
        preferred_element_type=F32,
    )


def mm(left, right):
    return dot(left, right, ((1,), (0,)))


def mm_nt(left, right):
    return dot(left, right, ((1,), (1,)))


def mm_tn(left, right):
    return dot(left, right, ((0,), (0,)))


def mm_low(left, right):
    return lax.dot_general(
        left, right, (((1,), (0,)), ((), ())), preferred_element_type=F32
    )


def split(value):
    high = value.astype(BF16)
    low = (value - high.astype(F32)).astype(BF16)
    return high, low


def over(count, step, body):
    def run(i, carry):
        body(pl.multiple_of(i * step, step))
        return carry

    lax.fori_loop(0, count // step, run, 0)


def log2(value):
    return jnp.log(value) * LOG2E


def tree(values, join):
    values = list(values)
    while len(values) > 1:
        values = [
            join(values[i], values[i + 1]) if i + 1 < len(values) else values[i]
            for i in range(0, len(values), 2)
        ]
    return values[0]


def iota(shape, dim):
    return lax.broadcasted_iota(jnp.int32, shape, dim)


def signal_all(barrier, cores, total):
    me = lax.axis_index("clouds") * cores + lax.axis_index("points")

    def send(d, carry):
        t = lax.rem(me + d, total)
        pl.semaphore_signal(
            barrier,
            inc=1,
            device_id=(lax.div(t, cores), lax.rem(t, cores)),
            device_id_type=MESH,
        )
        return carry

    lax.fori_loop(1, total, send, 0)


def gather_start(own, slots, send_sem, recv_sem, cores, total):
    me = lax.axis_index("clouds") * cores + lax.axis_index("points")
    slots[me] = own[...]

    def send(d, carry):
        t = lax.rem(me + d, total)
        pltpu.make_async_remote_copy(
            src_ref=own,
            dst_ref=slots.at[me],
            send_sem=send_sem,
            recv_sem=recv_sem,
            device_id=(lax.div(t, cores), lax.rem(t, cores)),
            device_id_type=MESH,
        ).start()
        return carry

    lax.fori_loop(1, total, send, 0)


def gather_wait(slots, send_sem, recv_sem, total):
    others = slots.at[pl.ds(0, total - 1)]
    arrived = pltpu.make_async_remote_copy(
        src_ref=others,
        dst_ref=others,
        send_sem=send_sem,
        recv_sem=recv_sem,
        device_id=(lax.axis_index("clouds"), 1 - lax.axis_index("points")),
        device_id_type=MESH,
    )
    arrived.wait_recv()
    arrived.wait_send()


def slot_sum(slots, total):
    def add(i, carry):
        return carry + slots[i]

    return lax.fori_loop(1, total, add, slots[0])


def to_partner(source, target, sems, index):
    return pltpu.make_async_remote_copy(
        src_ref=source,
        dst_ref=target,
        send_sem=sems.at[0, index],
        recv_sem=sems.at[1, index],
        device_id=(lax.axis_index("clouds"), 1 - lax.axis_index("points")),
        device_id_type=MESH,
    )


def edge_pass(subs, block, depth, part, index, table, own_rows, out_hbm, held, ring, sems, outs):
    level_ref, share_ref, moment_ref, inverse_ref = outs
    per = SUBLANES // subs
    groups = own_rows.shape[0] // SUBLANES
    stages = depth // part
    row = iota((SUBLANES, LANES), 0)
    mine = [(row >= subs * i) & (row < subs * (i + 1)) for i in range(per)]
    zero = jnp.zeros((SUBLANES, LANES), F32)

    def fetch(group, stage, slot):
        for k in range(part):
            target = held[slot].at[stage * part + k]
            for i in range(per):
                first = (k * per + i) * groups
                if stages > 1:
                    span = groups * (1 + (stages - 1) * part * per)
                    j = index.at[pl.ds(first, span)][stage * (part * per * groups) + group]
                else:
                    j = index.at[pl.ds(first, groups)][group]
                value = table[pl.ds(j, SUBLANES), :]
                if i == 0:
                    target[...] = value
                else:
                    pltpu.store(target, value, mask=mine[i])

    def work(group, stage, slot, ring_slot, place, carry):
        total0, share0, moment0 = carry
        rows = pl.ds(pl.multiple_of(group * SUBLANES, SUBLANES), SUBLANES)
        peak = tree([held[slot][k] for k in range(depth)], jnp.maximum)
        top = own_rows[rows, :] + peak
        shift = jnp.maximum(top, 0.0)
        rest = jnp.maximum(jnp.exp2(-shift), 2.0**-100)
        scale = jnp.exp2(top - shift)
        fifth = 0.2 * rest
        total, share, moment = [], [], []
        for k in range(part):
            value = held[slot][stage * part + k]
            away = value - peak
            grown = scale * jnp.exp2(away)
            root = jnp.exp2((away - log2(rest + grown)) * 0.2)
            weight = root * (fifth + grown)
            ring[ring_slot, place, stage * part + k] = weight
            total.append(root)
            share.append(weight)
            moment.append(weight * value)
        total, share, moment = [
            functools.reduce(jnp.add, parts) for parts in (total, share, moment)
        ]
        if stages > 1:
            start = stage == 0
            total = total + jnp.where(start, 0.0, total0)
            share = share + jnp.where(start, 0.0, share0)
            moment = moment + jnp.where(start, 0.0, moment0)
        mass = share + (0.8 * rest) * total
        inverse = 1.0 / mass
        level_ref[rows, :] = LN2 * (0.2 * top + 0.8 * shift + log2(mass)) - math.log(depth)
        inverse_ref[rows, :] = inverse
        share_ref[rows, :] = share * inverse
        moment_ref[rows, :] = moment * inverse
        return total, share, moment

    blocks = groups // block

    def push(b, slot):
        return pltpu.make_async_copy(
            ring.at[slot], out_hbm.at[pl.ds(b * block, block)], sems.at[slot]
        )

    for stage in range(stages):
        fetch(0, stage, 0)

    def one_block(b, carry):
        ring_slot = lax.rem(b, 2)

        @pl.when(b >= 2)
        def _():
            push(b - 2, ring_slot).wait()

        def pair(t, inner):
            for slot in range(2):
                place = t * 2 + slot
                group = b * block + place
                after = jnp.minimum(group + 1, groups - 1)
                if stages == 1:
                    work(group, 0, slot, ring_slot, place, (zero,) * 3)
                    fetch(after, 0, 1 - slot)
                else:

                    def one_stage(stage, sums):
                        sums = work(group, stage, slot, ring_slot, place, sums)
                        fetch(after, stage, 1 - slot)
                        return sums

                    lax.fori_loop(0, stages, one_stage, (zero,) * 3)
            return inner

        lax.fori_loop(0, block // 2, pair, 0)
        push(b, ring_slot).start()
        return carry

    lax.fori_loop(0, blocks, one_block, 0)
    if blocks > 1:
        push(blocks - 2, (blocks - 2) % 2).wait()
    push(blocks - 1, (blocks - 1) % 2).wait()


def lanes_to_rows(value, width):
    return [value[:, i * LANES : (i + 1) * LANES] for i in range(width // LANES)]


def rows_to_lanes(rows):
    return rows[0] if len(rows) == 1 else jnp.concatenate(rows, axis=1)


def forward_kernel(
    sizes,
    feat,
    near,
    live,
    index1,
    index2,
    lengths,
    weight1,
    gain1,
    bias1,
    weight2,
    gain2,
    bias2,
    pooled_grad,
    pooled,
    q1,
    q2,
    inverse1,
    share1,
    moment1,
    x1,
    away_own1,
    away_all1,
    counts,
    scales1,
    push2,
    extra2,
    x2_out,
    own2,
    grad_own2,
    scales2,
    x1_cm,
    links,
    live_col,
    parts1,
    parts2,
    u1,
    v1,
    n1,
    g1,
    table1,
    own_rows1,
    level1,
    table2,
    own_rows2,
    level2,
    share2,
    moment2,
    inverse2,
    x2,
    u2,
    v2,
    g2,
    xm,
    pool_parts,
    message,
    slots,
    held0,
    held1,
    ring,
    pair_sems,
    all_sems,
    ring_sems,
):
    cores, total = sizes
    points = feat.shape[1]
    cin = feat.shape[0]
    both = cores * points
    depth = near.shape[0]
    width1 = weight1.shape[0]
    width2 = weight2.shape[0]
    core = lax.axis_index("points")
    half = pl.multiple_of(core * points, points)
    barrier = pltpu.get_barrier_semaphore()
    signal_all(barrier, cores, total)

    row16 = iota((16, LANES), 0)
    one, none = jnp.ones((16, LANES), BF16), jnp.zeros((16, LANES), BF16)

    def build(columns):
        names = [near[k, :, columns] for k in range(depth)]

        def rows16(start):
            target = (row16 + start).astype(jnp.int16)
            found = [jnp.where(name == target, one, none) for name in names]
            links[pl.ds(start, 16), columns] = functools.reduce(jnp.add, found)

        over(both, 16, rows16)

    for tile in range(points // LANES):
        build(pl.ds(tile * LANES, LANES))

    x1_cm[core] = feat[...]
    pl.semaphore_wait(barrier, total - 1)
    swap = to_partner(feat, x1_cm.at[core], pair_sems, 0)
    swap.start()
    live_col[...] = jnp.broadcast_to(jnp.transpose(live[...])[:, :1], live_col.shape)
    swap.wait()

    direct1 = weight1[:, :cin] - weight1[:, cin:]
    relative1 = weight1[:, cin:]
    for c in range(cores):

        def turn(start):
            x1[pl.ds(c * points + start, CHUNK), :] = jnp.transpose(
                x1_cm[c, :, pl.ds(start, CHUNK)]
            )

        over(points, CHUNK, turn)
        value = x1_cm[c]
        high, low = split(value)
        lower = (value - high.astype(F32) - low.astype(F32)).astype(BF16)
        parts1[c, 0:cin, :] = high
        parts1[c, cin : 2 * cin, :] = low
        parts1[c, 2 * cin : 3 * cin, :] = lower

    def sums_near1(start):
        columns = pl.ds(start, CHUNK)
        value = mm_low(parts1[0], links[0:points, columns])
        for c in range(1, cores):
            value = value + mm_low(parts1[c], links[c * points : (c + 1) * points, columns])
        value = value[0:cin] + value[cin : 2 * cin] + value[2 * cin : 3 * cin]
        n1[columns, :] = jnp.transpose(value)

    over(points, CHUNK, sums_near1)

    own_high, own_low = split(x1_cm[core])
    both_parts = jnp.concatenate([own_high.astype(F32), own_low.astype(F32)], axis=0)
    x_parts = jnp.transpose(both_parts).astype(BF16)
    ones = jnp.ones((points, LANES), BF16)

    def linked1(start):
        rows = pl.ds(start, CHUNK)
        xm[rows, :] = mm_low(links[rows, :], x_parts)
        counts[rows, :] = mm_low(links[rows, :], ones)

    over(both, CHUNK, linked1)

    live_rows = live[...]
    live_sum = jnp.sum(live[0:1, :], axis=1, keepdims=True)
    mine = live_sum * depth

    def statistics(x_all, n_ref, direct, relative, u, v, g, width):
        def outer(start):
            rows = pl.ds(start, CHUNK)
            v[rows, :] = mm_nt(x_all[rows, :], relative)

        over(both, CHUNK, outer)

        def inner(start):
            rows = pl.ds(start, CHUNK)
            u[rows, :] = mm_nt(x_all[pl.ds(half + start, CHUNK), :], direct)
            g[rows, :] = mm_nt(n_ref[rows, :], relative)

        over(points, CHUNK, inner)
        u_sum = mm(live_rows, u[...])[0:1]
        g_sum = jnp.sum(g[...], axis=0, keepdims=True)
        u_mean = u_sum / live_sum
        v_mean = g_sum / mine
        centred = u[...] - u_mean
        spread = depth * centred * centred + 2.0 * centred * (g[...] - depth * v_mean)
        square = mm(live_rows, spread)[0:1]
        weights = rows_to_lanes([counts[...]] * (width // LANES))
        away = v[...] - v_mean
        square = square + jnp.sum(weights * away * away, axis=0, keepdims=True)
        return depth * u_sum + g_sum, square, v_mean

    def send_sums(use, rows):
        for i, value in enumerate(rows):
            message[use, i : i + 1, :] = value
        gather_start(
            message.at[use], slots.at[use], all_sems.at[0, use], all_sems.at[1, use], cores, total
        )

    def receive(use):
        gather_wait(slots.at[use], all_sems.at[0, use], all_sems.at[1, use], total)

    def combine(use, numbers, width):
        per = width // LANES
        count = numbers[0]
        for value in numbers[1:]:
            count = count + value

        def value_of(i, first):
            return rows_to_lanes([slots[use, i, first + h : first + h + 1, :] for h in range(per)])

        mean = value_of(0, 0)
        for i in range(1, total):
            mean = mean + value_of(i, 0)
        mean = mean / count
        square = None
        for i in range(total):
            gap = value_of(i, 0) / numbers[i] - mean
            term = value_of(i, per) + numbers[i] * gap * gap
            square = term if square is None else square + term
        return count, mean, square / count

    sums, square, v_mean1 = statistics(x1, n1, direct1, relative1, u1, v1, g1, width1)
    send_sums(0, [sums, square, jnp.broadcast_to(mine, (1, LANES)), jnp.zeros((1, LANES), F32)])
    receive(0)
    numbers = [slots[0, i, 2:3, 0:1] for i in range(total)]
    count, mean1, variance1 = combine(0, numbers, width1)
    r1 = lax.rsqrt(variance1 + EPSILON)
    slope1 = gain1[...] * r1
    scales1[...] = jnp.concatenate(
        [slope1, r1, jnp.broadcast_to(count, (1, LANES)), jnp.zeros((5, LANES), F32)], axis=0
    )

    def fill1(start):
        rows = pl.ds(start, CHUNK)
        table1[pl.ds(SUBLANES + start, CHUNK), :] = (v1[rows, :] - v_mean1) * (slope1 * LOG2E)
        shared = mm_nt(xm[rows, 0:cin] + xm[rows, cin : 2 * cin], direct1)
        away_all1[rows, :] = shared + counts[rows, :] * (v1[rows, :] - mean1)

    over(both, CHUNK, fill1)

    def fill_own1(start):
        rows = pl.ds(start, CHUNK)
        own_rows1[rows, :] = (u1[rows, :] - (mean1 - v_mean1)) * (slope1 * LOG2E) + bias1[
            ...
        ] * LOG2E
        away_own1[rows, :] = depth * live_col[rows, :] * (u1[rows, :] - mean1) + g1[rows, :]

    over(points, CHUNK, fill_own1)

    edge_pass(
        1,
        ring.shape[1],
        depth,
        depth // 2,
        index1,
        table1,
        own_rows1,
        q1,
        (held0, held1),
        ring,
        ring_sems,
        (level1, share1, moment1, inverse1),
    )

    def hidden(start):
        rows = pl.ds(start, CHUNK)
        x2[pl.ds(half + start, CHUNK), :] = level1[rows, :]
        offset = own_rows1[rows, :] - bias1[...] * LOG2E
        moment1[rows, :] = (share1[rows, :] * offset + moment1[rows, :]) / (gain1[...] * LOG2E)

    over(points, CHUNK, hidden)
    here = x2.at[pl.ds(half, points)]
    swap = to_partner(here, here, pair_sems, 1)
    swap.start()
    swap.wait()

    direct2 = weight2[:, :width1] - weight2[:, width1:]
    relative2 = weight2[:, width1:]

    def turn2(start):
        high, low = split(jnp.transpose(x2[pl.ds(start, CHUNK), :]))
        parts2[0:width1, pl.ds(start, CHUNK)] = high
        parts2[width1 : 2 * width1, pl.ds(start, CHUNK)] = low

    over(both, CHUNK, turn2)

    def sums_near2(start):
        columns = pl.ds(start, CHUNK)
        value = mm_low(parts2[...], links[:, columns])
        value = value[0:width1] + value[width1 : 2 * width1]
        g2[columns, :] = mm_nt(jnp.transpose(value), relative2)

    over(points, CHUNK, sums_near2)

    def statistics2():
        def outer(start):
            rows = pl.ds(start, CHUNK)
            v2[rows, :] = mm_nt(x2[rows, :], relative2)
            x2_out[rows, :] = x2[rows, :]

        over(both, CHUNK, outer)

        def inner(start):
            u2[pl.ds(start, CHUNK), :] = mm_nt(x2[pl.ds(half + start, CHUNK), :], direct2)

        over(points, CHUNK, inner)
        u_sum = jnp.zeros((1, width2), F32)
        g_sum = jnp.zeros((1, width2), F32)
        for s in range(0, points, CHUNK):
            u_sum = u_sum + mm(live[:, s : s + CHUNK], u2[s : s + CHUNK, :])[0:1]
            g_sum = g_sum + jnp.sum(g2[s : s + CHUNK, :], axis=0, keepdims=True)
        u_mean = u_sum / live_sum
        v_mean = g_sum / mine
        square = jnp.zeros((1, width2), F32)
        for s in range(0, points, CHUNK):
            centred = u2[s : s + CHUNK, :] - u_mean
            spread = depth * centred * centred + 2.0 * centred * (
                g2[s : s + CHUNK, :] - depth * v_mean
            )
            square = square + mm(live[:, s : s + CHUNK], spread)[0:1]

        def squares(i, carry):
            rows = pl.ds(pl.multiple_of(i * CHUNK, CHUNK), CHUNK)
            away = v2[rows, :] - v_mean
            weights = rows_to_lanes([counts[rows, :]] * (width2 // LANES))
            return carry + jnp.sum(weights * away * away, axis=0, keepdims=True)

        square = lax.fori_loop(0, both // CHUNK, squares, square)
        return depth * u_sum + g_sum, square, v_mean

    sums, square, v_mean2 = statistics2()
    send_sums(1, lanes_to_rows(sums, width2) + lanes_to_rows(square, width2))
    receive(1)
    count, mean2, variance2 = combine(1, numbers, width2)
    r2 = lax.rsqrt(variance2 + EPSILON)
    slope2 = gain2[...] * r2
    scales2[...] = jnp.concatenate([slope2, jnp.zeros((7, width2), F32)], axis=0)

    def fill2(start):
        rows = pl.ds(start, CHUNK)
        value = (v2[rows, :] - v_mean2) * (slope2 * LOG2E)
        for h in range(2):
            table2[pl.ds(SUBLANES + 2 * start + h, CHUNK, stride=2), :] = value[
                :, h * LANES : (h + 1) * LANES
            ]

    over(both, CHUNK, fill2)

    def fill_own2(start):
        rows = pl.ds(start, CHUNK)
        value = (u2[rows, :] - (mean2 - v_mean2)) * (slope2 * LOG2E) + bias2[...] * LOG2E
        for h in range(2):
            own_rows2[pl.ds(2 * start + h, CHUNK, stride=2), :] = value[
                :, h * LANES : (h + 1) * LANES
            ]

    over(points, CHUNK, fill_own2)

    edge_pass(
        2,
        ring.shape[1],
        depth,
        depth,
        index2,
        table2,
        own_rows2,
        q2,
        (held0, held1),
        ring,
        ring_sems,
        (level2, share2, moment2, inverse2),
    )

    clouds = pooled_grad.shape[0]
    starts, ends = [], []
    end = jnp.int32(0)
    for q in range(clouds):
        starts.append(end)
        end = end + lengths[q]
        ends.append(end)
    row = iota((SUBLANES, LANES), 0)
    odd = lax.rem(row, 2) == 1
    point_of_row = lax.div(row, 2)
    steps = level2.shape[0] // SUBLANES
    lowest = jnp.full((SUBLANES, LANES), -1e30, F32)
    zero = jnp.zeros((SUBLANES, LANES), F32)

    def members(t):
        position = point_of_row + (half + t * (SUBLANES // 2))
        return [(position >= starts[q]) & (position < ends[q]) for q in range(clouds)]

    def step_rows(t):
        return pl.ds(pl.multiple_of(t * SUBLANES, SUBLANES), SUBLANES)

    def by_parity(value, join):
        value = join(value, pltpu.roll(value, 2, 0))
        return join(value, pltpu.roll(value, 4, 0))

    def peaks(t, carry):
        value = level2[step_rows(t), :]
        inside = members(t)
        out = []
        for q in range(clouds):
            out.append(jnp.maximum(carry[q], jnp.where(inside[q], value, lowest)))
        for q in range(clouds):
            out.append(carry[clouds + q] + jnp.where(inside[q], value, zero))
        return tuple(out)

    state = lax.fori_loop(0, steps, peaks, (lowest,) * clouds + (zero,) * clouds)
    peak = [by_parity(value, jnp.maximum) for value in state[:clouds]]
    sums = [by_parity(value, jnp.add) for value in state[clouds:]]

    def pick(inside, values):
        value = values[0]
        for q in range(1, clouds):
            value = jnp.where(inside[q], values[q], value)
        return value

    def masses(t, carry):
        inside = members(t)
        value = jnp.exp(level2[step_rows(t), :] - pick(inside, peak))
        return tuple(carry[q] + jnp.where(inside[q], value, zero) for q in range(clouds))

    state = lax.fori_loop(0, steps, masses, (zero,) * clouds)
    mass = [by_parity(value, jnp.add) for value in state]
    for q in range(clouds):
        pool_parts[core, 3 * q] = peak[q]
        pool_parts[core, 3 * q + 1] = mass[q]
        pool_parts[core, 3 * q + 2] = sums[q]
    here = pool_parts.at[core]
    swap = to_partner(here, here, pair_sems, 2)
    swap.start()
    swap.wait()

    level, grad_level, grad_mean = [], [], []
    for q in range(clouds):
        top = pool_parts[0, 3 * q]
        for c in range(1, cores):
            top = jnp.maximum(top, pool_parts[c, 3 * q])
        whole, sum_all = zero, zero
        for c in range(cores):
            whole = whole + pool_parts[c, 3 * q + 1] * jnp.exp(pool_parts[c, 3 * q] - top)
            sum_all = sum_all + pool_parts[c, 3 * q + 2]
        level.append(top + jnp.log(whole))
        size = jnp.full((SUBLANES, LANES), lengths[q].astype(F32), F32)
        first = level[q] - jnp.log(size)
        second = sum_all / size
        for h in range(2):
            pooled[q : q + 1, h * LANES : (h + 1) * LANES] = first[h : h + 1]
            pooled[q : q + 1, (2 + h) * LANES : (3 + h) * LANES] = second[h : h + 1]
        given = [pooled_grad[q : q + 1, h * LANES : (h + 1) * LANES] for h in range(4)]
        grad_level.append(jnp.where(odd, given[1], given[0]))
        grad_mean.append(jnp.where(odd, given[3], given[2]) / size)

    slope_rows, bias_rows = [], []
    for ref_value, target in ((gain2[...], slope_rows), (bias2[...], bias_rows)):
        low_half, high_half = lanes_to_rows(ref_value * LOG2E, width2)
        target.append(jnp.where(odd, high_half, low_half))
    inverse_gain = 1.0 / slope_rows[0]
    bias_row = bias_rows[0]

    def gradient(t, carry):
        rows = step_rows(t)
        inside = members(t)
        value = pick(inside, grad_level) * jnp.exp(level2[rows, :] - pick(inside, level))
        value = value + pick(inside, grad_mean)
        push2[rows, :] = value * inverse2[rows, :]
        share = share2[rows, :]
        moment = (share * (own_rows2[rows, :] - bias_row) + moment2[rows, :]) * inverse_gain
        given = value * share
        share2[rows, :] = given
        return carry[0] + given, carry[1] + value * moment

    state = lax.fori_loop(0, steps, gradient, (zero, zero))
    grad_beta, grad_gamma = [by_parity(value, jnp.add) for value in state]
    send_sums(2, [grad_beta[0:1], grad_beta[1:2], grad_gamma[0:1], grad_gamma[1:2]])

    x_high, x_low = split(x2[pl.ds(half, points), :])

    def linked2(start):
        rows = pl.ds(start, CHUNK)
        value = mm_low(links[rows, :], x_high) + mm_low(links[rows, :], x_low)
        weights = rows_to_lanes([counts[rows, :]] * 2)
        v2[rows, :] = mm_nt(value, direct2) + weights * (v2[rows, :] - mean2)

    over(both, CHUNK, linked2)
    receive(2)
    sums = slot_sum(slots.at[2], total)
    grad_beta = rows_to_lanes([sums[0:1], sums[1:2]])
    grad_gamma = rows_to_lanes([sums[2:3], sums[3:4]])
    scales2[1:2, :] = grad_beta
    scales2[2:3, :] = grad_gamma
    outer_scale = slope2 / count
    gamma_scale = outer_scale * grad_gamma * r2
    beta_scale = outer_scale * grad_beta

    def extra(start):
        rows = pl.ds(start, CHUNK)
        weights = rows_to_lanes([counts[rows, :]] * 2)
        extra2[rows, :] = weights * beta_scale + v2[rows, :] * gamma_scale

    over(both, CHUNK, extra)
    grad_own2[...] = jnp.zeros(grad_own2.shape, F32)

    def own(start):
        rows = pl.ds(start, CHUNK)
        weights = rows_to_lanes([live_col[rows, :]] * 2)
        given = rows_to_lanes(
            [share2[pl.ds(2 * start + h, CHUNK, stride=2), :] for h in range(2)]
        )
        away = depth * weights * (u2[rows, :] - mean2) + g2[rows, :]
        value = given * slope2 - (depth * weights * beta_scale + away * gamma_scale)
        own2[rows, :] = mm(value, direct2)
        grad_own2[...] += mm_tn(x2[pl.ds(half + start, CHUNK), :], value)

    over(points, CHUNK, own)


def scatter_loop(subs, depth, block, step, index, q_ref, push, sums):
    per = SUBLANES // subs
    groups = index.shape[0] // (depth * per)
    row = iota((SUBLANES, LANES), 0)
    mine = [(row >= subs * i) & (row < subs * (i + 1)) for i in range(per)]
    ways = len(sums) // per

    def one_group(place, carry):
        group = step * block + place
        rows = pl.ds(pl.multiple_of(group * SUBLANES, SUBLANES), SUBLANES)
        given = push[rows, :]
        for k in range(depth):
            value = q_ref[place, k] * given
            for i in range(per):
                j = index.at[pl.ds((k * per + i) * groups, groups)][group]
                target = sums[i * ways + k % ways].at[pl.ds(j, SUBLANES), :]
                pltpu.store(target, target[...] + value, mask=mine[i])
        return carry

    lax.fori_loop(0, block, one_group, 0)


def clear(sums):
    def rows8(start):
        for ref in sums:
            ref[pl.ds(start, SUBLANES), :] = jnp.zeros((SUBLANES, LANES), F32)

    over(sums[0].shape[0], SUBLANES, rows8)


def scatter2_kernel(depth, index, q_ref, push, x2, weight, scales, extra, near, grad_near, *sums):
    step = pl.program_id(0)
    both = x2.shape[0]
    width = x2.shape[1]

    @pl.when(step == 0)
    def _():
        clear(sums)

    scatter_loop(2, depth, q_ref.shape[0], step, index, q_ref, push, sums)

    @pl.when(step == pl.num_programs(0) - 1)
    def _():
        relative = weight[:, width:]
        grad_near[...] = jnp.zeros(grad_near.shape, F32)

        def finish(start):
            rows = pl.ds(start, CHUNK)
            halves = []
            for h in range(2):
                here = pl.ds(SUBLANES + 2 * start + h, CHUNK, stride=2)
                halves.append(tree([ref[here, :] for ref in sums], jnp.add))
            value = rows_to_lanes(halves) * scales[0:1, :] - extra[rows, :]
            near[rows, :] = mm(value, relative)
            grad_near[...] += mm_tn(x2[rows, :], value)

        over(both, CHUNK, finish)


def scatter1_kernel(
    depth, index, q_ref, grad, inverse, share, moment, near, given, parts, push, *sums
):
    step = pl.program_id(0)
    both = near.shape[0]

    @pl.when(step == 0)
    def _():
        clear(sums)
        push[...] = grad[...] * inverse[...]
        weighted = grad[...] * share[...]
        given[...] = weighted
        parts[...] = jnp.concatenate(
            [
                jnp.sum(weighted, axis=0, keepdims=True),
                jnp.sum(grad[...] * moment[...], axis=0, keepdims=True),
                jnp.zeros((6, LANES), F32),
            ],
            axis=0,
        )

    scatter_loop(1, depth, q_ref.shape[0], step, index, q_ref, push, sums)

    @pl.when(step == pl.num_programs(0) - 1)
    def _():
        def finish(start):
            here = pl.ds(SUBLANES + start, CHUNK)
            near[pl.ds(start, CHUNK), :] = tree([ref[here, :] for ref in sums], jnp.add)

        over(both, CHUNK, finish)


def last_kernel(
    sizes,
    depth,
    near1,
    given1,
    parts,
    x1,
    away_own1,
    away_all1,
    counts,
    scales1,
    live,
    weight1,
    grad_own2,
    grad_near2,
    grad_features,
    grad_weight1,
    grad_gain1,
    grad_bias1,
    grad_weight2,
    slots,
    flat,
    pushed,
    arrived,
    halved,
    landed,
    reduced,
    whole,
    small_sems,
    pair_sems,
    ring_sems,
):
    cores, chips = sizes
    total = cores * chips
    points = given1.shape[0]
    both = near1.shape[0]
    cin = x1.shape[1]
    width1 = weight1.shape[0]
    piece = landed.shape[1]
    core = lax.axis_index("points")
    chip = lax.axis_index("clouds")
    half = pl.multiple_of(core * points, points)
    barrier = pltpu.get_barrier_semaphore()
    signal_all(barrier, cores, total)
    pl.semaphore_wait(barrier, total - 1)
    gather_start(parts, slots, small_sems.at[0], small_sems.at[1], cores, total)

    flat[5 * LANES :, :] = jnp.zeros((flat.shape[0] - 5 * LANES, LANES), F32)
    for h in range(2):
        columns = slice(h * LANES, (h + 1) * LANES)
        flat[h * LANES : (h + 1) * LANES, :] = grad_own2[:, columns]
        flat[(2 + h) * LANES : (3 + h) * LANES, :] = grad_near2[:, columns] - grad_own2[:, columns]

    direct1 = weight1[:, :cin] - weight1[:, cin:]
    relative1 = weight1[:, cin:]
    slope = scales1[0:1, :]
    r1 = scales1[1:2, :]
    outer_scale = slope / scales1[2:3, :]
    gather_wait(slots, small_sems.at[0], small_sems.at[1], total)
    sums = slot_sum(slots, total)
    grad_bias1[...] = sums[0:1]
    grad_gain1[...] = sums[1:2]
    beta_scale = outer_scale * sums[0:1]
    gamma_scale = outer_scale * sums[1:2] * r1

    grad_near1 = jnp.zeros((cin, width1), F32)
    for c in range(cores):

        def push(i, total_near):
            start = pl.multiple_of(i * CHUNK, CHUNK)
            rows = pl.ds(c * points + start, CHUNK)
            value = near1[rows, :] * slope
            value = value - (counts[rows, :] * beta_scale + away_all1[rows, :] * gamma_scale)
            pushed[c, :, pl.ds(start, CHUNK)] = jnp.transpose(mm(value, relative1))
            return total_near + mm_tn(x1[rows, :], value)

        grad_near1 = lax.fori_loop(0, points // CHUNK, push, grad_near1)
    swap = to_partner(pushed.at[1 - core], arrived, pair_sems, 0)
    swap.start()

    def own(i, total_own):
        start = pl.multiple_of(i * CHUNK, CHUNK)
        rows = pl.ds(start, CHUNK)
        weights = jnp.transpose(live[:, rows])[:, :1]
        value = given1[rows, :] * slope
        value = value - (depth * weights * beta_scale + away_own1[rows, :] * gamma_scale)
        grad_features[:, rows] = jnp.transpose(mm(value, direct1)) + pushed[core, :, rows]
        return total_own + mm_tn(x1[pl.ds(half + start, CHUNK), :], value)

    grad_own1 = lax.fori_loop(0, points // CHUNK, own, jnp.zeros((cin, width1), F32))
    flat[4 * LANES : 4 * LANES + cin, :] = grad_own1
    flat[4 * LANES + cin : 4 * LANES + 2 * cin, :] = grad_near1 - grad_own1
    swap.wait()
    grad_features[...] += arrived[...]

    side = chips * piece
    mine = pl.multiple_of(core * side, SUBLANES)
    other = pl.multiple_of((1 - core) * side, SUBLANES)
    swap = to_partner(flat.at[pl.ds(other, side)], halved, pair_sems, 1)
    swap.start()
    swap.wait()
    flat[pl.ds(mine, side), :] += halved[...]
    landed[chip] = flat[pl.ds(pl.multiple_of(mine + chip * piece, SUBLANES), piece), :]

    def chip_copy(d, source, target, use):
        return pltpu.make_async_remote_copy(
            src_ref=source,
            dst_ref=target,
            send_sem=ring_sems.at[0, use],
            recv_sem=ring_sems.at[1, use],
            device_id=(lax.rem(chip + d, chips), core),
            device_id_type=MESH,
        )

    def scatter(d, carry):
        to = lax.rem(chip + d, chips)
        source = flat.at[pl.ds(pl.multiple_of(mine + to * piece, SUBLANES), piece)]
        chip_copy(d, source, landed.at[chip], 0).start()
        return carry

    lax.fori_loop(1, chips, scatter, 0)
    others = landed.at[pl.ds(0, chips - 1)]
    arrival = chip_copy(1, others, others, 0)
    arrival.wait_recv()
    arrival.wait_send()
    reduced[...] = slot_sum(landed, chips)
    whole[core, chip] = reduced[...]

    def spread(d, carry):
        chip_copy(d, reduced, whole.at[core, chip], 1).start()
        return carry

    lax.fori_loop(1, chips, spread, 0)
    others = landed.at[pl.ds(0, chips - 1)]
    arrival = chip_copy(1, others, others, 1)
    arrival.wait_recv()
    arrival.wait_send()
    swap = to_partner(whole.at[core], whole.at[core], pair_sems, 2)
    swap.start()
    swap.wait()
    final = whole.reshape(cores * side, LANES)
    for h in range(2):
        rows = slice(h * LANES, (h + 1) * LANES)
        grad_weight2[rows, 0:LANES] = jnp.transpose(final[h * LANES : (h + 1) * LANES, :])
        grad_weight2[rows, LANES : 2 * LANES] = jnp.transpose(
            final[(2 + h) * LANES : (3 + h) * LANES, :]
        )
    grad_weight1[...] = jnp.transpose(final[4 * LANES : 5 * LANES, :])


def shaped(*shape):
    return jax.ShapeDtypeStruct(shape, F32)


def scratch(*shape, dtype=F32):
    return pltpu.VMEM(shape, dtype)


def program(mesh):
    cores, chips = mesh.shape["points"], mesh.shape["clouds"]
    total = cores * chips

    def on_device(
        features,
        lengths,
        mask,
        neighbours,
        first_layer_weight,
        first_norm_gain,
        first_norm_bias,
        second_layer_weight,
        second_norm_gain,
        second_norm_bias,
        pooled_grad,
    ):
        cin, points = features.shape
        depth = neighbours.shape[0]
        width1, width2 = first_layer_weight.shape[0], second_layer_weight.shape[0]
        both = cores * points
        clouds = lengths.shape[0]
        live = jnp.broadcast_to(mask.astype(F32)[None, :], (SUBLANES, points))
        near = jnp.where(mask[None, :] > 0, neighbours, -1).astype(jnp.int16)
        near = jnp.broadcast_to(near[:, None, :], (depth, 16, points))

        def layout(subs):
            per = SUBLANES // subs
            value = neighbours.reshape(depth, points // per, per) * subs
            value = value + (SUBLANES - subs * jnp.arange(per, dtype=jnp.int32))
            return value.transpose(0, 2, 1).reshape(-1)

        index1, index2 = layout(1), layout(2)
        groups1, groups2 = points // SUBLANES, points // 4
        block = 32
        anywhere = pl.BlockSpec(memory_space=pl.ANY)
        outs = pl.pallas_call(
            functools.partial(forward_kernel, (cores, total)),
            out_shape=[
                shaped(clouds, 2 * width2),
                shaped(groups1, depth, SUBLANES, LANES),
                shaped(groups2, depth, SUBLANES, LANES),
                shaped(points, width1),
                shaped(points, width1),
                shaped(points, width1),
                shaped(both, cin),
                shaped(points, width1),
                shaped(both, width1),
                shaped(both, LANES),
                shaped(SUBLANES, width1),
                shaped(2 * points, LANES),
                shaped(both, width2),
                shaped(both, width1),
                shaped(points, width1),
                shaped(width1, width2),
                shaped(SUBLANES, width2),
            ],
            in_specs=[VMEM] * 3 + [SMEM] * 3 + [VMEM] * 7,
            out_specs=[VMEM, anywhere, anywhere] + [VMEM] * 14,
            scratch_shapes=[
                scratch(cores, cin, points),
                scratch(both, points, dtype=BF16),
                scratch(points, LANES),
                scratch(cores, 3 * cin, points, dtype=BF16),
                scratch(2 * width1, both, dtype=BF16),
                scratch(points, width1),
                scratch(both, width1),
                scratch(points, cin),
                scratch(points, width1),
                scratch(both + 2 * SUBLANES, LANES),
                scratch(points, LANES),
                scratch(points, LANES),
                scratch(2 * both + 2 * SUBLANES, LANES),
                scratch(2 * points, LANES),
                scratch(2 * points, LANES),
                scratch(2 * points, LANES),
                scratch(2 * points, LANES),
                scratch(2 * points, LANES),
                scratch(both, width1),
                scratch(points, width2),
                scratch(both, width2),
                scratch(points, width2),
                scratch(both, 2 * cin),
                scratch(cores, 3 * clouds, SUBLANES, LANES),
                scratch(3, 4, LANES),
                scratch(3, total, 4, LANES),
                scratch(depth, SUBLANES, LANES),
                scratch(depth, SUBLANES, LANES),
                scratch(2, block, depth, SUBLANES, LANES),
                pltpu.SemaphoreType.DMA((2, 3)),
                pltpu.SemaphoreType.DMA((2, 3)),
                pltpu.SemaphoreType.DMA((2,)),
            ],
            compiler_params=pltpu.CompilerParams(
                collective_id=1, has_side_effects=True, vmem_limit_bytes=MEMORY
            ),
            name="forward",
        )(
            features,
            near,
            live,
            index1,
            index2,
            lengths,
            first_layer_weight,
            first_norm_gain[None, :],
            first_norm_bias[None, :],
            second_layer_weight,
            second_norm_gain[None, :],
            second_norm_bias[None, :],
            pooled_grad,
        )
        (
            pooled,
            q1,
            q2,
            inverse1,
            share1,
            moment1,
            x1,
            away_own1,
            away_all1,
            counts,
            scales1,
            push2,
            extra2,
            x2,
            own2,
            grad_own2,
            scales2,
        ) = outs

        def q_blocks():
            return pl.BlockSpec((block, depth, SUBLANES, LANES), lambda s: (s, 0, 0, 0))

        near2, grad_near2 = pl.pallas_call(
            functools.partial(scatter2_kernel, depth),
            grid=(groups2 // block,),
            out_shape=[shaped(both, width1), shaped(width1, width2)],
            in_specs=[SMEM, q_blocks()] + [VMEM] * 5,
            out_specs=[VMEM, VMEM],
            scratch_shapes=[scratch(2 * both + 2 * SUBLANES, LANES)] * 8,
            compiler_params=pltpu.CompilerParams(vmem_limit_bytes=MEMORY),
            name="scatter2",
        )(index2, q2, push2, x2, second_layer_weight, scales2, extra2)

        core = lax.axis_index("points")
        sent = lax.dynamic_slice(near2, ((1 - core) * points, 0), (points, width1))
        kept = lax.dynamic_slice(near2, (core * points, 0), (points, width1))
        other = lax.ppermute(sent, "points", [(0, 1), (1, 0)])
        grad1 = own2 + kept + other

        near1, given1, parts = pl.pallas_call(
            functools.partial(scatter1_kernel, depth),
            grid=(groups1 // block,),
            out_shape=[shaped(both, width1), shaped(points, width1), shaped(SUBLANES, width1)],
            in_specs=[SMEM, q_blocks()] + [VMEM] * 4,
            out_specs=[VMEM] * 3,
            scratch_shapes=[scratch(points, width1)]
            + [scratch(both + 2 * SUBLANES, LANES)] * SUBLANES,
            compiler_params=pltpu.CompilerParams(vmem_limit_bytes=MEMORY),
            name="scatter1",
        )(index1, q1, grad1, inverse1, share1, moment1)

        piece = -(-5 * LANES // (total * SUBLANES)) * SUBLANES
        side = chips * piece
        grad_features, grad_weight1, grad_gain1, grad_bias1, grad_weight2 = pl.pallas_call(
            functools.partial(last_kernel, (cores, chips), depth),
            out_shape=[
                shaped(cin, points),
                shaped(width1, 2 * cin),
                shaped(1, width1),
                shaped(1, width1),
                shaped(width2, 2 * width1),
            ],
            in_specs=[VMEM] * 12,
            out_specs=[VMEM] * 5,
            scratch_shapes=[
                scratch(total, SUBLANES, LANES),
                scratch(cores * side, LANES),
                scratch(cores, cin, points),
                scratch(cin, points),
                scratch(side, LANES),
                scratch(chips, piece, LANES),
                scratch(piece, LANES),
                scratch(cores, chips, piece, LANES),
                pltpu.SemaphoreType.DMA((2,)),
                pltpu.SemaphoreType.DMA((2, 3)),
                pltpu.SemaphoreType.DMA((2, 2)),
            ],
            compiler_params=pltpu.CompilerParams(
                collective_id=2, has_side_effects=True, vmem_limit_bytes=MEMORY
            ),
            name="last",
        )(
            near1,
            given1,
            parts,
            x1,
            away_own1,
            away_all1,
            counts,
            scales1,
            live,
            first_layer_weight,
            grad_own2,
            grad_near2,
        )
        return (
            pooled,
            grad_features,
            grad_weight1,
            grad_gain1.reshape(width1),
            grad_bias1.reshape(width1),
            grad_weight2,
            scales2[2],
            scales2[1],
        )

    return on_device


def solution(mesh):
    in_specs = (
        P(None, ("clouds", "points")),
        P("clouds"),
        P(("clouds", "points")),
        P(None, ("clouds", "points")),
        P(),
        P(),
        P(),
        P(),
        P(),
        P(),
        P("clouds", None),
    )
    out_specs = (P("clouds", None), P(None, ("clouds", "points")), P(), P(), P(), P(), P(), P())
    return jax.shard_map(
        program(mesh), mesh=mesh, in_specs=in_specs, out_specs=out_specs, check_vma=False
    )
```

time: 970 us -> 244 us (0.25)
  other arithmetic: 381 us -> 4.49 us
  blocking collectives: 252 us -> 0 us
  Pallas kernels: 0 us -> 223 us
  local copies, waits for them, and re-layouts: 175 us -> 14.7 us
  matrix products: 122 us -> 0 us
  between operations: 15.1 us -> 0.72 us
  waiting for transfers between devices: 13.5 us -> 0.2 us
    psum x6 -> x0, blocking collectives: 244 us -> none  [the longest x2 82.8 us: edgeconv_forward(): lax.psum((jnp.sum(edge_value_rows * active_flag, axis=(1, 2)), jnp.sum(ac...]
    pallas_call x0 -> x4, Pallas kernels: none -> 223 us  [the longest x1 141 us: on_device(): pl.pallas_call(functools.partial(forward_kernel, (cores, total)), out_sha...]
    scatter-add x2 -> x0, other arithmetic: 220 us -> none  [scatter_columns(): return start.at[:, neighbours].add(values)]
    gather x4 -> x0, local copies, waits for them, and re-layouts: 158 us -> none  [gather_columns(): return jnp.take(table, neighbours, axis=1)]
    dot_general x15 -> x0, matrix products: 122 us -> none  [the longest x2 45.8 us: edgeconv_forward(): jnp.einsum('cd,dkp->ckp', relative, spread, precision=FULL_ACCURACY)]
    reduce_sum x10 -> x0, other arithmetic: 121 us -> none  [the longest x2 45.9 us: edgeconv_backward(): jnp.sum(grad_shift, axis=(1, 2))]
    reduce_max x3 -> x0, other arithmetic: 31.4 us -> none  [the longest x2 31 us: edgeconv_forward(): outputs = jax.nn.logsumexp(active, axis=1) - math.log(depth)]
  transfers between devices with their start and end apart: 4 -> 1, of which waited for: 2 -> 1; matrix products, arithmetic and copies ran while one was open for 16% -> 1% of each run, Pallas kernels for 0% -> 0%
where the time goes in v1:
time: 244 us
  Pallas kernels  223 us (91%)
  local copies, waits for them, and re-layouts  14.7 us (6%)
  other arithmetic  4.49 us (2%)
    pallas_call x1, Pallas kernels, on_device(): pl.pallas_call(functools.partial(forward_kernel, (cores, total)), out_sha...  141 us
    pallas_call x1, Pallas kernels, on_device(): pl.pallas_call(functools.partial(last_kernel, (cores, chips), depth), out...  32.9 us
    pallas_call x1, Pallas kernels, on_device(): pl.pallas_call(functools.partial(scatter2_kernel, depth), grid=(groups2 /...  28.2 us
    pallas_call x1, Pallas kernels, on_device(): pl.pallas_call(functools.partial(scatter1_kernel, depth), grid=(groups1 /...  21.2 us
    unnamed x12, local copies, waits for them, and re-layouts  9.41 us
  transfers between devices with their start and end apart: 1, of which 1 were waited for; matrix products, arithmetic and copies ran while one was open for 1% of the time, Pallas kernels for 0%

profile of v1, /device:TPU:0, one launch (start us, length us, event | category | flops | bytes accessed | tf_op | source)
XLA Modules:
  0.0 243.5 jit_solution(4078832967881417016)
XLA Ops:
  0.7 0.7 broadcast_compare_fusion
  1.3 0.7 convert_element_type.7
  2.0 1.1 copy.19
  3.1 0.9 broadcast_multiply_fusion
  4.1 0.2 copy.21
  4.3 0.2 add_bitcast_fusion
  4.4 0.2 copy.22
  4.7 0.7 copy.23
  5.3 0.1 fusion
  5.5 0.9 copy.20
  6.3 0.9 broadcast_in_dim.41.near
  7.2 0.6 broadcast_in_dim.42.live
  7.9 140.7 %forward.1 = (f32[4,512]{1,0:T(4,128)}, f32[128,20,8,128]{3,2,1,0:T(8,128)}, f32[256,20,8,128]{3,2,1,0:T(8,128)}, f32[1024,128]{1,0:T(8,128)}, f32[1024,128]{1,0...) custom-call(f32[64,1024]{1,0:T(8,128)} %feat.1, ...), custom_call_target="tpu_custom_call" | custom-call | tf_op jit(solution)/shard_map/forward/pallas_call | solution.py:1046
  148.6 0.0 copy-start
  148.6 28.2 %scatter2.1 = (f32[2048,128]{1,0:T(8,128)}, f32[128,256]{1,0:T(8,128)}) custom-call(s32[20480]{0:T(1024)} %bitcast.24, f32[256,20,8,128]{3,2,1,0:T(8,128)} %get-tuple-element.38.q_ref, f32[2048,128]{1,0:T(8,128)} %get-tuple-element.39.push, f32[2048,128]{1,0:T(8,128)} %get-tuple-element.40.x2, f32[256,256]{1,0:T(8,128)} %weight.1, ...), custom_call_target="tpu_custom_call" | custom-call | tf_op jit(solution)/shard_map/scatter2/pallas_call | solution.py:1145
  176.8 0.0 copy-start.1
  176.8 1.1 constant_dynamic-slice_fusion
  177.9 0.4 collective-permute-start
  178.4 1.3 fusion.1
  179.7 0.2 collective-permute-done
  179.9 0.0 copy-done
  179.9 1.9 add_add_fusion.grad
  181.8 21.2 %scatter1.1 = (f32[2048,128]{1,0:T(8,128)}, f32[1024,128]{1,0:T(8,128)}, f32[8,128]{1,0:T(8,128)}) custom-call(s32[20480]{0:T(1024)} %bitcast.22, f32[128,20,8,128]{3,2,1,0:T(8,128)} %get-tuple-element.36.q_ref, f32[1024,128]{1,0:T(8,128)} %add_add_fusion.grad, f32[1024,128]{1,0:T(8,128)} %get-tuple-element.44.inverse, f32[1024,128]{1,0:T(8,128)} %get-tuple-element.45.share, ...), custom_call_target="tpu_custom_call" | custom-call | tf_op jit(solution)/shard_map/scatter1/pallas_call | solution.py:1162
  203.0 32.9 %last.1 = (f32[64,1024]{1,0:T(8,128)}, f32[128,128]{1,0:T(8,128)}, f32[1,128]{1,0:T(1,128)}, f32[1,128]{1,0:T(1,128)}, f32[256,256]{1,0:T(8,128)}) custom-call(f32[2048,128]{1,0:T(8,128)} %get-tuple-element.47.near1, f32[1024,128]{1,0:T(8,128)} %get-tuple-element.48.given1, f32[8,128]{1,0:T(8,128)} %get-tuple-element.49.parts, ...), custom_call_target="tpu_custom_call" | custom-call | tf_op jit(solution)/shard_map/last/pallas_call | solution.py:1176
  235.9 0.0 copy-done.1
  235.9 0.6 copy.30
  236.5 1.7 copy.31
  238.2 1.5 copy.32
  239.6 1.1 copy.33
  240.8 1.1 copy.34
  241.8 1.7 copy.35
  (2 shorter events, 0.0 us)
Async XLA Ops:
  148.6 31.3 %copy-start = (f32[1024,128]{1,0:T(8,128)S(1)}, f32[1024,128]{1,0:T(8,128)}, u32[]{:S(2)}) copy-start(f32[1024,128]{1,0:T(8,128)} %get-tuple-element.37) | copy-start | bytes 1572868
  176.8 59.1 %copy-start.1 = (f32[4,512]{1,0:T(4,128)S(1)}, f32[4,512]{1,0:T(4,128)}, u32[]{:S(2)}) copy-start(f32[4,512]{1,0:T(4,128)} %get-tuple-element.74) | copy-start | bytes 24580
  177.9 2.0 collective-permute-start

commit v2 on v1

--- a/solution.py
+++ b/solution.py
@@ -20,6 +20,7 @@
 MEMORY = 60 * 2**20
 VMEM = pl.BlockSpec(memory_space=pltpu.VMEM)
 SMEM = pl.BlockSpec(memory_space=pltpu.SMEM)
+ANY = pl.BlockSpec(memory_space=pl.ANY)
 
 
 def dot(left, right, dims):
@@ -54,6 +55,27 @@
     high = value.astype(BF16)
     low = (value - high.astype(F32)).astype(BF16)
     return high, low
+
+
+def product(left, right, dims):
+    def part(a, b):
+        return lax.dot_general(a, b, (dims, ((), ())), preferred_element_type=F32)
+
+    left_high, left_low = split(left)
+    right_high, right_low = split(right)
+    return part(left_high, right_high) + (part(left_high, right_low) + part(left_low, right_high))
+
+
+def by(left, right):
+    return product(left, right, ((1,), (0,)))
+
+
+def by_t(left, right):
+    return product(left, right, ((1,), (1,)))
+
+
+def t_by(left, right):
+    return product(left, right, ((0,), (0,)))
 
 
 def over(count, step, body):
@@ -267,20 +289,37 @@
     sizes,
     feat,
     near,
-    live,
-    index1,
-    index2,
+    mask,
+    index1_in,
+    index2_in,
     lengths,
     weight1,
     gain1,
     bias1,
-    weight2,
+    weight2_in,
     gain2,
     bias2,
     pooled_grad,
     pooled,
     q1,
     q2,
+    inverse1_out,
+    share1_out,
+    moment1_out,
+    x1_out,
+    away_own1_out,
+    away_all1_out,
+    counts_out,
+    x2_out,
+    scales1,
+    push2,
+    extra2,
+    own2,
+    grad_own2,
+    scales2,
+    index1,
+    index2,
+    weight2,
     inverse1,
     share1,
     moment1,
@@ -288,15 +327,10 @@
     away_own1,
     away_all1,
     counts,
-    scales1,
-    push2,
-    extra2,
-    x2_out,
-    own2,
-    grad_own2,
-    scales2,
     x1_cm,
+    tallies,
     links,
+    live,
     live_col,
     parts1,
     parts2,
@@ -307,6 +341,8 @@
     table1,
     own_rows1,
     level1,
+    share_rows1,
+    moment_rows1,
     table2,
     own_rows2,
     level2,
@@ -317,7 +353,7 @@
     u2,
     v2,
     g2,
-    xm,
+    u_parts,
     pool_parts,
     message,
     slots,
@@ -327,6 +363,8 @@
     pair_sems,
     all_sems,
     ring_sems,
+    load_sems,
+    store_sems,
 ):
     cores, total = sizes
     points = feat.shape[1]
@@ -334,32 +372,67 @@
     both = cores * points
     depth = near.shape[0]
     width1 = weight1.shape[0]
-    width2 = weight2.shape[0]
+    width2 = gain2.shape[1]
+    groups1, groups2 = points // SUBLANES, 2 * points // SUBLANES
     core = lax.axis_index("points")
     half = pl.multiple_of(core * points, points)
     barrier = pltpu.get_barrier_semaphore()
     signal_all(barrier, cores, total)
-
+    loads = [
+        pltpu.make_async_copy(source, target, load_sems.at[i])
+        for i, (source, target) in enumerate(
+            ((index1_in, index1), (index2_in, index2), (weight2_in, weight2))
+        )
+    ]
+    for copy in loads:
+        copy.start()
+    stores = [
+        pltpu.make_async_copy(source, target, store_sems.at[i])
+        for i, (source, target) in enumerate(
+            (
+                (x1, x1_out),
+                (counts, counts_out),
+                (away_own1, away_own1_out),
+                (away_all1, away_all1_out),
+                (inverse1, inverse1_out),
+                (share1, share1_out),
+                (moment1, moment1_out),
+                (x2, x2_out),
+            )
+        )
+    ]
+
+    live[...] = jnp.broadcast_to(mask[...].astype(F32), live.shape)
     row16 = iota((16, LANES), 0)
     one, none = jnp.ones((16, LANES), BF16), jnp.zeros((16, LANES), BF16)
 
-    def build(columns):
-        names = [near[k, :, columns] for k in range(depth)]
-
-        def rows16(start):
-            target = (row16 + start).astype(jnp.int16)
-            found = [jnp.where(name == target, one, none) for name in names]
-            links[pl.ds(start, 16), columns] = functools.reduce(jnp.add, found)
-
-        over(both, 16, rows16)
-
-    for tile in range(points // LANES):
-        build(pl.ds(tile * LANES, LANES))
-
+    def build(columns, first):
+        names = []
+        for k in range(depth):
+            name = jnp.where(mask[:, columns] > 0, near[k : k + 1, columns], -1)
+            names.append(jnp.broadcast_to(name, (16, LANES)).astype(jnp.int16))
+
+        def rows64(start):
+            for s in range(0, 64, 16):
+                target = (row16 + (start + s)).astype(jnp.int16)
+                found = [jnp.where(name == target, one, none) for name in names]
+                found = tree(found, jnp.add)
+                links[pl.ds(start + s, 16), columns] = found
+                here = pl.ds(start + s, 16)
+                tallies[here, :] = found if first else tallies[here, :] + found
+
+        over(both, 64, rows64)
+
+    tiles = points // LANES
+    early = tiles - tiles // 4
+    for tile in range(early):
+        build(pl.ds(tile * LANES, LANES), tile == 0)
     x1_cm[core] = feat[...]
     pl.semaphore_wait(barrier, total - 1)
     swap = to_partner(feat, x1_cm.at[core], pair_sems, 0)
     swap.start()
+    for tile in range(early, tiles):
+        build(pl.ds(tile * LANES, LANES), tile == 0)
     live_col[...] = jnp.broadcast_to(jnp.transpose(live[...])[:, :1], live_col.shape)
     swap.wait()
 
@@ -390,21 +463,23 @@
 
     over(points, CHUNK, sums_near1)
 
-    own_high, own_low = split(x1_cm[core])
-    both_parts = jnp.concatenate([own_high.astype(F32), own_low.astype(F32)], axis=0)
-    x_parts = jnp.transpose(both_parts).astype(BF16)
-    ones = jnp.ones((points, LANES), BF16)
-
-    def linked1(start):
+    stores[0].start()
+    ones = jnp.ones((LANES, LANES), BF16)
+
+    def count_links(start):
         rows = pl.ds(start, CHUNK)
-        xm[rows, :] = mm_low(links[rows, :], x_parts)
-        counts[rows, :] = mm_low(links[rows, :], ones)
-
-    over(both, CHUNK, linked1)
-
-    live_rows = live[...]
+        counts[rows, :] = mm_low(tallies[rows, :], ones)
+
+    over(both, CHUNK, count_links)
+    stores[1].start()
+
     live_sum = jnp.sum(live[0:1, :], axis=1, keepdims=True)
     mine = live_sum * depth
+
+    def live_total(start, size, value):
+        high, low = split(value)
+        weights = live[:, start : start + size].astype(BF16)
+        return (mm_low(weights, high) + mm_low(weights, low))[0:1]
 
     def statistics(x_all, n_ref, direct, relative, u, v, g, width):
         def outer(start):
@@ -419,17 +494,17 @@
             g[rows, :] = mm_nt(n_ref[rows, :], relative)
 
         over(points, CHUNK, inner)
-        u_sum = mm(live_rows, u[...])[0:1]
+        u_sum = live_total(0, points, u[...])
         g_sum = jnp.sum(g[...], axis=0, keepdims=True)
         u_mean = u_sum / live_sum
         v_mean = g_sum / mine
         centred = u[...] - u_mean
         spread = depth * centred * centred + 2.0 * centred * (g[...] - depth * v_mean)
-        square = mm(live_rows, spread)[0:1]
+        square = live_total(0, points, spread)
         weights = rows_to_lanes([counts[...]] * (width // LANES))
         away = v[...] - v_mean
         square = square + jnp.sum(weights * away * away, axis=0, keepdims=True)
-        return depth * u_sum + g_sum, square, v_mean
+        return depth * u_sum + g_sum, square, u_mean, v_mean
 
     def send_sums(use, rows):
         for i, value in enumerate(rows):
@@ -461,8 +536,18 @@
             square = term if square is None else square + term
         return count, mean, square / count
 
-    sums, square, v_mean1 = statistics(x1, n1, direct1, relative1, u1, v1, g1, width1)
+    sums, square, u_mean1, v_mean1 = statistics(x1, n1, direct1, relative1, u1, v1, g1, width1)
     send_sums(0, [sums, square, jnp.broadcast_to(mine, (1, LANES)), jnp.zeros((1, LANES), F32)])
+
+    for part, value in enumerate(split(u1[...] - u_mean1)):
+        u_parts[:, part * LANES : (part + 1) * LANES] = value
+
+    def shared1(start):
+        rows = pl.ds(start, CHUNK)
+        value = mm_low(links[rows, :], u_parts[:, 0 : 2 * LANES])
+        away_all1[rows, :] = value[:, :LANES] + value[:, LANES:]
+
+    over(both, CHUNK, shared1)
     receive(0)
     numbers = [slots[0, i, 2:3, 0:1] for i in range(total)]
     count, mean1, variance1 = combine(0, numbers, width1)
@@ -475,20 +560,23 @@
     def fill1(start):
         rows = pl.ds(start, CHUNK)
         table1[pl.ds(SUBLANES + start, CHUNK), :] = (v1[rows, :] - v_mean1) * (slope1 * LOG2E)
-        shared = mm_nt(xm[rows, 0:cin] + xm[rows, cin : 2 * cin], direct1)
-        away_all1[rows, :] = shared + counts[rows, :] * (v1[rows, :] - mean1)
+        away_all1[rows, :] += counts[rows, :] * (v1[rows, :] - (mean1 - u_mean1))
 
     over(both, CHUNK, fill1)
 
     def fill_own1(start):
         rows = pl.ds(start, CHUNK)
-        own_rows1[rows, :] = (u1[rows, :] - (mean1 - v_mean1)) * (slope1 * LOG2E) + bias1[
-            ...
-        ] * LOG2E
+        value = (u1[rows, :] - (mean1 - v_mean1)) * (slope1 * LOG2E) + bias1[...] * LOG2E
+        for s in range(0, CHUNK, groups1):
+            here = pl.ds(lax.div(start, groups1) + s // groups1, groups1, stride=SUBLANES)
+            own_rows1[here, :] = value[s : s + groups1]
         away_own1[rows, :] = depth * live_col[rows, :] * (u1[rows, :] - mean1) + g1[rows, :]
 
     over(points, CHUNK, fill_own1)
 
+    stores[2].start()
+    stores[3].start()
+    loads[0].wait()
     edge_pass(
         1,
         ring.shape[1],
@@ -501,20 +589,26 @@
         (held0, held1),
         ring,
         ring_sems,
-        (level1, share1, moment1, inverse1),
+        (level1, share_rows1, moment_rows1, inverse1),
     )
 
-    def hidden(start):
-        rows = pl.ds(start, CHUNK)
-        x2[pl.ds(half + start, CHUNK), :] = level1[rows, :]
-        offset = own_rows1[rows, :] - bias1[...] * LOG2E
-        moment1[rows, :] = (share1[rows, :] * offset + moment1[rows, :]) / (gain1[...] * LOG2E)
-
-    over(points, CHUNK, hidden)
+    inverse_gain1 = 1.0 / (gain1[...] * LOG2E)
+    for i in range(SUBLANES):
+        here = pl.ds(i, groups1, stride=SUBLANES)
+        x2[pl.ds(half + i * groups1, groups1), :] = level1[here, :]
+        offset = own_rows1[here, :] - bias1[...] * LOG2E
+        rows = slice(i * groups1, (i + 1) * groups1)
+        moment1[rows, :] = (share_rows1[here, :] * offset + moment_rows1[here, :]) * inverse_gain1
+        share1[rows, :] = share_rows1[here, :]
+    for copy in stores[4:7]:
+        copy.start()
     here = x2.at[pl.ds(half, points)]
     swap = to_partner(here, here, pair_sems, 1)
     swap.start()
+    loads[1].wait()
+    loads[2].wait()
     swap.wait()
+    stores[7].start()
 
     direct2 = weight2[:, :width1] - weight2[:, width1:]
     relative2 = weight2[:, width1:]
@@ -538,7 +632,6 @@
         def outer(start):
             rows = pl.ds(start, CHUNK)
             v2[rows, :] = mm_nt(x2[rows, :], relative2)
-            x2_out[rows, :] = x2[rows, :]
 
         over(both, CHUNK, outer)
 
@@ -549,7 +642,7 @@
         u_sum = jnp.zeros((1, width2), F32)
         g_sum = jnp.zeros((1, width2), F32)
         for s in range(0, points, CHUNK):
-            u_sum = u_sum + mm(live[:, s : s + CHUNK], u2[s : s + CHUNK, :])[0:1]
+            u_sum = u_sum + live_total(s, CHUNK, u2[s : s + CHUNK, :])
             g_sum = g_sum + jnp.sum(g2[s : s + CHUNK, :], axis=0, keepdims=True)
         u_mean = u_sum / live_sum
         v_mean = g_sum / mine
@@ -559,7 +652,7 @@
             spread = depth * centred * centred + 2.0 * centred * (
                 g2[s : s + CHUNK, :] - depth * v_mean
             )
-            square = square + mm(live[:, s : s + CHUNK], spread)[0:1]
+            square = square + live_total(s, CHUNK, spread)
 
         def squares(i, carry):
             rows = pl.ds(pl.multiple_of(i * CHUNK, CHUNK), CHUNK)
@@ -568,10 +661,20 @@
             return carry + jnp.sum(weights * away * away, axis=0, keepdims=True)
 
         square = lax.fori_loop(0, both // CHUNK, squares, square)
-        return depth * u_sum + g_sum, square, v_mean
-
-    sums, square, v_mean2 = statistics2()
+        return depth * u_sum + g_sum, square, u_mean, v_mean
+
+    sums, square, u_mean2, v_mean2 = statistics2()
     send_sums(1, lanes_to_rows(sums, width2) + lanes_to_rows(square, width2))
+    for part, value in enumerate(split(u2[...] - u_mean2)):
+        u_parts[:, part * width2 : (part + 1) * width2] = value
+
+    def shared2(start):
+        rows = pl.ds(start, CHUNK)
+        extra2[rows, :] = mm_low(links[rows, :], u_parts[:, 0:width2]) + mm_low(
+            links[rows, :], u_parts[:, width2:]
+        )
+
+    over(both, CHUNK, shared2)
     receive(1)
     count, mean2, variance2 = combine(1, numbers, width2)
     r2 = lax.rsqrt(variance2 + EPSILON)
@@ -588,15 +691,13 @@
 
     over(both, CHUNK, fill2)
 
-    def fill_own2(start):
-        rows = pl.ds(start, CHUNK)
+    for i in range(SUBLANES // 2):
+        rows = slice(i * groups2, (i + 1) * groups2)
         value = (u2[rows, :] - (mean2 - v_mean2)) * (slope2 * LOG2E) + bias2[...] * LOG2E
         for h in range(2):
-            own_rows2[pl.ds(2 * start + h, CHUNK, stride=2), :] = value[
+            own_rows2[pl.ds(2 * i + h, groups2, stride=SUBLANES), :] = value[
                 :, h * LANES : (h + 1) * LANES
             ]
-
-    over(points, CHUNK, fill_own2)
 
     edge_pass(
         2,
@@ -614,22 +715,32 @@
     )
 
     clouds = pooled_grad.shape[0]
-    starts, ends = [], []
-    end = jnp.int32(0)
-    for q in range(clouds):
-        starts.append(end)
-        end = end + lengths[q]
-        ends.append(end)
+    ends = [lengths[0]]
+    for q in range(1, clouds):
+        ends.append(ends[-1] + lengths[q])
     row = iota((SUBLANES, LANES), 0)
     odd = lax.rem(row, 2) == 1
-    point_of_row = lax.div(row, 2)
+    point_of_row = half + lax.div(row, 2) * groups2
     steps = level2.shape[0] // SUBLANES
     lowest = jnp.full((SUBLANES, LANES), -1e30, F32)
     zero = jnp.zeros((SUBLANES, LANES), F32)
 
-    def members(t):
-        position = point_of_row + (half + t * (SUBLANES // 2))
-        return [(position >= starts[q]) & (position < ends[q]) for q in range(clouds)]
+    def past(t):
+        position = point_of_row + t
+        return [position >= ends[q] for q in range(clouds - 1)]
+
+    def pick(after, values):
+        value = values[0]
+        for q in range(1, clouds):
+            value = jnp.where(after[q - 1], values[q], value)
+        return value
+
+    def apart(after, value, none):
+        out = []
+        for q in range(clouds):
+            kept = value if q == 0 else jnp.where(after[q - 1], value, none)
+            out.append(kept if q == clouds - 1 else jnp.where(after[q], none, kept))
+        return out
 
     def step_rows(t):
         return pl.ds(pl.multiple_of(t * SUBLANES, SUBLANES), SUBLANES)
@@ -638,32 +749,31 @@
         value = join(value, pltpu.roll(value, 2, 0))
         return join(value, pltpu.roll(value, 4, 0))
 
+    def unrolled(body, state, times):
+        def several(i, carry):
+            for u in range(times):
+                carry = body(i * times + u, carry)
+            return carry
+
+        return lax.fori_loop(0, steps // times, several, state)
+
     def peaks(t, carry):
         value = level2[step_rows(t), :]
-        inside = members(t)
-        out = []
-        for q in range(clouds):
-            out.append(jnp.maximum(carry[q], jnp.where(inside[q], value, lowest)))
-        for q in range(clouds):
-            out.append(carry[clouds + q] + jnp.where(inside[q], value, zero))
-        return tuple(out)
-
-    state = lax.fori_loop(0, steps, peaks, (lowest,) * clouds + (zero,) * clouds)
+        after = past(t)
+        tops = [jnp.maximum(a, b) for a, b in zip(carry, apart(after, value, lowest))]
+        adds = [a + b for a, b in zip(carry[clouds:], apart(after, value, zero))]
+        return tuple(tops + adds)
+
+    state = unrolled(peaks, (lowest,) * clouds + (zero,) * clouds, 8)
     peak = [by_parity(value, jnp.maximum) for value in state[:clouds]]
     sums = [by_parity(value, jnp.add) for value in state[clouds:]]
 
-    def pick(inside, values):
-        value = values[0]
-        for q in range(1, clouds):
-            value = jnp.where(inside[q], values[q], value)
-        return value
-
     def masses(t, carry):
-        inside = members(t)
-        value = jnp.exp(level2[step_rows(t), :] - pick(inside, peak))
-        return tuple(carry[q] + jnp.where(inside[q], value, zero) for q in range(clouds))
-
-    state = lax.fori_loop(0, steps, masses, (zero,) * clouds)
+        after = past(t)
+        value = jnp.exp(level2[step_rows(t), :] - pick(after, peak))
+        return tuple(a + b for a, b in zip(carry, apart(after, value, zero)))
+
+    state = unrolled(masses, (zero,) * clouds, 8)
     mass = [by_parity(value, jnp.add) for value in state]
     for q in range(clouds):
         pool_parts[core, 3 * q] = peak[q]
@@ -703,9 +813,9 @@
 
     def gradient(t, carry):
         rows = step_rows(t)
-        inside = members(t)
-        value = pick(inside, grad_level) * jnp.exp(level2[rows, :] - pick(inside, level))
-        value = value + pick(inside, grad_mean)
+        after = past(t)
+        value = pick(after, grad_level) * jnp.exp(level2[rows, :] - pick(after, level))
+        value = value + pick(after, grad_mean)
         push2[rows, :] = value * inverse2[rows, :]
         share = share2[rows, :]
         moment = (share * (own_rows2[rows, :] - bias_row) + moment2[rows, :]) * inverse_gain
@@ -713,19 +823,10 @@
         share2[rows, :] = given
         return carry[0] + given, carry[1] + value * moment
 
-    state = lax.fori_loop(0, steps, gradient, (zero, zero))
+    state = unrolled(gradient, (zero, zero), 8)
     grad_beta, grad_gamma = [by_parity(value, jnp.add) for value in state]
     send_sums(2, [grad_beta[0:1], grad_beta[1:2], grad_gamma[0:1], grad_gamma[1:2]])
 
-    x_high, x_low = split(x2[pl.ds(half, points), :])
-
-    def linked2(start):
-        rows = pl.ds(start, CHUNK)
-        value = mm_low(links[rows, :], x_high) + mm_low(links[rows, :], x_low)
-        weights = rows_to_lanes([counts[rows, :]] * 2)
-        v2[rows, :] = mm_nt(value, direct2) + weights * (v2[rows, :] - mean2)
-
-    over(both, CHUNK, linked2)
     receive(2)
     sums = slot_sum(slots.at[2], total)
     grad_beta = rows_to_lanes([sums[0:1], sums[1:2]])
@@ -739,114 +840,192 @@
     def extra(start):
         rows = pl.ds(start, CHUNK)
         weights = rows_to_lanes([counts[rows, :]] * 2)
-        extra2[rows, :] = weights * beta_scale + v2[rows, :] * gamma_scale
+        away = extra2[rows, :] + weights * (v2[rows, :] - (mean2 - u_mean2))
+        extra2[rows, :] = weights * beta_scale + away * gamma_scale
 
     over(both, CHUNK, extra)
     grad_own2[...] = jnp.zeros(grad_own2.shape, F32)
 
-    def own(start):
-        rows = pl.ds(start, CHUNK)
+    for i in range(SUBLANES // 2):
+        rows = slice(i * groups2, (i + 1) * groups2)
         weights = rows_to_lanes([live_col[rows, :]] * 2)
         given = rows_to_lanes(
-            [share2[pl.ds(2 * start + h, CHUNK, stride=2), :] for h in range(2)]
+            [share2[pl.ds(2 * i + h, groups2, stride=SUBLANES), :] for h in range(2)]
         )
         away = depth * weights * (u2[rows, :] - mean2) + g2[rows, :]
         value = given * slope2 - (depth * weights * beta_scale + away * gamma_scale)
-        own2[rows, :] = mm(value, direct2)
-        grad_own2[...] += mm_tn(x2[pl.ds(half + start, CHUNK), :], value)
-
-    over(points, CHUNK, own)
-
-
-def scatter_loop(subs, depth, block, step, index, q_ref, push, sums):
+        own2[rows, :] = by(value, direct2)
+        grad_own2[...] += t_by(x2[pl.ds(half + i * groups2, groups2), :], value)
+    for copy in stores:
+        copy.wait()
+
+
+def scatter_loop(subs, depth, index, q_hbm, ring, sems, push, sums, clear):
     per = SUBLANES // subs
-    groups = index.shape[0] // (depth * per)
+    groups = q_hbm.shape[0]
+    slots, block = ring.shape[0], ring.shape[1]
+    blocks = groups // block
     row = iota((SUBLANES, LANES), 0)
     mine = [(row >= subs * i) & (row < subs * (i + 1)) for i in range(per)]
     ways = len(sums) // per
 
-    def one_group(place, carry):
-        group = step * block + place
-        rows = pl.ds(pl.multiple_of(group * SUBLANES, SUBLANES), SUBLANES)
-        given = push[rows, :]
-        for k in range(depth):
-            value = q_ref[place, k] * given
-            for i in range(per):
-                j = index.at[pl.ds((k * per + i) * groups, groups)][group]
-                target = sums[i * ways + k % ways].at[pl.ds(j, SUBLANES), :]
-                pltpu.store(target, target[...] + value, mask=mine[i])
+    def pull(b):
+        slot = lax.rem(b, slots)
+        return pltpu.make_async_copy(
+            q_hbm.at[pl.ds(b * block, block)], ring.at[slot], sems.at[slot]
+        )
+
+    for b in range(slots - 1):
+        pull(b).start()
+    clear()
+
+    def one_block(b, carry):
+        @pl.when(b + slots - 1 < blocks)
+        def _():
+            pull(b + slots - 1).start()
+
+        pull(b).wait()
+        slot = lax.rem(b, slots)
+
+        def one_group(place, inner):
+            group = b * block + place
+            rows = pl.ds(pl.multiple_of(group * SUBLANES, SUBLANES), SUBLANES)
+            given = push[rows, :]
+            for k in range(depth):
+                value = ring[slot, place, k] * given
+                for i in range(per):
+                    j = index.at[pl.ds((k * per + i) * groups, groups)][group]
+                    target = sums[i * ways + k % ways].at[pl.ds(j, SUBLANES), :]
+                    pltpu.store(target, target[...] + value, mask=mine[i])
+            return inner
+
+        lax.fori_loop(0, block, one_group, 0)
         return carry
 
-    lax.fori_loop(0, block, one_group, 0)
+    lax.fori_loop(0, blocks, one_block, 0)
 
 
 def clear(sums):
-    def rows8(start):
+    rows = sums[0].shape[0]
+    zero = jnp.zeros((SUBLANES, LANES), F32)
+
+    def rows32(start):
         for ref in sums:
-            ref[pl.ds(start, SUBLANES), :] = jnp.zeros((SUBLANES, LANES), F32)
-
-    over(sums[0].shape[0], SUBLANES, rows8)
-
-
-def scatter2_kernel(depth, index, q_ref, push, x2, weight, scales, extra, near, grad_near, *sums):
-    step = pl.program_id(0)
-    both = x2.shape[0]
-    width = x2.shape[1]
-
-    @pl.when(step == 0)
-    def _():
+            for s in range(0, 4 * SUBLANES, SUBLANES):
+                ref[pl.ds(start + s, SUBLANES), :] = zero
+
+    over(rows, 4 * SUBLANES, rows32)
+    for s in range(rows // 32 * 32, rows, SUBLANES):
+        for ref in sums:
+            ref[s : s + SUBLANES, :] = zero
+
+
+def scatter2_kernel(
+    depth,
+    index_in,
+    q_hbm,
+    push_in,
+    x2_in,
+    weight_in,
+    scales,
+    extra_in,
+    kept,
+    sent,
+    grad_near,
+    index,
+    push,
+    x2,
+    weight,
+    extra,
+    ring,
+    load_sems,
+    ring_sems,
+    *sums,
+):
+    loads = [
+        pltpu.make_async_copy(source, target, load_sems.at[i])
+        for i, (source, target) in enumerate(
+            ((index_in, index), (push_in, push), (x2_in, x2), (weight_in, weight), (extra_in, extra))
+        )
+    ]
+
+    def prepare():
         clear(sums)
-
-    scatter_loop(2, depth, q_ref.shape[0], step, index, q_ref, push, sums)
-
-    @pl.when(step == pl.num_programs(0) - 1)
-    def _():
-        relative = weight[:, width:]
-        grad_near[...] = jnp.zeros(grad_near.shape, F32)
+        loads[0].wait()
+        loads[1].wait()
+
+    for copy in loads:
+        copy.start()
+    scatter_loop(2, depth, index, q_hbm, ring, ring_sems, push, sums, prepare)
+    for copy in loads[2:]:
+        copy.wait()
+    points, width = kept.shape
+    relative = weight[:, width:]
+    core = lax.axis_index("points")
+    grad_near[...] = jnp.zeros(grad_near.shape, F32)
+    for part, out in ((1 - core, sent), (core, kept)):
 
         def finish(start):
-            rows = pl.ds(start, CHUNK)
+            first = pl.multiple_of(part * points + start, CHUNK)
+            rows = pl.ds(first, CHUNK)
             halves = []
             for h in range(2):
-                here = pl.ds(SUBLANES + 2 * start + h, CHUNK, stride=2)
+                here = pl.ds(SUBLANES + 2 * first + h, CHUNK, stride=2)
                 halves.append(tree([ref[here, :] for ref in sums], jnp.add))
             value = rows_to_lanes(halves) * scales[0:1, :] - extra[rows, :]
-            near[rows, :] = mm(value, relative)
-            grad_near[...] += mm_tn(x2[rows, :], value)
-
-        over(both, CHUNK, finish)
+            out[pl.ds(start, CHUNK), :] = by(value, relative)
+            grad_near[...] += t_by(x2[rows, :], value)
+
+        over(points, CHUNK, finish)
 
 
 def scatter1_kernel(
-    depth, index, q_ref, grad, inverse, share, moment, near, given, parts, push, *sums
+    depth,
+    index_in,
+    q_hbm,
+    own,
+    kept,
+    other,
+    inverse,
+    share,
+    moment,
+    near,
+    given,
+    parts,
+    index,
+    push,
+    ring,
+    load_sems,
+    ring_sems,
+    *sums,
 ):
-    step = pl.program_id(0)
-    both = near.shape[0]
-
-    @pl.when(step == 0)
-    def _():
+    load = pltpu.make_async_copy(index_in, index, load_sems.at[0])
+    load.start()
+
+    def prepare():
         clear(sums)
-        push[...] = grad[...] * inverse[...]
-        weighted = grad[...] * share[...]
-        given[...] = weighted
-        parts[...] = jnp.concatenate(
-            [
-                jnp.sum(weighted, axis=0, keepdims=True),
-                jnp.sum(grad[...] * moment[...], axis=0, keepdims=True),
-                jnp.zeros((6, LANES), F32),
-            ],
-            axis=0,
-        )
-
-    scatter_loop(1, depth, q_ref.shape[0], step, index, q_ref, push, sums)
-
-    @pl.when(step == pl.num_programs(0) - 1)
-    def _():
-        def finish(start):
-            here = pl.ds(SUBLANES + start, CHUNK)
-            near[pl.ds(start, CHUNK), :] = tree([ref[here, :] for ref in sums], jnp.add)
-
-        over(both, CHUNK, finish)
+        groups = own.shape[0] // SUBLANES
+        grad_beta = jnp.zeros((1, LANES), F32)
+        grad_gamma = jnp.zeros((1, LANES), F32)
+        for i in range(SUBLANES):
+            here = pl.ds(i, groups, stride=SUBLANES)
+            rows = slice(i * groups, (i + 1) * groups)
+            grad = own[rows, :] + kept[rows, :] + other[rows, :]
+            push[here, :] = grad * inverse[here, :]
+            weighted = grad * share[rows, :]
+            given[rows, :] = weighted
+            grad_beta = grad_beta + jnp.sum(weighted, axis=0, keepdims=True)
+            grad_gamma = grad_gamma + jnp.sum(grad * moment[rows, :], axis=0, keepdims=True)
+        parts[...] = jnp.concatenate([grad_beta, grad_gamma, jnp.zeros((6, LANES), F32)], axis=0)
+        load.wait()
+
+    scatter_loop(1, depth, index, q_hbm, ring, ring_sems, push, sums, prepare)
+
+    def finish(start):
+        here = pl.ds(SUBLANES + start, CHUNK)
+        near[pl.ds(start, CHUNK), :] = tree([ref[here, :] for ref in sums], jnp.add)
+
+    over(near.shape[0], CHUNK, finish)
 
 
 def last_kernel(
@@ -860,23 +1039,28 @@
     away_all1,
     counts,
     scales1,
-    live,
+    mask,
     weight1,
     grad_own2,
     grad_near2,
-    grad_features,
-    grad_weight1,
-    grad_gain1,
-    grad_bias1,
-    grad_weight2,
+    from_own,
+    from_near,
+    norm1,
+    whole1,
+    whole2,
     slots,
-    flat,
+    flat1,
+    flat2,
     pushed,
     arrived,
-    halved,
-    landed,
-    reduced,
-    whole,
+    halved1,
+    halved2,
+    landed1,
+    landed2,
+    reduced1,
+    reduced2,
+    all1,
+    all2,
     small_sems,
     pair_sems,
     ring_sems,
@@ -884,74 +1068,13 @@
     cores, chips = sizes
     total = cores * chips
     points = given1.shape[0]
-    both = near1.shape[0]
     cin = x1.shape[1]
     width1 = weight1.shape[0]
-    piece = landed.shape[1]
     core = lax.axis_index("points")
     chip = lax.axis_index("clouds")
     half = pl.multiple_of(core * points, points)
     barrier = pltpu.get_barrier_semaphore()
     signal_all(barrier, cores, total)
-    pl.semaphore_wait(barrier, total - 1)
-    gather_start(parts, slots, small_sems.at[0], small_sems.at[1], cores, total)
-
-    flat[5 * LANES :, :] = jnp.zeros((flat.shape[0] - 5 * LANES, LANES), F32)
-    for h in range(2):
-        columns = slice(h * LANES, (h + 1) * LANES)
-        flat[h * LANES : (h + 1) * LANES, :] = grad_own2[:, columns]
-        flat[(2 + h) * LANES : (3 + h) * LANES, :] = grad_near2[:, columns] - grad_own2[:, columns]
-
-    direct1 = weight1[:, :cin] - weight1[:, cin:]
-    relative1 = weight1[:, cin:]
-    slope = scales1[0:1, :]
-    r1 = scales1[1:2, :]
-    outer_scale = slope / scales1[2:3, :]
-    gather_wait(slots, small_sems.at[0], small_sems.at[1], total)
-    sums = slot_sum(slots, total)
-    grad_bias1[...] = sums[0:1]
-    grad_gain1[...] = sums[1:2]
-    beta_scale = outer_scale * sums[0:1]
-    gamma_scale = outer_scale * sums[1:2] * r1
-
-    grad_near1 = jnp.zeros((cin, width1), F32)
-    for c in range(cores):
-
-        def push(i, total_near):
-            start = pl.multiple_of(i * CHUNK, CHUNK)
-            rows = pl.ds(c * points + start, CHUNK)
-            value = near1[rows, :] * slope
-            value = value - (counts[rows, :] * beta_scale + away_all1[rows, :] * gamma_scale)
-            pushed[c, :, pl.ds(start, CHUNK)] = jnp.transpose(mm(value, relative1))
-            return total_near + mm_tn(x1[rows, :], value)
-
-        grad_near1 = lax.fori_loop(0, points // CHUNK, push, grad_near1)
-    swap = to_partner(pushed.at[1 - core], arrived, pair_sems, 0)
-    swap.start()
-
-    def own(i, total_own):
-        start = pl.multiple_of(i * CHUNK, CHUNK)
-        rows = pl.ds(start, CHUNK)
-        weights = jnp.transpose(live[:, rows])[:, :1]
-        value = given1[rows, :] * slope
-        value = value - (depth * weights * beta_scale + away_own1[rows, :] * gamma_scale)
-        grad_features[:, rows] = jnp.transpose(mm(value, direct1)) + pushed[core, :, rows]
-        return total_own + mm_tn(x1[pl.ds(half + start, CHUNK), :], value)
-
-    grad_own1 = lax.fori_loop(0, points // CHUNK, own, jnp.zeros((cin, width1), F32))
-    flat[4 * LANES : 4 * LANES + cin, :] = grad_own1
-    flat[4 * LANES + cin : 4 * LANES + 2 * cin, :] = grad_near1 - grad_own1
-    swap.wait()
-    grad_features[...] += arrived[...]
-
-    side = chips * piece
-    mine = pl.multiple_of(core * side, SUBLANES)
-    other = pl.multiple_of((1 - core) * side, SUBLANES)
-    swap = to_partner(flat.at[pl.ds(other, side)], halved, pair_sems, 1)
-    swap.start()
-    swap.wait()
-    flat[pl.ds(mine, side), :] += halved[...]
-    landed[chip] = flat[pl.ds(pl.multiple_of(mine + chip * piece, SUBLANES), piece), :]
 
     def chip_copy(d, source, target, use):
         return pltpu.make_async_remote_copy(
@@ -963,40 +1086,158 @@
             device_id_type=MESH,
         )
 
-    def scatter(d, carry):
-        to = lax.rem(chip + d, chips)
-        source = flat.at[pl.ds(pl.multiple_of(mine + to * piece, SUBLANES), piece)]
-        chip_copy(d, source, landed.at[chip], 0).start()
-        return carry
-
-    lax.fori_loop(1, chips, scatter, 0)
-    others = landed.at[pl.ds(0, chips - 1)]
-    arrival = chip_copy(1, others, others, 0)
-    arrival.wait_recv()
-    arrival.wait_send()
-    reduced[...] = slot_sum(landed, chips)
-    whole[core, chip] = reduced[...]
-
-    def spread(d, carry):
-        chip_copy(d, reduced, whole.at[core, chip], 1).start()
-        return carry
-
-    lax.fori_loop(1, chips, spread, 0)
-    others = landed.at[pl.ds(0, chips - 1)]
-    arrival = chip_copy(1, others, others, 1)
-    arrival.wait_recv()
-    arrival.wait_send()
-    swap = to_partner(whole.at[core], whole.at[core], pair_sems, 2)
+    class Summed:
+        def __init__(self, flat, halved, landed, reduced, whole, first):
+            self.flat, self.halved, self.landed, self.reduced, self.whole = (
+                flat,
+                halved,
+                landed,
+                reduced,
+                whole,
+            )
+            self.first = first
+            self.piece = landed.shape[1]
+            self.side = chips * self.piece
+            self.mine = pl.multiple_of(core * self.side, SUBLANES)
+            other = pl.multiple_of((1 - core) * self.side, SUBLANES)
+            self.swap = to_partner(flat.at[pl.ds(other, self.side)], halved, pair_sems, first)
+            here = whole.at[core]
+            self.back = to_partner(here, here, pair_sems, first + 1)
+
+        def scatter(self):
+            self.swap.wait()
+            self.flat[pl.ds(self.mine, self.side), :] += self.halved[...]
+            start = pl.multiple_of(self.mine + chip * self.piece, SUBLANES)
+            self.landed[chip] = self.flat[pl.ds(start, self.piece), :]
+
+            def send(d, carry):
+                to = lax.rem(chip + d, chips)
+                place = pl.multiple_of(self.mine + to * self.piece, SUBLANES)
+                source = self.flat.at[pl.ds(place, self.piece)]
+                chip_copy(d, source, self.landed.at[chip], self.first).start()
+                return carry
+
+            lax.fori_loop(1, chips, send, 0)
+
+        def wait(self, use):
+            others = self.landed.at[pl.ds(0, chips - 1)]
+            arrival = chip_copy(1, others, others, use)
+            arrival.wait_recv()
+            arrival.wait_send()
+
+        def spread(self):
+            self.wait(self.first)
+            self.reduced[...] = slot_sum(self.landed, chips)
+            self.whole[core, chip] = self.reduced[...]
+
+            def send(d, carry):
+                chip_copy(d, self.reduced, self.whole.at[core, chip], self.first + 1).start()
+                return carry
+
+            lax.fori_loop(1, chips, send, 0)
+
+        def finish(self):
+            self.wait(self.first + 1)
+            self.back.start()
+
+    sum1 = Summed(flat1, halved1, landed1, reduced1, all1, 0)
+    sum2 = Summed(flat2, halved2, landed2, reduced2, all2, 2)
+    for flat, rows in ((flat1, LANES), (flat2, 4 * LANES)):
+        if flat.shape[0] > rows:
+            flat[rows:, :] = jnp.zeros((flat.shape[0] - rows, LANES), F32)
+    for h in range(2):
+        columns = slice(h * LANES, (h + 1) * LANES)
+        flat2[h * LANES : (h + 1) * LANES, :] = grad_own2[:, columns]
+        flat2[(2 + h) * LANES : (3 + h) * LANES, :] = grad_near2[:, columns] - grad_own2[:, columns]
+    direct1 = weight1[:, :cin] - weight1[:, cin:]
+    relative1 = weight1[:, cin:]
+    slope = scales1[0:1, :]
+    r1 = scales1[1:2, :]
+    outer_scale = slope / scales1[2:3, :]
+
+    pl.semaphore_wait(barrier, total - 1)
+    sum2.swap.start()
+    gather_start(parts, slots, small_sems.at[0], small_sems.at[1], cores, total)
+    sum2.scatter()
+    gather_wait(slots, small_sems.at[0], small_sems.at[1], total)
+    sums = slot_sum(slots, total)
+    norm1[...] = sums
+    beta_scale = outer_scale * sums[0:1]
+    gamma_scale = outer_scale * sums[1:2] * r1
+
+    grad_near1 = jnp.zeros((cin, width1), F32)
+    for c in range(cores):
+
+        def push(i, total_near):
+            start = pl.multiple_of(i * CHUNK, CHUNK)
+            rows = pl.ds(c * points + start, CHUNK)
+            value = near1[rows, :] * slope
+            value = value - (counts[rows, :] * beta_scale + away_all1[rows, :] * gamma_scale)
+            pushed[c, :, pl.ds(start, CHUNK)] = jnp.transpose(by(value, relative1))
+            return total_near + t_by(x1[rows, :], value)
+
+        grad_near1 = lax.fori_loop(0, points // CHUNK, push, grad_near1)
+    swap = to_partner(pushed.at[1 - core], arrived, pair_sems, 4)
     swap.start()
+
+    def own(i, total_own):
+        start = pl.multiple_of(i * CHUNK, CHUNK)
+        rows = pl.ds(start, CHUNK)
+        weights = jnp.broadcast_to(mask[:, rows].astype(F32), (SUBLANES, CHUNK))
+        weights = jnp.transpose(weights)[:, :1]
+        value = given1[rows, :] * slope
+        value = value - (depth * weights * beta_scale + away_own1[rows, :] * gamma_scale)
+        from_own[:, rows] = jnp.transpose(by(value, direct1)) + pushed[core, :, rows]
+        return total_own + t_by(x1[pl.ds(half + start, CHUNK), :], value)
+
+    grad_own1 = lax.fori_loop(0, points // CHUNK, own, jnp.zeros((cin, width1), F32))
+    flat1[0:cin, :] = grad_own1
+    flat1[cin : 2 * cin, :] = grad_near1 - grad_own1
+    sum1.swap.start()
+    sum2.spread()
+    sum1.scatter()
     swap.wait()
-    final = whole.reshape(cores * side, LANES)
+    from_near[...] = arrived[...]
+    sum2.finish()
+    sum1.spread()
+    sum2.back.wait()
+    whole2[...] = all2[...]
+    sum1.finish()
+    sum1.back.wait()
+    whole1[...] = all1[...]
+
+
+def finish_kernel(
+    from_own,
+    from_near,
+    norm1,
+    whole1,
+    whole2,
+    scales2,
+    pooled_in,
+    pooled,
+    grad_features,
+    grad_weight1,
+    grad_gain1,
+    grad_bias1,
+    grad_weight2,
+    grad_gain2,
+    grad_bias2,
+):
+    pooled[...] = pooled_in[...]
+    grad_features[...] = from_own[...] + from_near[...]
+    grad_weight1[...] = jnp.transpose(whole1[0:LANES, :])
+    grad_bias1[...] = norm1[0:1, :]
+    grad_gain1[...] = norm1[1:2, :]
     for h in range(2):
         rows = slice(h * LANES, (h + 1) * LANES)
-        grad_weight2[rows, 0:LANES] = jnp.transpose(final[h * LANES : (h + 1) * LANES, :])
-        grad_weight2[rows, LANES : 2 * LANES] = jnp.transpose(
-            final[(2 + h) * LANES : (3 + h) * LANES, :]
-        )
-    grad_weight1[...] = jnp.transpose(final[4 * LANES : 5 * LANES, :])
+        for part in range(2):
+            block = (2 * part + h) * LANES
+            grad_weight2[rows, part * LANES : (part + 1) * LANES] = jnp.transpose(
+                whole2[block : block + LANES, :]
+            )
+    grad_bias2[...] = scales2[1:2, :]
+    grad_gain2[...] = scales2[2:3, :]
 
 
 def shaped(*shape):
@@ -1029,20 +1270,15 @@
         width1, width2 = first_layer_weight.shape[0], second_layer_weight.shape[0]
         both = cores * points
         clouds = lengths.shape[0]
-        live = jnp.broadcast_to(mask.astype(F32)[None, :], (SUBLANES, points))
-        near = jnp.where(mask[None, :] > 0, neighbours, -1).astype(jnp.int16)
-        near = jnp.broadcast_to(near[:, None, :], (depth, 16, points))
-
-        def layout(subs):
-            per = SUBLANES // subs
-            value = neighbours.reshape(depth, points // per, per) * subs
-            value = value + (SUBLANES - subs * jnp.arange(per, dtype=jnp.int32))
-            return value.transpose(0, 2, 1).reshape(-1)
-
-        index1, index2 = layout(1), layout(2)
+        mask_row = mask[None, :]
         groups1, groups2 = points // SUBLANES, points // 4
+
+        def layout(subs, groups):
+            place = jnp.arange(points, dtype=jnp.int32) // groups
+            return (neighbours * subs + (SUBLANES - subs * place)).reshape(-1)
+
+        index1, index2 = layout(1, groups1), layout(2, groups2)
         block = 32
-        anywhere = pl.BlockSpec(memory_space=pl.ANY)
         outs = pl.pallas_call(
             functools.partial(forward_kernel, (cores, total)),
             out_shape=[
@@ -1056,19 +1292,31 @@
                 shaped(points, width1),
                 shaped(both, width1),
                 shaped(both, LANES),
+                shaped(both, width1),
                 shaped(SUBLANES, width1),
                 shaped(2 * points, LANES),
                 shaped(both, width2),
-                shaped(both, width1),
                 shaped(points, width1),
                 shaped(width1, width2),
                 shaped(SUBLANES, width2),
             ],
-            in_specs=[VMEM] * 3 + [SMEM] * 3 + [VMEM] * 7,
-            out_specs=[VMEM, anywhere, anywhere] + [VMEM] * 14,
+            in_specs=[VMEM] * 3 + [ANY] * 2 + [SMEM] + [VMEM] * 3 + [ANY] + [VMEM] * 3,
+            out_specs=[VMEM] + [ANY] * 10 + [VMEM] * 6,
             scratch_shapes=[
+                pltpu.SMEM((depth * points,), jnp.int32),
+                pltpu.SMEM((depth * points,), jnp.int32),
+                scratch(width2, 2 * width1),
+                scratch(points, width1),
+                scratch(points, width1),
+                scratch(points, width1),
+                scratch(both, cin),
+                scratch(points, width1),
+                scratch(both, width1),
+                scratch(both, LANES),
                 scratch(cores, cin, points),
+                scratch(both, LANES, dtype=BF16),
                 scratch(both, points, dtype=BF16),
+                scratch(SUBLANES, points),
                 scratch(points, LANES),
                 scratch(cores, 3 * cin, points, dtype=BF16),
                 scratch(2 * width1, both, dtype=BF16),
@@ -1077,6 +1325,8 @@
                 scratch(points, cin),
                 scratch(points, width1),
                 scratch(both + 2 * SUBLANES, LANES),
+                scratch(points, LANES),
+                scratch(points, LANES),
                 scratch(points, LANES),
                 scratch(points, LANES),
                 scratch(2 * both + 2 * SUBLANES, LANES),
@@ -1089,7 +1339,7 @@
                 scratch(points, width2),
                 scratch(both, width2),
                 scratch(points, width2),
-                scratch(both, 2 * cin),
+                scratch(points, 2 * width2, dtype=BF16),
                 scratch(cores, 3 * clouds, SUBLANES, LANES),
                 scratch(3, 4, LANES),
                 scratch(3, total, 4, LANES),
@@ -1099,6 +1349,8 @@
                 pltpu.SemaphoreType.DMA((2, 3)),
                 pltpu.SemaphoreType.DMA((2, 3)),
                 pltpu.SemaphoreType.DMA((2,)),
+                pltpu.SemaphoreType.DMA((3,)),
+                pltpu.SemaphoreType.DMA((8,)),
             ],
             compiler_params=pltpu.CompilerParams(
                 collective_id=1, has_side_effects=True, vmem_limit_bytes=MEMORY
@@ -1106,8 +1358,8 @@
             name="forward",
         )(
             features,
-            near,
-            live,
+            neighbours,
+            mask_row,
             index1,
             index2,
             lengths,
@@ -1130,72 +1382,87 @@
             away_own1,
             away_all1,
             counts,
+            x2,
             scales1,
             push2,
             extra2,
-            x2,
             own2,
             grad_own2,
             scales2,
         ) = outs
 
-        def q_blocks():
-            return pl.BlockSpec((block, depth, SUBLANES, LANES), lambda s: (s, 0, 0, 0))
-
-        near2, grad_near2 = pl.pallas_call(
+        ring = scratch(3, block, depth, SUBLANES, LANES)
+        kept, sent, grad_near2 = pl.pallas_call(
             functools.partial(scatter2_kernel, depth),
-            grid=(groups2 // block,),
-            out_shape=[shaped(both, width1), shaped(width1, width2)],
-            in_specs=[SMEM, q_blocks()] + [VMEM] * 5,
-            out_specs=[VMEM, VMEM],
-            scratch_shapes=[scratch(2 * both + 2 * SUBLANES, LANES)] * 8,
+            out_shape=[shaped(points, width1), shaped(points, width1), shaped(width1, width2)],
+            in_specs=[ANY] * 5 + [VMEM, ANY],
+            out_specs=[VMEM] * 3,
+            scratch_shapes=[
+                pltpu.SMEM((depth * points,), jnp.int32),
+                scratch(2 * points, LANES),
+                scratch(both, width1),
+                scratch(width2, 2 * width1),
+                scratch(both, width2),
+                ring,
+                pltpu.SemaphoreType.DMA((5,)),
+                pltpu.SemaphoreType.DMA((3,)),
+            ]
+            + [scratch(2 * both + 2 * SUBLANES, LANES)] * 8,
             compiler_params=pltpu.CompilerParams(vmem_limit_bytes=MEMORY),
             name="scatter2",
         )(index2, q2, push2, x2, second_layer_weight, scales2, extra2)
-
-        core = lax.axis_index("points")
-        sent = lax.dynamic_slice(near2, ((1 - core) * points, 0), (points, width1))
-        kept = lax.dynamic_slice(near2, (core * points, 0), (points, width1))
         other = lax.ppermute(sent, "points", [(0, 1), (1, 0)])
-        grad1 = own2 + kept + other
 
         near1, given1, parts = pl.pallas_call(
             functools.partial(scatter1_kernel, depth),
-            grid=(groups1 // block,),
             out_shape=[shaped(both, width1), shaped(points, width1), shaped(SUBLANES, width1)],
-            in_specs=[SMEM, q_blocks()] + [VMEM] * 4,
+            in_specs=[ANY] * 2 + [VMEM] * 6,
             out_specs=[VMEM] * 3,
-            scratch_shapes=[scratch(points, width1)]
+            scratch_shapes=[
+                pltpu.SMEM((depth * points,), jnp.int32),
+                scratch(points, width1),
+                ring,
+                pltpu.SemaphoreType.DMA((1,)),
+                pltpu.SemaphoreType.DMA((3,)),
+            ]
             + [scratch(both + 2 * SUBLANES, LANES)] * SUBLANES,
             compiler_params=pltpu.CompilerParams(vmem_limit_bytes=MEMORY),
             name="scatter1",
-        )(index1, q1, grad1, inverse1, share1, moment1)
-
-        piece = -(-5 * LANES // (total * SUBLANES)) * SUBLANES
-        side = chips * piece
-        grad_features, grad_weight1, grad_gain1, grad_bias1, grad_weight2 = pl.pallas_call(
+        )(index1, q1, own2, kept, other, inverse1, share1, moment1)
+
+        def piece_of(rows):
+            return -(-rows // (total * SUBLANES)) * SUBLANES
+
+        piece1, piece2 = piece_of(LANES), piece_of(4 * LANES)
+        side1, side2 = chips * piece1, chips * piece2
+        from_own, from_near, norm1, whole1, whole2 = pl.pallas_call(
             functools.partial(last_kernel, (cores, chips), depth),
             out_shape=[
                 shaped(cin, points),
-                shaped(width1, 2 * cin),
-                shaped(1, width1),
-                shaped(1, width1),
-                shaped(width2, 2 * width1),
+                shaped(cin, points),
+                shaped(SUBLANES, width1),
+                shaped(cores, chips, piece1, LANES),
+                shaped(cores, chips, piece2, LANES),
             ],
             in_specs=[VMEM] * 12,
             out_specs=[VMEM] * 5,
             scratch_shapes=[
                 scratch(total, SUBLANES, LANES),
-                scratch(cores * side, LANES),
+                scratch(cores * side1, LANES),
+                scratch(cores * side2, LANES),
                 scratch(cores, cin, points),
                 scratch(cin, points),
-                scratch(side, LANES),
-                scratch(chips, piece, LANES),
-                scratch(piece, LANES),
-                scratch(cores, chips, piece, LANES),
+                scratch(side1, LANES),
+                scratch(side2, LANES),
+                scratch(chips, piece1, LANES),
+                scratch(chips, piece2, LANES),
+                scratch(piece1, LANES),
+                scratch(piece2, LANES),
+                scratch(cores, chips, piece1, LANES),
+                scratch(cores, chips, piece2, LANES),
                 pltpu.SemaphoreType.DMA((2,)),
-                pltpu.SemaphoreType.DMA((2, 3)),
-                pltpu.SemaphoreType.DMA((2, 2)),
+                pltpu.SemaphoreType.DMA((2, 5)),
+                pltpu.SemaphoreType.DMA((2, 4)),
             ],
             compiler_params=pltpu.CompilerParams(
                 collective_id=2, has_side_effects=True, vmem_limit_bytes=MEMORY
@@ -1210,20 +1477,38 @@
             away_all1,
             counts,
             scales1,
-            live,
+            mask_row,
             first_layer_weight,
             grad_own2,
             grad_near2,
         )
-        return (
+        outs = pl.pallas_call(
+            finish_kernel,
+            out_shape=[
+                shaped(clouds, 2 * width2),
+                shaped(cin, points),
+                shaped(width1, 2 * cin),
+                shaped(1, width1),
+                shaped(1, width1),
+                shaped(width2, 2 * width1),
+                shaped(1, width2),
+                shaped(1, width2),
+            ],
+            in_specs=[VMEM] * 7,
+            out_specs=[VMEM] * 8,
+            compiler_params=pltpu.CompilerParams(vmem_limit_bytes=MEMORY),
+            name="finish",
+        )(
+            from_own,
+            from_near,
+            norm1,
+            whole1.reshape(cores * side1, LANES),
+            whole2.reshape(cores * side2, LANES),
+            scales2,
             pooled,
-            grad_features,
-            grad_weight1,
-            grad_gain1.reshape(width1),
-            grad_bias1.reshape(width1),
-            grad_weight2,
-            scales2[2],
-            scales2[1],
+        )
+        return tuple(
+            value.reshape(-1) if value.shape[0] == 1 else value for value in outs
         )
 
     return on_device

time: 244 us -> 185 us (0.76)
  Pallas kernels: 223 us -> 178 us
  local copies, waits for them, and re-layouts: 14.7 us -> 2.12 us
  other arithmetic: 4.49 us -> 0.92 us
    pallas_call x1, Pallas kernels: 141 us -> 103 us  [on_device(): pl.pallas_call(functools.partial(forward_kernel, (cores, total)), out_sha...]
    unnamed x12 -> x2, local copies, waits for them, and re-layouts: 9.41 us -> 0.81 us
    pallas_call x2 -> x3, Pallas kernels: 49.4 us -> 45.3 us  [the longest x1 22.6 us: on_device(): pl.pallas_call(functools.partial(scatter2_kernel, depth), out_shape=[shap...]
    pallas_call x1, Pallas kernels: 32.9 us -> 29.8 us  [on_device(): pl.pallas_call(functools.partial(last_kernel, (cores, chips), depth), out...]
  transfers between devices with their start and end apart: 1 -> 1, of which waited for: 1 -> 1; matrix products, arithmetic and copies ran while one was open for 1% -> 0% of each run, Pallas kernels for 0% -> 0%
where the time goes in v2:
time: 185 us; the launch traced here: 184 us
  Pallas kernels  178 us (96%)
  local copies, waits for them, and re-layouts  2.12 us (1%)
  waiting for transfers between devices  1.93 us (1%)
    pallas_call x1, Pallas kernels, on_device(): pl.pallas_call(functools.partial(forward_kernel, (cores, total)), out_sha...  103 us
    pallas_call x1, Pallas kernels, on_device(): pl.pallas_call(functools.partial(last_kernel, (cores, chips), depth), out...  29.8 us
    pallas_call x1, Pallas kernels, on_device(): pl.pallas_call(functools.partial(scatter2_kernel, depth), out_shape=[shap...  22.6 us
    pallas_call x1, Pallas kernels, on_device(): pl.pallas_call(functools.partial(scatter1_kernel, depth), out_shape=[shap...  20.6 us
  transfers between devices with their start and end apart: 1, of which 1 were waited for; matrix products, arithmetic and copies ran while one was open for 0% of the time, Pallas kernels for 0%

profile of v2, /device:TPU:0, one launch (start us, length us, event | category | flops | bytes accessed | tf_op | source)
XLA Modules:
  0.0 184.1 jit_solution(1763218858576630154)
XLA Ops:
  0.6 0.9 multiply_add_fusion
  1.6 0.7 reshape.69.index2_in.index_in
  2.2 0.7 reshape.68.index1_in.index_in
  2.9 103.1 %forward.1 = (f32[4,512]{1,0:T(4,128)}, f32[128,20,8,128]{3,2,1,0:T(8,128)}, f32[256,20,8,128]{3,2,1,0:T(8,128)}, f32[1024,128]{1,0:T(8,128)}, f32[1024,128]{1,0...) custom-call(f32[64,1024]{1,0:T(8,128)} %feat.1, ...), custom_call_target="tpu_custom_call" | custom-call | tf_op jit(solution)/shard_map/forward/pallas_call | solution.py:1282
  106.0 22.6 %scatter2.1 = (f32[1024,128]{1,0:T(8,128)}, f32[1024,128]{1,0:T(8,128)}, f32[128,256]{1,0:T(8,128)}) custom-call(s32[20480]{0:T(1024)} %reshape.69.index2_in.index_in, f32[256,20,8,128]{3,2,1,0:T(8,128)} %get-tuple-element.46.q_hbm, f32[2048,128]{1,0:T(8,128)} %get-tuple-element.47.push_in, f32[2048,128]{1,0:T(8,128)} %get-tuple-element.48.x2_in, ...), custom_call_target="tpu_custom_call" | custom-call | tf_op jit(solution)/shard_map/scatter2/pallas_call | solution.py:1395
  128.6 0.3 collective-permute-start
  128.8 1.9 %collective-permute-done.other = f32[1024,128]{1,0:T(8,128)S(1)} collective-permute-done((f32[1024,128]{1,0:T(8,128)}, f32[1024,128]{1,0:T(8,128)S(1)}, u32[]{:S(2)}, u32[]{:S(2)}) %collective-permute-start) | collective-permute-done | bytes 524320 | tf_op jit(solution)/shard_map/ppermute | solution.py:1414
  130.8 0.0 copy-start
  130.8 0.8 copy-done
  131.6 20.6 %scatter1.1 = (f32[2048,128]{1,0:T(8,128)}, f32[1024,128]{1,0:T(8,128)}, f32[8,128]{1,0:T(8,128)}) custom-call(s32[20480]{0:T(1024)} %reshape.68.index1_in.index_in, f32[128,20,8,128]{3,2,1,0:T(8,128)} %get-tuple-element.44.q_hbm, f32[1024,128]{1,0:T(8,128)} %get-tuple-element.45.own, f32[1024,128]{1,0:T(8,128)} %get-tuple-element.51.kept, ...), custom_call_target="tpu_custom_call" | custom-call | tf_op jit(solution)/shard_map/scatter1/pallas_call | solution.py:1416
  152.2 29.8 %last.1 = (f32[64,1024]{1,0:T(8,128)}, f32[64,1024]{1,0:T(8,128)}, f32[8,128]{1,0:T(8,128)}, f32[2,16,8,128]{3,2,1,0:T(8,128)}, f32[2,16,16,128]{3,2,1,0:T(8,128)}) custom-call(f32[2048,128]{1,0:T(8,128)} %get-tuple-element.56.near1, f32[1024,128]{1,0:T(8,128)} %get-tuple-element.57.given1, f32[8,128]{1,0:T(8,128)} %get-tuple-element.58.parts, ...), custom_call_target="tpu_custom_call" | custom-call | tf_op jit(solution)/shard_map/last/pallas_call | solution.py:1438
  182.0 2.1 %finish.1 = (f32[4,512]{1,0:T(4,128)}, f32[64,1024]{1,0:T(8,128)}, f32[128,128]{1,0:T(8,128)}, f32[1,128]{1,0:T(1,128)}, f32[1,128]{1,0:T(1,128)}, /*index=5*/f3...) custom-call(f32[64,1024]{1,0:T(8,128)} %get-tuple-element.66.from_own, f32[64,1024]{1,0:T(8,128)} %get-tuple-element.67.from_near, ...), custom_call_target="tpu_custom_call" | custom-call | tf_op jit(solution)/shard_map/finish/pallas_call | solution.py:1485
  (1 shorter events, 0.0 us)
Async XLA Ops:
  128.6 2.2 %collective-permute-start = (f32[1024,128]{1,0:T(8,128)}, f32[1024,128]{1,0:T(8,128)S(1)}, u32[]{:S(2)}, u32[]{:S(2)}) collective-permute-start(f32[1024,128]{1,0:T(8,128)} %get-tuple-element.52), channel_id=1, source_target_pairs={{0,1},{1,0},{2,3},{3,2},{4,5},{5,4},{6,7},{7,6},{8,9},{9,8},{10,11... | collective-permute-start | bytes 1572872 | tf_op jit(solution)/shard_map/ppermute | solution.py:1414
  130.8 0.8 copy-start

commit v3 on v2

--- a/solution.py
+++ b/solution.py
@@ -86,10 +86,6 @@
     lax.fori_loop(0, count // step, run, 0)
 
 
-def log2(value):
-    return jnp.log(value) * LOG2E
-
-
 def tree(values, join):
     values = list(values)
     while len(values) > 1:
@@ -171,7 +167,9 @@
     )
 
 
-def edge_pass(subs, block, depth, part, index, table, own_rows, out_hbm, held, ring, sems, outs):
+def edge_pass(
+    subs, block, depth, part, index, table, own_rows, out_hbm, held, ring, sems, outs, pending, after_block
+):
     level_ref, share_ref, moment_ref, inverse_ref = outs
     per = SUBLANES // subs
     groups = own_rows.shape[0] // SUBLANES
@@ -203,14 +201,15 @@
         top = own_rows[rows, :] + peak
         shift = jnp.maximum(top, 0.0)
         rest = jnp.maximum(jnp.exp2(-shift), 2.0**-100)
-        scale = jnp.exp2(top - shift)
+        under = jnp.maximum(jnp.minimum(top, 0.0), -100.0)
+        offset = under - peak
         fifth = 0.2 * rest
         total, share, moment = [], [], []
         for k in range(part):
             value = held[slot][stage * part + k]
-            away = value - peak
-            grown = scale * jnp.exp2(away)
-            root = jnp.exp2((away - log2(rest + grown)) * 0.2)
+            power = value + offset
+            grown = jnp.exp2(power)
+            root = jnp.exp2((power - lax.log2(rest + grown)) * 0.2)
             weight = root * (fifth + grown)
             ring[ring_slot, place, stage * part + k] = weight
             total.append(root)
@@ -226,7 +225,8 @@
             moment = moment + jnp.where(start, 0.0, moment0)
         mass = share + (0.8 * rest) * total
         inverse = 1.0 / mass
-        level_ref[rows, :] = LN2 * (0.2 * top + 0.8 * shift + log2(mass)) - math.log(depth)
+        level = 0.2 * (top - under) + 0.8 * shift + lax.log2(mass)
+        level_ref[rows, :] = LN2 * level - math.log(depth)
         inverse_ref[rows, :] = inverse
         share_ref[rows, :] = share * inverse
         moment_ref[rows, :] = moment * inverse
@@ -236,7 +236,7 @@
 
     def push(b, slot):
         return pltpu.make_async_copy(
-            ring.at[slot], out_hbm.at[pl.ds(b * block, block)], sems.at[slot]
+            ring.at[slot, pl.ds(0, block)], out_hbm.at[pl.ds(b * block, block)], sems.at[slot]
         )
 
     for stage in range(stages):
@@ -245,9 +245,21 @@
     def one_block(b, carry):
         ring_slot = lax.rem(b, 2)
 
-        @pl.when(b >= 2)
-        def _():
-            push(b - 2, ring_slot).wait()
+        if pending is None:
+
+            @pl.when(b >= 2)
+            def _():
+                push(b - 2, ring_slot).wait()
+
+        else:
+
+            @pl.when(b < 2)
+            def _():
+                pending(ring_slot).wait()
+
+            @pl.when(b >= 2)
+            def _():
+                push(b - 2, ring_slot).wait()
 
         def pair(t, inner):
             for slot in range(2):
@@ -269,12 +281,12 @@
 
         lax.fori_loop(0, block // 2, pair, 0)
         push(b, ring_slot).start()
+        if after_block is not None:
+            after_block(b)
         return carry
 
     lax.fori_loop(0, blocks, one_block, 0)
-    if blocks > 1:
-        push(blocks - 2, (blocks - 2) % 2).wait()
-    push(blocks - 1, (blocks - 1) % 2).wait()
+    return lambda slot: push(blocks - 2 + slot, slot)
 
 
 def lanes_to_rows(value, width):
@@ -311,12 +323,15 @@
     away_all1_out,
     counts_out,
     x2_out,
+    push2_out,
+    extra2_out,
     scales1,
-    push2,
-    extra2,
     own2,
     grad_own2,
     scales2,
+    known1,
+    push2,
+    extra2,
     index1,
     index2,
     weight2,
@@ -329,6 +344,7 @@
     counts,
     x1_cm,
     tallies,
+    lows,
     links,
     live,
     live_col,
@@ -341,6 +357,7 @@
     table1,
     own_rows1,
     level1,
+    other1,
     share_rows1,
     moment_rows1,
     table2,
@@ -386,6 +403,10 @@
     ]
     for copy in loads:
         copy.start()
+    late = [
+        pltpu.make_async_copy(source, target, store_sems.at[8 + i])
+        for i, (source, target) in enumerate(((push2, push2_out), (extra2, extra2_out)))
+    ]
     stores = [
         pltpu.make_async_copy(source, target, store_sems.at[i])
         for i, (source, target) in enumerate(
@@ -407,21 +428,28 @@
     one, none = jnp.ones((16, LANES), BF16), jnp.zeros((16, LANES), BF16)
 
     def build(columns, first):
-        names = []
+        high_names, low_names = [], []
         for k in range(depth):
-            name = jnp.where(mask[:, columns] > 0, near[k : k + 1, columns], -1)
-            names.append(jnp.broadcast_to(name, (16, LANES)).astype(jnp.int16))
-
-        def rows64(start):
-            for s in range(0, 64, 16):
-                target = (row16 + (start + s)).astype(jnp.int16)
-                found = [jnp.where(name == target, one, none) for name in names]
-                found = tree(found, jnp.add)
-                links[pl.ds(start + s, 16), columns] = found
+            name = near[k : k + 1, columns]
+            high = jnp.where(mask[:, columns] > 0, lax.shift_right_logical(name, 7), -1)
+            for names, value in ((high_names, high), (low_names, name & (LANES - 1))):
+                names.append(jnp.broadcast_to(value, (16, LANES)).astype(jnp.int16))
+        for s in range(0, LANES, 16):
+            target = (row16 + s).astype(jnp.int16)
+            for k in range(depth):
+                lows[k, s : s + 16, :] = jnp.where(low_names[k] == target, one, none)
+
+        def one_high(start):
+            target = jnp.full((16, LANES), lax.shift_right_logical(start, 7), jnp.int32)
+            target = target.astype(jnp.int16)
+            meant = [jnp.where(name == target, one, none) for name in high_names]
+            for s in range(0, LANES, 16):
+                found = tree([meant[k] * lows[k, s : s + 16, :] for k in range(depth)], jnp.add)
                 here = pl.ds(start + s, 16)
+                links[here, columns] = found
                 tallies[here, :] = found if first else tallies[here, :] + found
 
-        over(both, 64, rows64)
+        over(both, LANES, one_high)
 
     tiles = points // LANES
     early = tiles - tiles // 4
@@ -577,9 +605,17 @@
     stores[2].start()
     stores[3].start()
     loads[0].wait()
-    edge_pass(
+    block1, block2 = groups1 // 4, ring.shape[1]
+    block_rows = block1 * SUBLANES
+    blocks1 = 4
+
+    def hand_over(b):
+        rows = pl.ds(pl.multiple_of(b * block_rows, block_rows), block_rows)
+        return to_partner(level1.at[rows], other1.at[rows], pair_sems, 3 + b)
+
+    pending = edge_pass(
         1,
-        ring.shape[1],
+        block1,
         depth,
         depth // 2,
         index1,
@@ -590,6 +626,8 @@
         ring,
         ring_sems,
         (level1, share_rows1, moment_rows1, inverse1),
+        None,
+        lambda b: hand_over(b).start(),
     )
 
     inverse_gain1 = 1.0 / (gain1[...] * LOG2E)
@@ -602,12 +640,14 @@
         share1[rows, :] = share_rows1[here, :]
     for copy in stores[4:7]:
         copy.start()
-    here = x2.at[pl.ds(half, points)]
-    swap = to_partner(here, here, pair_sems, 1)
-    swap.start()
     loads[1].wait()
     loads[2].wait()
-    swap.wait()
+    for b in range(blocks1):
+        hand_over(b).wait()
+    other_half = pl.multiple_of((1 - core) * points, points)
+    for i in range(SUBLANES):
+        here = pl.ds(i, groups1, stride=SUBLANES)
+        x2[pl.ds(other_half + i * groups1, groups1), :] = other1[here, :]
     stores[7].start()
 
     direct2 = weight2[:, :width1] - weight2[:, width1:]
@@ -699,9 +739,9 @@
                 :, h * LANES : (h + 1) * LANES
             ]
 
-    edge_pass(
+    pending = edge_pass(
         2,
-        ring.shape[1],
+        block2,
         depth,
         depth,
         index2,
@@ -712,6 +752,8 @@
         ring,
         ring_sems,
         (level2, share2, moment2, inverse2),
+        pending,
+        None,
     )
 
     clouds = pooled_grad.shape[0]
@@ -825,8 +867,27 @@
 
     state = unrolled(gradient, (zero, zero), 8)
     grad_beta, grad_gamma = [by_parity(value, jnp.add) for value in state]
+    late[0].start()
     send_sums(2, [grad_beta[0:1], grad_beta[1:2], grad_gamma[0:1], grad_gamma[1:2]])
 
+    known1[...] = jnp.zeros(known1.shape, F32)
+
+    def known(start):
+        near_rows = pl.ds(start, CHUNK)
+        known1[0, cin:, :] += t_by(x1[near_rows, :], away_all1[near_rows, :])
+        known1[1, cin:, :] += t_by(x1[near_rows, :], counts[near_rows, :])
+
+    over(both, CHUNK, known)
+
+    def known_own(start):
+        rows = pl.ds(start, CHUNK)
+        here = x1[pl.ds(half + start, CHUNK), :]
+        known1[0, 0:cin, :] += t_by(here, away_own1[rows, :])
+        known1[1, 0:cin, :] += t_by(here, depth * live_col[rows, :])
+
+    over(points, CHUNK, known_own)
+    for i in range(2):
+        known1[i, cin:, :] -= known1[i, 0:cin, :]
     receive(2)
     sums = slot_sum(slots.at[2], total)
     grad_beta = rows_to_lanes([sums[0:1], sums[1:2]])
@@ -844,6 +905,7 @@
         extra2[rows, :] = weights * beta_scale + away * gamma_scale
 
     over(both, CHUNK, extra)
+    late[1].start()
     grad_own2[...] = jnp.zeros(grad_own2.shape, F32)
 
     for i in range(SUBLANES // 2):
@@ -856,11 +918,11 @@
         value = given * slope2 - (depth * weights * beta_scale + away * gamma_scale)
         own2[rows, :] = by(value, direct2)
         grad_own2[...] += t_by(x2[pl.ds(half + i * groups2, groups2), :], value)
-    for copy in stores:
+    for copy in stores + late + [pending(0), pending(1)]:
         copy.wait()
 
 
-def scatter_loop(subs, depth, index, q_hbm, ring, sems, push, sums, clear):
+def scatter_loop(subs, depth, part, index, q_hbm, ring, sems, push, sums, clear):
     per = SUBLANES // subs
     groups = q_hbm.shape[0]
     slots, block = ring.shape[0], ring.shape[1]
@@ -868,6 +930,7 @@
     row = iota((SUBLANES, LANES), 0)
     mine = [(row >= subs * i) & (row < subs * (i + 1)) for i in range(per)]
     ways = len(sums) // per
+    stages = depth // part
 
     def pull(b):
         slot = lax.rem(b, slots)
@@ -891,12 +954,24 @@
             group = b * block + place
             rows = pl.ds(pl.multiple_of(group * SUBLANES, SUBLANES), SUBLANES)
             given = push[rows, :]
-            for k in range(depth):
-                value = ring[slot, place, k] * given
-                for i in range(per):
-                    j = index.at[pl.ds((k * per + i) * groups, groups)][group]
-                    target = sums[i * ways + k % ways].at[pl.ds(j, SUBLANES), :]
-                    pltpu.store(target, target[...] + value, mask=mine[i])
+
+            def one_part(stage):
+                for k in range(part):
+                    value = ring[slot, place, stage * part + k] * given
+                    for i in range(per):
+                        first = (k * per + i) * groups
+                        if stages > 1:
+                            span = groups * (1 + (stages - 1) * part * per)
+                            j = index.at[pl.ds(first, span)][stage * (part * per * groups) + group]
+                        else:
+                            j = index.at[pl.ds(first, groups)][group]
+                        target = sums[i * ways + k % ways].at[pl.ds(j, SUBLANES), :]
+                        pltpu.store(target, target[...] + value, mask=mine[i])
+
+            if stages == 1:
+                one_part(0)
+            else:
+                lax.fori_loop(0, stages, lambda stage, c: (one_part(stage), c)[1], 0)
             return inner
 
         lax.fori_loop(0, block, one_group, 0)
@@ -950,13 +1025,15 @@
     ]
 
     def prepare():
+        for copy in loads[2:]:
+            copy.start()
         clear(sums)
         loads[0].wait()
         loads[1].wait()
 
-    for copy in loads:
+    for copy in loads[:2]:
         copy.start()
-    scatter_loop(2, depth, index, q_hbm, ring, ring_sems, push, sums, prepare)
+    scatter_loop(2, depth, depth, index, q_hbm, ring, ring_sems, push, sums, prepare)
     for copy in loads[2:]:
         copy.wait()
     points, width = kept.shape
@@ -1019,7 +1096,7 @@
         parts[...] = jnp.concatenate([grad_beta, grad_gamma, jnp.zeros((6, LANES), F32)], axis=0)
         load.wait()
 
-    scatter_loop(1, depth, index, q_hbm, ring, ring_sems, push, sums, prepare)
+    scatter_loop(1, depth, depth // 1, index, q_hbm, ring, ring_sems, push, sums, prepare)
 
     def finish(start):
         here = pl.ds(SUBLANES + start, CHUNK)
@@ -1031,23 +1108,33 @@
 def last_kernel(
     sizes,
     depth,
-    near1,
-    given1,
+    near1_in,
+    given1_in,
     parts,
-    x1,
-    away_own1,
-    away_all1,
-    counts,
+    x1_in,
+    away_own1_in,
+    away_all1_in,
+    counts_in,
     scales1,
     mask,
     weight1,
-    grad_own2,
-    grad_near2,
+    grad_own2_in,
+    grad_near2_in,
+    known1_in,
     from_own,
     from_near,
     norm1,
     whole1,
     whole2,
+    near1,
+    given1,
+    x1,
+    away_own1,
+    away_all1,
+    counts,
+    grad_own2,
+    grad_near2,
+    known1,
     slots,
     flat1,
     flat2,
@@ -1064,6 +1151,7 @@
     small_sems,
     pair_sems,
     ring_sems,
+    load_sems,
 ):
     cores, chips = sizes
     total = cores * chips
@@ -1075,6 +1163,24 @@
     half = pl.multiple_of(core * points, points)
     barrier = pltpu.get_barrier_semaphore()
     signal_all(barrier, cores, total)
+    loads = [
+        pltpu.make_async_copy(source, target, load_sems.at[i])
+        for i, (source, target) in enumerate(
+            (
+                (x1_in, x1),
+                (near1_in, near1),
+                (given1_in, given1),
+                (known1_in, known1),
+                (grad_own2_in, grad_own2),
+                (grad_near2_in, grad_near2),
+                (counts_in, counts),
+                (away_all1_in, away_all1),
+                (away_own1_in, away_own1),
+            )
+        )
+    ]
+    for copy in loads:
+        copy.start()
 
     def chip_copy(d, source, target, use):
         return pltpu.make_async_remote_copy(
@@ -1088,46 +1194,33 @@
 
     class Summed:
         def __init__(self, flat, halved, landed, reduced, whole, first):
-            self.flat, self.halved, self.landed, self.reduced, self.whole = (
-                flat,
-                halved,
-                landed,
-                reduced,
-                whole,
-            )
-            self.first = first
-            self.piece = landed.shape[1]
-            self.side = chips * self.piece
-            self.mine = pl.multiple_of(core * self.side, SUBLANES)
-            other = pl.multiple_of((1 - core) * self.side, SUBLANES)
-            self.swap = to_partner(flat.at[pl.ds(other, self.side)], halved, pair_sems, first)
+            self.flat, self.halved, self.landed = flat, halved, landed
+            self.reduced, self.whole, self.first = reduced, whole, first
+            self.swap = to_partner(flat.at[1 - core], halved, pair_sems, first)
             here = whole.at[core]
             self.back = to_partner(here, here, pair_sems, first + 1)
 
         def scatter(self):
             self.swap.wait()
-            self.flat[pl.ds(self.mine, self.side), :] += self.halved[...]
-            start = pl.multiple_of(self.mine + chip * self.piece, SUBLANES)
-            self.landed[chip] = self.flat[pl.ds(start, self.piece), :]
+            self.flat[core] += self.halved[...]
+            self.landed[chip] = self.flat[core, chip]
 
             def send(d, carry):
-                to = lax.rem(chip + d, chips)
-                place = pl.multiple_of(self.mine + to * self.piece, SUBLANES)
-                source = self.flat.at[pl.ds(place, self.piece)]
+                source = self.flat.at[core, lax.rem(chip + d, chips)]
                 chip_copy(d, source, self.landed.at[chip], self.first).start()
                 return carry
 
             lax.fori_loop(1, chips, send, 0)
 
-        def wait(self, use):
-            others = self.landed.at[pl.ds(0, chips - 1)]
+        def wait(self, ref, use):
+            others = ref.at[pl.ds(0, chips - 1)]
             arrival = chip_copy(1, others, others, use)
             arrival.wait_recv()
             arrival.wait_send()
 
-        def spread(self):
-            self.wait(self.first)
-            self.reduced[...] = slot_sum(self.landed, chips)
+        def spread(self, change):
+            self.wait(self.landed, self.first)
+            self.reduced[...] = change(slot_sum(self.landed, chips))
             self.whole[core, chip] = self.reduced[...]
 
             def send(d, carry):
@@ -1137,74 +1230,109 @@
             lax.fori_loop(1, chips, send, 0)
 
         def finish(self):
-            self.wait(self.first + 1)
+            self.wait(self.whole.at[core], self.first + 1)
             self.back.start()
 
     sum1 = Summed(flat1, halved1, landed1, reduced1, all1, 0)
     sum2 = Summed(flat2, halved2, landed2, reduced2, all2, 2)
-    for flat, rows in ((flat1, LANES), (flat2, 4 * LANES)):
-        if flat.shape[0] > rows:
-            flat[rows:, :] = jnp.zeros((flat.shape[0] - rows, LANES), F32)
-    for h in range(2):
-        columns = slice(h * LANES, (h + 1) * LANES)
-        flat2[h * LANES : (h + 1) * LANES, :] = grad_own2[:, columns]
-        flat2[(2 + h) * LANES : (3 + h) * LANES, :] = grad_near2[:, columns] - grad_own2[:, columns]
     direct1 = weight1[:, :cin] - weight1[:, cin:]
     relative1 = weight1[:, cin:]
     slope = scales1[0:1, :]
     r1 = scales1[1:2, :]
     outer_scale = slope / scales1[2:3, :]
 
+    pieces = [(n // chips, n % chips) for n in range(total)]
+    size1 = -(-2 * cin // total)
+    size2 = reduced2.shape[0]
+    blocks2 = 4 * LANES // size2
+    for copy in loads[:6]:
+        copy.wait()
+
+    def sums_of(count, base, values):
+        def add(i, carry):
+            start = pl.multiple_of(i * CHUNK, CHUNK)
+            rows = pl.ds(start, CHUNK)
+            return carry + t_by(x1[pl.ds(base + start, CHUNK), :], values[rows, :])
+
+        return lax.fori_loop(0, count // CHUNK, add, jnp.zeros((cin, width1), F32))
+
+    grad_own1 = sums_of(points, half, given1) * slope
+    grad_near1 = sums_of(cores * points, 0, near1) * slope
+    summed = [
+        jnp.concatenate([grad_own1, grad_near1 - grad_own1], axis=0),
+        known1[0],
+        known1[1],
+    ]
+    flat1[...] = jnp.zeros(flat1.shape, F32)
+    for n, (c, place) in enumerate(pieces):
+        if n * size1 < 2 * cin:
+            for i, value in enumerate(summed):
+                flat1[c, place, i * size1 : (i + 1) * size1, :] = value[
+                    n * size1 : (n + 1) * size1
+                ]
+    flat2[...] = jnp.zeros(flat2.shape, F32)
+    for n, (c, place) in enumerate(pieces[:blocks2]):
+        block, row = divmod(n * size2, LANES)
+        columns = slice(block % 2 * LANES, (block % 2 + 1) * LANES)
+        value = grad_own2[row : row + size2, columns]
+        if block >= 2:
+            value = grad_near2[row : row + size2, columns] - value
+        flat2[c, place] = value
+
     pl.semaphore_wait(barrier, total - 1)
+    sum1.swap.start()
     sum2.swap.start()
     gather_start(parts, slots, small_sems.at[0], small_sems.at[1], cores, total)
+    sum1.scatter()
     sum2.scatter()
+    for copy in loads[6:]:
+        copy.wait()
     gather_wait(slots, small_sems.at[0], small_sems.at[1], total)
     sums = slot_sum(slots, total)
     norm1[...] = sums
     beta_scale = outer_scale * sums[0:1]
     gamma_scale = outer_scale * sums[1:2] * r1
 
-    grad_near1 = jnp.zeros((cin, width1), F32)
+    def corrected(value):
+        main, gamma_part, beta_part = [
+            value[i * size1 : (i + 1) * size1] for i in range(3)
+        ]
+        main = main - (gamma_part * gamma_scale + beta_part * beta_scale)
+        if size1 == SUBLANES:
+            return main
+        return jnp.concatenate([main, jnp.zeros((SUBLANES - size1, LANES), F32)], axis=0)
+
+    sum1.spread(corrected)
+    sum2.spread(lambda value: value)
     for c in range(cores):
 
-        def push(i, total_near):
-            start = pl.multiple_of(i * CHUNK, CHUNK)
+        def push(start):
             rows = pl.ds(c * points + start, CHUNK)
             value = near1[rows, :] * slope
             value = value - (counts[rows, :] * beta_scale + away_all1[rows, :] * gamma_scale)
             pushed[c, :, pl.ds(start, CHUNK)] = jnp.transpose(by(value, relative1))
-            return total_near + t_by(x1[rows, :], value)
-
-        grad_near1 = lax.fori_loop(0, points // CHUNK, push, grad_near1)
+
+        over(points, CHUNK, push)
     swap = to_partner(pushed.at[1 - core], arrived, pair_sems, 4)
     swap.start()
 
-    def own(i, total_own):
-        start = pl.multiple_of(i * CHUNK, CHUNK)
+    def own(start):
         rows = pl.ds(start, CHUNK)
         weights = jnp.broadcast_to(mask[:, rows].astype(F32), (SUBLANES, CHUNK))
         weights = jnp.transpose(weights)[:, :1]
         value = given1[rows, :] * slope
         value = value - (depth * weights * beta_scale + away_own1[rows, :] * gamma_scale)
         from_own[:, rows] = jnp.transpose(by(value, direct1)) + pushed[core, :, rows]
-        return total_own + t_by(x1[pl.ds(half + start, CHUNK), :], value)
-
-    grad_own1 = lax.fori_loop(0, points // CHUNK, own, jnp.zeros((cin, width1), F32))
-    flat1[0:cin, :] = grad_own1
-    flat1[cin : 2 * cin, :] = grad_near1 - grad_own1
-    sum1.swap.start()
-    sum2.spread()
-    sum1.scatter()
+
+    over(points, CHUNK, own)
+    sum1.finish()
+    sum2.finish()
     swap.wait()
     from_near[...] = arrived[...]
-    sum2.finish()
-    sum1.spread()
+    sum1.back.wait()
+    whole1[...] = all1[...]
     sum2.back.wait()
     whole2[...] = all2[...]
-    sum1.finish()
-    sum1.back.wait()
-    whole1[...] = all1[...]
 
 
 def finish_kernel(
@@ -1226,15 +1354,23 @@
 ):
     pooled[...] = pooled_in[...]
     grad_features[...] = from_own[...] + from_near[...]
-    grad_weight1[...] = jnp.transpose(whole1[0:LANES, :])
+    cores, chips = whole1.shape[:2]
+    cin = from_own.shape[0]
+    size1 = -(-2 * cin // (cores * chips))
+    rows1 = [whole1[n // chips, n % chips, 0:size1, :] for n in range(2 * cin // size1)]
+    grad_weight1[...] = jnp.transpose(jnp.concatenate(rows1, axis=0))
+    size2 = whole2.shape[2]
     grad_bias1[...] = norm1[0:1, :]
     grad_gain1[...] = norm1[1:2, :]
     for h in range(2):
         rows = slice(h * LANES, (h + 1) * LANES)
         for part in range(2):
-            block = (2 * part + h) * LANES
+            first = (2 * part + h) * LANES // size2
+            block = [
+                whole2[n // chips, n % chips] for n in range(first, first + LANES // size2)
+            ]
             grad_weight2[rows, part * LANES : (part + 1) * LANES] = jnp.transpose(
-                whole2[block : block + LANES, :]
+                jnp.concatenate(block, axis=0)
             )
     grad_bias2[...] = scales2[1:2, :]
     grad_gain2[...] = scales2[2:3, :]
@@ -1293,16 +1429,19 @@
                 shaped(both, width1),
                 shaped(both, LANES),
                 shaped(both, width1),
-                shaped(SUBLANES, width1),
                 shaped(2 * points, LANES),
                 shaped(both, width2),
+                shaped(SUBLANES, width1),
                 shaped(points, width1),
                 shaped(width1, width2),
                 shaped(SUBLANES, width2),
+                shaped(2, 2 * cin, width1),
             ],
             in_specs=[VMEM] * 3 + [ANY] * 2 + [SMEM] + [VMEM] * 3 + [ANY] + [VMEM] * 3,
-            out_specs=[VMEM] + [ANY] * 10 + [VMEM] * 6,
+            out_specs=[VMEM] + [ANY] * 12 + [VMEM] * 5,
             scratch_shapes=[
+                scratch(2 * points, LANES),
+                scratch(both, width2),
                 pltpu.SMEM((depth * points,), jnp.int32),
                 pltpu.SMEM((depth * points,), jnp.int32),
                 scratch(width2, 2 * width1),
@@ -1315,6 +1454,7 @@
                 scratch(both, LANES),
                 scratch(cores, cin, points),
                 scratch(both, LANES, dtype=BF16),
+                scratch(depth, LANES, LANES, dtype=BF16),
                 scratch(both, points, dtype=BF16),
                 scratch(SUBLANES, points),
                 scratch(points, LANES),
@@ -1325,6 +1465,7 @@
                 scratch(points, cin),
                 scratch(points, width1),
                 scratch(both + 2 * SUBLANES, LANES),
+                scratch(points, LANES),
                 scratch(points, LANES),
                 scratch(points, LANES),
                 scratch(points, LANES),
@@ -1345,12 +1486,12 @@
                 scratch(3, total, 4, LANES),
                 scratch(depth, SUBLANES, LANES),
                 scratch(depth, SUBLANES, LANES),
-                scratch(2, block, depth, SUBLANES, LANES),
-                pltpu.SemaphoreType.DMA((2, 3)),
+                scratch(2, 2 * block, depth, SUBLANES, LANES),
+                pltpu.SemaphoreType.DMA((2, 7)),
                 pltpu.SemaphoreType.DMA((2, 3)),
                 pltpu.SemaphoreType.DMA((2,)),
                 pltpu.SemaphoreType.DMA((3,)),
-                pltpu.SemaphoreType.DMA((8,)),
+                pltpu.SemaphoreType.DMA((10,)),
             ],
             compiler_params=pltpu.CompilerParams(
                 collective_id=1, has_side_effects=True, vmem_limit_bytes=MEMORY
@@ -1383,12 +1524,13 @@
             away_all1,
             counts,
             x2,
-            scales1,
             push2,
             extra2,
+            scales1,
             own2,
             grad_own2,
             scales2,
+            known1,
         ) = outs
 
         ring = scratch(3, block, depth, SUBLANES, LANES)
@@ -1407,7 +1549,7 @@
                 pltpu.SemaphoreType.DMA((5,)),
                 pltpu.SemaphoreType.DMA((3,)),
             ]
-            + [scratch(2 * both + 2 * SUBLANES, LANES)] * 8,
+            + [scratch(2 * both + 2 * SUBLANES, LANES)] * 12,
             compiler_params=pltpu.CompilerParams(vmem_limit_bytes=MEMORY),
             name="scatter2",
         )(index2, q2, push2, x2, second_layer_weight, scales2, extra2)
@@ -1425,44 +1567,53 @@
                 pltpu.SemaphoreType.DMA((1,)),
                 pltpu.SemaphoreType.DMA((3,)),
             ]
-            + [scratch(both + 2 * SUBLANES, LANES)] * SUBLANES,
+            + [scratch(both + 2 * SUBLANES, LANES)] * (SUBLANES * 2),
             compiler_params=pltpu.CompilerParams(vmem_limit_bytes=MEMORY),
             name="scatter1",
         )(index1, q1, own2, kept, other, inverse1, share1, moment1)
 
-        def piece_of(rows):
-            return -(-rows // (total * SUBLANES)) * SUBLANES
-
-        piece1, piece2 = piece_of(LANES), piece_of(4 * LANES)
-        side1, side2 = chips * piece1, chips * piece2
+        size1 = -(-2 * cin // total)
+        size2 = -(-4 * LANES // (total * SUBLANES)) * SUBLANES
+        stacked1 = -(-3 * size1 // SUBLANES) * SUBLANES
+        padded1 = -(-size1 // SUBLANES) * SUBLANES
         from_own, from_near, norm1, whole1, whole2 = pl.pallas_call(
             functools.partial(last_kernel, (cores, chips), depth),
             out_shape=[
                 shaped(cin, points),
                 shaped(cin, points),
                 shaped(SUBLANES, width1),
-                shaped(cores, chips, piece1, LANES),
-                shaped(cores, chips, piece2, LANES),
+                shaped(cores, chips, padded1, LANES),
+                shaped(cores, chips, size2, LANES),
             ],
-            in_specs=[VMEM] * 12,
+            in_specs=[ANY] * 2 + [VMEM] + [ANY] * 4 + [VMEM] * 3 + [ANY] * 3,
             out_specs=[VMEM] * 5,
             scratch_shapes=[
+                scratch(both, width1),
+                scratch(points, width1),
+                scratch(both, cin),
+                scratch(points, width1),
+                scratch(both, width1),
+                scratch(both, LANES),
+                scratch(width1, width2),
+                scratch(width1, width2),
+                scratch(2, 2 * cin, width1),
                 scratch(total, SUBLANES, LANES),
-                scratch(cores * side1, LANES),
-                scratch(cores * side2, LANES),
+                scratch(cores, chips, stacked1, LANES),
+                scratch(cores, chips, size2, LANES),
                 scratch(cores, cin, points),
                 scratch(cin, points),
-                scratch(side1, LANES),
-                scratch(side2, LANES),
-                scratch(chips, piece1, LANES),
-                scratch(chips, piece2, LANES),
-                scratch(piece1, LANES),
-                scratch(piece2, LANES),
-                scratch(cores, chips, piece1, LANES),
-                scratch(cores, chips, piece2, LANES),
+                scratch(chips, stacked1, LANES),
+                scratch(chips, size2, LANES),
+                scratch(chips, stacked1, LANES),
+                scratch(chips, size2, LANES),
+                scratch(padded1, LANES),
+                scratch(size2, LANES),
+                scratch(cores, chips, padded1, LANES),
+                scratch(cores, chips, size2, LANES),
                 pltpu.SemaphoreType.DMA((2,)),
                 pltpu.SemaphoreType.DMA((2, 5)),
                 pltpu.SemaphoreType.DMA((2, 4)),
+                pltpu.SemaphoreType.DMA((9,)),
             ],
             compiler_params=pltpu.CompilerParams(
                 collective_id=2, has_side_effects=True, vmem_limit_bytes=MEMORY
@@ -1481,6 +1632,7 @@
             first_layer_weight,
             grad_own2,
             grad_near2,
+            known1,
         )
         outs = pl.pallas_call(
             finish_kernel,
@@ -1502,8 +1654,8 @@
             from_own,
             from_near,
             norm1,
-            whole1.reshape(cores * side1, LANES),
-            whole2.reshape(cores * side2, LANES),
+            whole1,
+            whole2,
             scales2,
             pooled,
         )

time: 185 us -> 167 us (0.903)
  Pallas kernels: 178 us -> 161 us
    pallas_call x1, Pallas kernels: 103 us -> 95.2 us  [on_device(): pl.pallas_call(functools.partial(forward_kernel, (cores, total)), out_sha...]
    pallas_call x1, Pallas kernels: 29.8 us -> 24.8 us  [on_device(): pl.pallas_call(functools.partial(last_kernel, (cores, chips), depth), out...]
    pallas_call x1, Pallas kernels: 20.6 us -> 18 us  [on_device(): pl.pallas_call(functools.partial(scatter1_kernel, depth), out_shape=[shap...]
where the time goes in v3:
time: 167 us
  Pallas kernels  161 us (96%)
  local copies, waits for them, and re-layouts  2.11 us (1%)
  waiting for transfers between devices  2.01 us (1%)
    pallas_call x1, Pallas kernels, on_device(): pl.pallas_call(functools.partial(forward_kernel, (cores, total)), out_sha...  95.2 us
    pallas_call x1, Pallas kernels, on_device(): pl.pallas_call(functools.partial(last_kernel, (cores, chips), depth), out...  24.8 us
    pallas_call x1, Pallas kernels, on_device(): pl.pallas_call(functools.partial(scatter2_kernel, depth), out_shape=[shap...  21.1 us
    pallas_call x1, Pallas kernels, on_device(): pl.pallas_call(functools.partial(scatter1_kernel, depth), out_shape=[shap...  18 us
  transfers between devices with their start and end apart: 1, of which 1 were waited for; matrix products, arithmetic and copies ran while one was open for 0% of the time, Pallas kernels for 0%

profile of v3, /device:TPU:0, one launch (start us, length us, event | category | flops | bytes accessed | tf_op | source)
XLA Modules:
  0.0 167.2 jit_solution(6108364970526018714)
XLA Ops:
  0.6 0.9 multiply_add_fusion
  1.6 0.6 reshape.63.index2_in.index_in
  2.2 0.7 reshape.62.index1_in.index_in
  2.9 95.2 %forward.1 = (f32[4,512]{1,0:T(4,128)}, f32[128,20,8,128]{3,2,1,0:T(8,128)}, f32[256,20,8,128]{3,2,1,0:T(8,128)}, f32[1024,128]{1,0:T(8,128)}, f32[1024,128]{1,0...) custom-call(f32[64,1024]{1,0:T(8,128)} %feat.1, ...), custom_call_target="tpu_custom_call" | custom-call | tf_op jit(solution)/shard_map/forward/pallas_call | solution.py:1418
  98.1 21.1 %scatter2.1 = (f32[1024,128]{1,0:T(8,128)}, f32[1024,128]{1,0:T(8,128)}, f32[128,256]{1,0:T(8,128)}) custom-call(s32[20480]{0:T(1024)} %reshape.63.index2_in.index_in, f32[256,20,8,128]{3,2,1,0:T(8,128)} %get-tuple-element.47.q_hbm, f32[2048,128]{1,0:T(8,128)} %get-tuple-element.48.push_in, f32[2048,128]{1,0:T(8,128)} %get-tuple-element.49.x2_in, ...), custom_call_target="tpu_custom_call" | custom-call | tf_op jit(solution)/shard_map/scatter2/pallas_call | solution.py:1537
  119.2 0.2 collective-permute-start
  119.4 2.0 %collective-permute-done.other = f32[1024,128]{1,0:T(8,128)S(1)} collective-permute-done((f32[1024,128]{1,0:T(8,128)}, f32[1024,128]{1,0:T(8,128)S(1)}, u32[]{:S(2)}, u32[]{:S(2)}) %collective-permute-start) | collective-permute-done | bytes 524320 | tf_op jit(solution)/shard_map/ppermute | solution.py:1556
  121.4 0.0 copy-start
  121.4 0.8 copy-done
  122.2 18.0 %scatter1.1 = (f32[2048,128]{1,0:T(8,128)}, f32[1024,128]{1,0:T(8,128)}, f32[8,128]{1,0:T(8,128)}) custom-call(s32[20480]{0:T(1024)} %reshape.62.index1_in.index_in, f32[128,20,8,128]{3,2,1,0:T(8,128)} %get-tuple-element.45.q_hbm, f32[1024,128]{1,0:T(8,128)} %get-tuple-element.46.own, f32[1024,128]{1,0:T(8,128)} %get-tuple-element.52.kept, ...), custom_call_target="tpu_custom_call" | custom-call | tf_op jit(solution)/shard_map/scatter1/pallas_call | solution.py:1558
  140.2 24.8 %last.1 = (f32[64,1024]{1,0:T(8,128)}, f32[64,1024]{1,0:T(8,128)}, f32[8,128]{1,0:T(8,128)}, f32[2,16,8,128]{3,2,1,0:T(8,128)}, f32[2,16,16,128]{3,2,1,0:T(8,128)}) custom-call(f32[2048,128]{1,0:T(8,128)} %get-tuple-element.57.near1_in, f32[1024,128]{1,0:T(8,128)} %get-tuple-element.58.given1_in, f32[8,128]{1,0:T(8,128)} %get-tuple-element.59.parts, ...), custom_call_target="tpu_custom_call" | custom-call | tf_op jit(solution)/shard_map/last/pallas_call | solution.py:1579
  165.0 2.2 %finish.1 = (f32[4,512]{1,0:T(4,128)}, f32[64,1024]{1,0:T(8,128)}, f32[128,128]{1,0:T(8,128)}, f32[1,128]{1,0:T(1,128)}, f32[1,128]{1,0:T(1,128)}, /*index=5*/f3...) custom-call(f32[64,1024]{1,0:T(8,128)} %get-tuple-element.68.from_own, f32[64,1024]{1,0:T(8,128)} %get-tuple-element.69.from_near, ...), custom_call_target="tpu_custom_call" | custom-call | tf_op jit(solution)/shard_map/finish/pallas_call | solution.py:1637
  (1 shorter events, 0.0 us)
Async XLA Ops:
  119.2 2.2 %collective-permute-start = (f32[1024,128]{1,0:T(8,128)}, f32[1024,128]{1,0:T(8,128)S(1)}, u32[]{:S(2)}, u32[]{:S(2)}) collective-permute-start(f32[1024,128]{1,0:T(8,128)} %get-tuple-element.53), channel_id=1, source_target_pairs={{0,1},{1,0},{2,3},{3,2},{4,5},{5,4},{6,7},{7,6},{8,9},{9,8},{10,11... | collective-permute-start | bytes 1572872 | tf_op jit(solution)/shard_map/ppermute | solution.py:1556
  121.4 0.8 copy-start

commit v4 on v3

--- a/solution.py
+++ b/solution.py
@@ -78,12 +78,60 @@
     return product(left, right, ((0,), (0,)))
 
 
-def over(count, step, body):
+def thirds(value):
+    high, rest = value.astype(BF16), value - value.astype(BF16).astype(F32)
+    middle = rest.astype(BF16)
+    return high, middle, (rest - middle.astype(F32)).astype(BF16)
+
+
+def stacks(value, dim):
+    high, middle, low = thirds(value)
+    return [jnp.concatenate(parts, axis=dim) for parts in ((high, middle), (high, low))]
+
+
+def weight_stacks(value, dim):
+    high, middle, low = thirds(value)
+    return [
+        jnp.concatenate(parts, axis=dim)
+        for parts in ((high, high), (middle, middle), (low, high))
+    ]
+
+
+def exact(left, right, dims):
+    def part(a, b):
+        return lax.dot_general(a, b, (dims, ((), ())), preferred_element_type=F32)
+
+    return part(left[0], right[0]) + (part(left[0], right[1]) + part(left[1], right[2]))
+
+
+def quad_stacks(value):
+    high, middle, low = thirds(value)
+    return [
+        jnp.concatenate(parts, axis=0) for parts in ((high, high, middle, middle), (high, low))
+    ]
+
+
+def quad_weights(value):
+    high, middle, low = thirds(value)
+    return [
+        jnp.concatenate(parts, axis=0) for parts in ((high, middle, high, middle), (low, high))
+    ]
+
+
+def exact_quad(left, right):
+    def part(a, b):
+        return lax.dot_general(a, b, (((0,), (0,)), ((), ())), preferred_element_type=F32)
+
+    return part(left[0], right[0]) + part(left[1], right[1])
+
+
+def over(count, step, body, times=1):
     def run(i, carry):
-        body(pl.multiple_of(i * step, step))
+        for t in range(times):
+            body(pl.multiple_of((i * times + t) * step, step))
         return carry
 
-    lax.fori_loop(0, count // step, run, 0)
+    lax.fori_loop(0, count // (step * times), run, 0)
 
 
 def tree(values, join):
@@ -168,34 +216,26 @@
 
 
 def edge_pass(
-    subs, block, depth, part, index, table, own_rows, out_hbm, held, ring, sems, outs, pending, after_block
+    subs, block, depth, index, table, own_rows, out_hbm, held, ring, sems, outs, pending, after_block
 ):
     level_ref, share_ref, moment_ref, inverse_ref = outs
     per = SUBLANES // subs
     groups = own_rows.shape[0] // SUBLANES
-    stages = depth // part
     row = iota((SUBLANES, LANES), 0)
     mine = [(row >= subs * i) & (row < subs * (i + 1)) for i in range(per)]
-    zero = jnp.zeros((SUBLANES, LANES), F32)
-
-    def fetch(group, stage, slot):
-        for k in range(part):
-            target = held[slot].at[stage * part + k]
+    def fetch(group, slot):
+        for k in range(depth):
+            target = held[slot].at[k]
             for i in range(per):
                 first = (k * per + i) * groups
-                if stages > 1:
-                    span = groups * (1 + (stages - 1) * part * per)
-                    j = index.at[pl.ds(first, span)][stage * (part * per * groups) + group]
-                else:
-                    j = index.at[pl.ds(first, groups)][group]
+                j = index.at[pl.ds(first, groups)][group]
                 value = table[pl.ds(j, SUBLANES), :]
                 if i == 0:
                     target[...] = value
                 else:
                     pltpu.store(target, value, mask=mine[i])
 
-    def work(group, stage, slot, ring_slot, place, carry):
-        total0, share0, moment0 = carry
+    def work(group, slot, ring_slot, place):
         rows = pl.ds(pl.multiple_of(group * SUBLANES, SUBLANES), SUBLANES)
         peak = tree([held[slot][k] for k in range(depth)], jnp.maximum)
         top = own_rows[rows, :] + peak
@@ -205,24 +245,19 @@
         offset = under - peak
         fifth = 0.2 * rest
         total, share, moment = [], [], []
-        for k in range(part):
-            value = held[slot][stage * part + k]
+        for k in range(depth):
+            value = held[slot][k]
             power = value + offset
             grown = jnp.exp2(power)
             root = jnp.exp2((power - lax.log2(rest + grown)) * 0.2)
             weight = root * (fifth + grown)
-            ring[ring_slot, place, stage * part + k] = weight
+            ring[ring_slot, place, k] = weight
             total.append(root)
             share.append(weight)
             moment.append(weight * value)
         total, share, moment = [
             functools.reduce(jnp.add, parts) for parts in (total, share, moment)
         ]
-        if stages > 1:
-            start = stage == 0
-            total = total + jnp.where(start, 0.0, total0)
-            share = share + jnp.where(start, 0.0, share0)
-            moment = moment + jnp.where(start, 0.0, moment0)
         mass = share + (0.8 * rest) * total
         inverse = 1.0 / mass
         level = 0.2 * (top - under) + 0.8 * shift + lax.log2(mass)
@@ -230,7 +265,6 @@
         inverse_ref[rows, :] = inverse
         share_ref[rows, :] = share * inverse
         moment_ref[rows, :] = moment * inverse
-        return total, share, moment
 
     blocks = groups // block
 
@@ -239,8 +273,7 @@
             ring.at[slot, pl.ds(0, block)], out_hbm.at[pl.ds(b * block, block)], sems.at[slot]
         )
 
-    for stage in range(stages):
-        fetch(0, stage, 0)
+    fetch(0, 0)
 
     def one_block(b, carry):
         ring_slot = lax.rem(b, 2)
@@ -261,25 +294,16 @@
             def _():
                 push(b - 2, ring_slot).wait()
 
-        def pair(t, inner):
-            for slot in range(2):
-                place = t * 2 + slot
+        def several(t, inner):
+            for unit in range(4):
+                slot = unit % 2
+                place = t * 4 + unit
                 group = b * block + place
-                after = jnp.minimum(group + 1, groups - 1)
-                if stages == 1:
-                    work(group, 0, slot, ring_slot, place, (zero,) * 3)
-                    fetch(after, 0, 1 - slot)
-                else:
-
-                    def one_stage(stage, sums):
-                        sums = work(group, stage, slot, ring_slot, place, sums)
-                        fetch(after, stage, 1 - slot)
-                        return sums
-
-                    lax.fori_loop(0, stages, one_stage, (zero,) * 3)
+                work(group, slot, ring_slot, place)
+                fetch(jnp.minimum(group + 1, groups - 1), 1 - slot)
             return inner
 
-        lax.fori_loop(0, block // 2, pair, 0)
+        lax.fori_loop(0, block // 4, several, 0)
         push(b, ring_slot).start()
         if after_block is not None:
             after_block(b)
@@ -352,7 +376,6 @@
     parts2,
     u1,
     v1,
-    n1,
     g1,
     table1,
     own_rows1,
@@ -473,7 +496,7 @@
                 x1_cm[c, :, pl.ds(start, CHUNK)]
             )
 
-        over(points, CHUNK, turn)
+        over(points, CHUNK, turn, 2)
         value = x1_cm[c]
         high, low = split(value)
         lower = (value - high.astype(F32) - low.astype(F32)).astype(BF16)
@@ -481,15 +504,18 @@
         parts1[c, cin : 2 * cin, :] = low
         parts1[c, 2 * cin : 3 * cin, :] = lower
 
+    direct_parts1 = quad_weights(jnp.transpose(direct1))
+    relative_parts1 = quad_weights(jnp.transpose(relative1))
+
     def sums_near1(start):
         columns = pl.ds(start, CHUNK)
         value = mm_low(parts1[0], links[0:points, columns])
         for c in range(1, cores):
             value = value + mm_low(parts1[c], links[c * points : (c + 1) * points, columns])
         value = value[0:cin] + value[cin : 2 * cin] + value[2 * cin : 3 * cin]
-        n1[columns, :] = jnp.transpose(value)
-
-    over(points, CHUNK, sums_near1)
+        g1[columns, :] = exact_quad(quad_stacks(value), relative_parts1)
+
+    over(points, CHUNK, sums_near1, 2)
 
     stores[0].start()
     ones = jnp.ones((LANES, LANES), BF16)
@@ -498,7 +524,7 @@
         rows = pl.ds(start, CHUNK)
         counts[rows, :] = mm_low(tallies[rows, :], ones)
 
-    over(both, CHUNK, count_links)
+    over(both, CHUNK, count_links, 4)
     stores[1].start()
 
     live_sum = jnp.sum(live[0:1, :], axis=1, keepdims=True)
@@ -509,19 +535,20 @@
         weights = live[:, start : start + size].astype(BF16)
         return (mm_low(weights, high) + mm_low(weights, low))[0:1]
 
-    def statistics(x_all, n_ref, direct, relative, u, v, g, width):
-        def outer(start):
-            rows = pl.ds(start, CHUNK)
-            v[rows, :] = mm_nt(x_all[rows, :], relative)
-
-        over(both, CHUNK, outer)
+    def statistics(u, v, g, width):
+        for c in range(cores):
+
+            def outer(start):
+                left = quad_stacks(x1_cm[c, :, pl.ds(start, CHUNK)])
+                v[pl.ds(c * points + start, CHUNK), :] = exact_quad(left, relative_parts1)
+
+            over(points, CHUNK, outer, 2)
 
         def inner(start):
             rows = pl.ds(start, CHUNK)
-            u[rows, :] = mm_nt(x_all[pl.ds(half + start, CHUNK), :], direct)
-            g[rows, :] = mm_nt(n_ref[rows, :], relative)
-
-        over(points, CHUNK, inner)
+            u[rows, :] = exact_quad(quad_stacks(x1_cm[core, :, rows]), direct_parts1)
+
+        over(points, CHUNK, inner, 2)
         u_sum = live_total(0, points, u[...])
         g_sum = jnp.sum(g[...], axis=0, keepdims=True)
         u_mean = u_sum / live_sum
@@ -564,7 +591,7 @@
             square = term if square is None else square + term
         return count, mean, square / count
 
-    sums, square, u_mean1, v_mean1 = statistics(x1, n1, direct1, relative1, u1, v1, g1, width1)
+    sums, square, u_mean1, v_mean1 = statistics(u1, v1, g1, width1)
     send_sums(0, [sums, square, jnp.broadcast_to(mine, (1, LANES)), jnp.zeros((1, LANES), F32)])
 
     for part, value in enumerate(split(u1[...] - u_mean1)):
@@ -575,7 +602,7 @@
         value = mm_low(links[rows, :], u_parts[:, 0 : 2 * LANES])
         away_all1[rows, :] = value[:, :LANES] + value[:, LANES:]
 
-    over(both, CHUNK, shared1)
+    over(both, CHUNK, shared1, 2)
     receive(0)
     numbers = [slots[0, i, 2:3, 0:1] for i in range(total)]
     count, mean1, variance1 = combine(0, numbers, width1)
@@ -590,7 +617,7 @@
         table1[pl.ds(SUBLANES + start, CHUNK), :] = (v1[rows, :] - v_mean1) * (slope1 * LOG2E)
         away_all1[rows, :] += counts[rows, :] * (v1[rows, :] - (mean1 - u_mean1))
 
-    over(both, CHUNK, fill1)
+    over(both, CHUNK, fill1, 2)
 
     def fill_own1(start):
         rows = pl.ds(start, CHUNK)
@@ -600,7 +627,7 @@
             own_rows1[here, :] = value[s : s + groups1]
         away_own1[rows, :] = depth * live_col[rows, :] * (u1[rows, :] - mean1) + g1[rows, :]
 
-    over(points, CHUNK, fill_own1)
+    over(points, CHUNK, fill_own1, 2)
 
     stores[2].start()
     stores[3].start()
@@ -617,7 +644,6 @@
         1,
         block1,
         depth,
-        depth // 2,
         index1,
         table1,
         own_rows1,
@@ -653,32 +679,36 @@
     direct2 = weight2[:, :width1] - weight2[:, width1:]
     relative2 = weight2[:, width1:]
 
+    direct_parts2 = weight_stacks(direct2, 1)
+    relative_parts2 = weight_stacks(relative2, 1)
+
     def turn2(start):
         high, low = split(jnp.transpose(x2[pl.ds(start, CHUNK), :]))
         parts2[0:width1, pl.ds(start, CHUNK)] = high
         parts2[width1 : 2 * width1, pl.ds(start, CHUNK)] = low
 
-    over(both, CHUNK, turn2)
+    over(both, CHUNK, turn2, 4)
 
     def sums_near2(start):
         columns = pl.ds(start, CHUNK)
         value = mm_low(parts2[...], links[:, columns])
         value = value[0:width1] + value[width1 : 2 * width1]
-        g2[columns, :] = mm_nt(jnp.transpose(value), relative2)
-
-    over(points, CHUNK, sums_near2)
+        g2[columns, :] = exact(stacks(jnp.transpose(value), 1), relative_parts2, ((1,), (1,)))
+
+    over(points, CHUNK, sums_near2, 2)
 
     def statistics2():
         def outer(start):
             rows = pl.ds(start, CHUNK)
-            v2[rows, :] = mm_nt(x2[rows, :], relative2)
-
-        over(both, CHUNK, outer)
+            v2[rows, :] = exact(stacks(x2[rows, :], 1), relative_parts2, ((1,), (1,)))
+
+        over(both, CHUNK, outer, 2)
 
         def inner(start):
-            u2[pl.ds(start, CHUNK), :] = mm_nt(x2[pl.ds(half + start, CHUNK), :], direct2)
-
-        over(points, CHUNK, inner)
+            left = stacks(x2[pl.ds(half + start, CHUNK), :], 1)
+            u2[pl.ds(start, CHUNK), :] = exact(left, direct_parts2, ((1,), (1,)))
+
+        over(points, CHUNK, inner, 2)
         u_sum = jnp.zeros((1, width2), F32)
         g_sum = jnp.zeros((1, width2), F32)
         for s in range(0, points, CHUNK):
@@ -714,7 +744,7 @@
             links[rows, :], u_parts[:, width2:]
         )
 
-    over(both, CHUNK, shared2)
+    over(both, CHUNK, shared2, 2)
     receive(1)
     count, mean2, variance2 = combine(1, numbers, width2)
     r2 = lax.rsqrt(variance2 + EPSILON)
@@ -729,7 +759,7 @@
                 :, h * LANES : (h + 1) * LANES
             ]
 
-    over(both, CHUNK, fill2)
+    over(both, CHUNK, fill2, 2)
 
     for i in range(SUBLANES // 2):
         rows = slice(i * groups2, (i + 1) * groups2)
@@ -742,7 +772,6 @@
     pending = edge_pass(
         2,
         block2,
-        depth,
         depth,
         index2,
         table2,
@@ -877,7 +906,7 @@
         known1[0, cin:, :] += t_by(x1[near_rows, :], away_all1[near_rows, :])
         known1[1, cin:, :] += t_by(x1[near_rows, :], counts[near_rows, :])
 
-    over(both, CHUNK, known)
+    over(both, CHUNK, known, 2)
 
     def known_own(start):
         rows = pl.ds(start, CHUNK)
@@ -885,7 +914,7 @@
         known1[0, 0:cin, :] += t_by(here, away_own1[rows, :])
         known1[1, 0:cin, :] += t_by(here, depth * live_col[rows, :])
 
-    over(points, CHUNK, known_own)
+    over(points, CHUNK, known_own, 2)
     for i in range(2):
         known1[i, cin:, :] -= known1[i, 0:cin, :]
     receive(2)
@@ -904,7 +933,7 @@
         away = extra2[rows, :] + weights * (v2[rows, :] - (mean2 - u_mean2))
         extra2[rows, :] = weights * beta_scale + away * gamma_scale
 
-    over(both, CHUNK, extra)
+    over(both, CHUNK, extra, 2)
     late[1].start()
     grad_own2[...] = jnp.zeros(grad_own2.shape, F32)
 
@@ -922,7 +951,7 @@
         copy.wait()
 
 
-def scatter_loop(subs, depth, part, index, q_hbm, ring, sems, push, sums, clear):
+def scatter_loop(subs, depth, index, q_hbm, ring, sems, push, sums, clear):
     per = SUBLANES // subs
     groups = q_hbm.shape[0]
     slots, block = ring.shape[0], ring.shape[1]
@@ -930,7 +959,6 @@
     row = iota((SUBLANES, LANES), 0)
     mine = [(row >= subs * i) & (row < subs * (i + 1)) for i in range(per)]
     ways = len(sums) // per
-    stages = depth // part
 
     def pull(b):
         slot = lax.rem(b, slots)
@@ -955,23 +983,12 @@
             rows = pl.ds(pl.multiple_of(group * SUBLANES, SUBLANES), SUBLANES)
             given = push[rows, :]
 
-            def one_part(stage):
-                for k in range(part):
-                    value = ring[slot, place, stage * part + k] * given
-                    for i in range(per):
-                        first = (k * per + i) * groups
-                        if stages > 1:
-                            span = groups * (1 + (stages - 1) * part * per)
-                            j = index.at[pl.ds(first, span)][stage * (part * per * groups) + group]
-                        else:
-                            j = index.at[pl.ds(first, groups)][group]
-                        target = sums[i * ways + k % ways].at[pl.ds(j, SUBLANES), :]
-                        pltpu.store(target, target[...] + value, mask=mine[i])
-
-            if stages == 1:
-                one_part(0)
-            else:
-                lax.fori_loop(0, stages, lambda stage, c: (one_part(stage), c)[1], 0)
+            for k in range(depth):
+                value = ring[slot, place, k] * given
+                for i in range(per):
+                    j = index.at[pl.ds((k * per + i) * groups, groups)][group]
+                    target = sums[i * ways + k % ways].at[pl.ds(j, SUBLANES), :]
+                    pltpu.store(target, target[...] + value, mask=mine[i])
             return inner
 
         lax.fori_loop(0, block, one_group, 0)
@@ -1033,7 +1050,7 @@
 
     for copy in loads[:2]:
         copy.start()
-    scatter_loop(2, depth, depth, index, q_hbm, ring, ring_sems, push, sums, prepare)
+    scatter_loop(2, depth, index, q_hbm, ring, ring_sems, push, sums, prepare)
     for copy in loads[2:]:
         copy.wait()
     points, width = kept.shape
@@ -1053,7 +1070,7 @@
             out[pl.ds(start, CHUNK), :] = by(value, relative)
             grad_near[...] += t_by(x2[rows, :], value)
 
-        over(points, CHUNK, finish)
+        over(points, CHUNK, finish, 2)
 
 
 def scatter1_kernel(
@@ -1093,16 +1110,16 @@
             given[rows, :] = weighted
             grad_beta = grad_beta + jnp.sum(weighted, axis=0, keepdims=True)
             grad_gamma = grad_gamma + jnp.sum(grad * moment[rows, :], axis=0, keepdims=True)
-        parts[...] = jnp.concatenate([grad_beta, grad_gamma, jnp.zeros((6, LANES), F32)], axis=0)
+        parts[...] = jnp.concatenate([grad_beta, grad_gamma], axis=0)
         load.wait()
 
-    scatter_loop(1, depth, depth // 1, index, q_hbm, ring, ring_sems, push, sums, prepare)
+    scatter_loop(1, depth, index, q_hbm, ring, ring_sems, push, sums, prepare)
 
     def finish(start):
         here = pl.ds(SUBLANES + start, CHUNK)
         near[pl.ds(start, CHUNK), :] = tree([ref[here, :] for ref in sums], jnp.add)
 
-    over(near.shape[0], CHUNK, finish)
+    over(near.shape[0], CHUNK, finish, 2)
 
 
 def last_kernel(
@@ -1312,7 +1329,7 @@
             value = value - (counts[rows, :] * beta_scale + away_all1[rows, :] * gamma_scale)
             pushed[c, :, pl.ds(start, CHUNK)] = jnp.transpose(by(value, relative1))
 
-        over(points, CHUNK, push)
+        over(points, CHUNK, push, 2)
     swap = to_partner(pushed.at[1 - core], arrived, pair_sems, 4)
     swap.start()
 
@@ -1324,7 +1341,7 @@
         value = value - (depth * weights * beta_scale + away_own1[rows, :] * gamma_scale)
         from_own[:, rows] = jnp.transpose(by(value, direct1)) + pushed[core, :, rows]
 
-    over(points, CHUNK, own)
+    over(points, CHUNK, own, 2)
     sum1.finish()
     sum2.finish()
     swap.wait()
@@ -1462,7 +1479,6 @@
                 scratch(2 * width1, both, dtype=BF16),
                 scratch(points, width1),
                 scratch(both, width1),
-                scratch(points, cin),
                 scratch(points, width1),
                 scratch(both + 2 * SUBLANES, LANES),
                 scratch(points, LANES),
@@ -1557,7 +1573,7 @@
 
         near1, given1, parts = pl.pallas_call(
             functools.partial(scatter1_kernel, depth),
-            out_shape=[shaped(both, width1), shaped(points, width1), shaped(SUBLANES, width1)],
+            out_shape=[shaped(both, width1), shaped(points, width1), shaped(2, width1)],
             in_specs=[ANY] * 2 + [VMEM] * 6,
             out_specs=[VMEM] * 3,
             scratch_shapes=[
@@ -1581,7 +1597,7 @@
             out_shape=[
                 shaped(cin, points),
                 shaped(cin, points),
-                shaped(SUBLANES, width1),
+                shaped(2, width1),
                 shaped(cores, chips, padded1, LANES),
                 shaped(cores, chips, size2, LANES),
             ],
@@ -1597,7 +1613,7 @@
                 scratch(width1, width2),
                 scratch(width1, width2),
                 scratch(2, 2 * cin, width1),
-                scratch(total, SUBLANES, LANES),
+                scratch(total, 2, LANES),
                 scratch(cores, chips, stacked1, LANES),
                 scratch(cores, chips, size2, LANES),
                 scratch(cores, cin, points),

time: 167 us -> 156 us (0.934)
  Pallas kernels: 161 us -> 150 us
    pallas_call x1, Pallas kernels: 95.2 us -> 85.7 us  [on_device(): pl.pallas_call(functools.partial(forward_kernel, (cores, total)), out_sha...]
where the time goes in v4:
time: 156 us
  Pallas kernels  150 us (96%)
  local copies, waits for them, and re-layouts  2.11 us (1%)
  waiting for transfers between devices  2.01 us (1%)
    pallas_call x1, Pallas kernels, on_device(): pl.pallas_call(functools.partial(forward_kernel, (cores, total)), out_sha...  85.7 us
    pallas_call x1, Pallas kernels, on_device(): pl.pallas_call(functools.partial(last_kernel, (cores, chips), depth), out...  23.4 us
    pallas_call x1, Pallas kernels, on_device(): pl.pallas_call(functools.partial(scatter2_kernel, depth), out_shape=[shap...  20.6 us
    pallas_call x1, Pallas kernels, on_device(): pl.pallas_call(functools.partial(scatter1_kernel, depth), out_shape=[shap...  18.1 us
  transfers between devices with their start and end apart: 1, of which 1 were waited for; matrix products, arithmetic and copies ran while one was open for 0% of the time, Pallas kernels for 0%

profile of v4, /device:TPU:0, one launch (start us, length us, event | category | flops | bytes accessed | tf_op | source)
XLA Modules:
  0.0 155.8 jit_solution(12652027365947139713)
XLA Ops:
  0.6 0.9 multiply_add_fusion
  1.6 0.6 reshape.63.index2_in.index_in
  2.2 0.7 reshape.62.index1_in.index_in
  2.9 85.7 %forward.1 = (f32[4,512]{1,0:T(4,128)}, f32[128,20,8,128]{3,2,1,0:T(8,128)}, f32[256,20,8,128]{3,2,1,0:T(8,128)}, f32[1024,128]{1,0:T(8,128)}, f32[1024,128]{1,0...) custom-call(f32[64,1024]{1,0:T(8,128)} %feat.1, ...), custom_call_target="tpu_custom_call" | custom-call | tf_op jit(solution)/shard_map/forward/pallas_call | solution.py:1435
  88.6 20.6 %scatter2.1 = (f32[1024,128]{1,0:T(8,128)}, f32[1024,128]{1,0:T(8,128)}, f32[128,256]{1,0:T(8,128)}) custom-call(s32[20480]{0:T(1024)} %reshape.63.index2_in.index_in, f32[256,20,8,128]{3,2,1,0:T(8,128)} %get-tuple-element.47.q_hbm, f32[2048,128]{1,0:T(8,128)} %get-tuple-element.48.push_in, f32[2048,128]{1,0:T(8,128)} %get-tuple-element.49.x2_in, ...), custom_call_target="tpu_custom_call" | custom-call | tf_op jit(solution)/shard_map/scatter2/pallas_call | solution.py:1553
  109.1 0.2 collective-permute-start
  109.3 2.0 %collective-permute-done.other = f32[1024,128]{1,0:T(8,128)S(1)} collective-permute-done((f32[1024,128]{1,0:T(8,128)}, f32[1024,128]{1,0:T(8,128)S(1)}, u32[]{:S(2)}, u32[]{:S(2)}) %collective-permute-start) | collective-permute-done | bytes 524320 | tf_op jit(solution)/shard_map/ppermute | solution.py:1572
  111.3 0.0 copy-start
  111.3 0.8 copy-done
  112.1 18.1 %scatter1.1 = (f32[2048,128]{1,0:T(8,128)}, f32[1024,128]{1,0:T(8,128)}, f32[2,128]{1,0:T(2,128)}) custom-call(s32[20480]{0:T(1024)} %reshape.62.index1_in.index_in, f32[128,20,8,128]{3,2,1,0:T(8,128)} %get-tuple-element.45.q_hbm, f32[1024,128]{1,0:T(8,128)} %get-tuple-element.46.own, f32[1024,128]{1,0:T(8,128)} %get-tuple-element.52.kept, ...), custom_call_target="tpu_custom_call" | custom-call | tf_op jit(solution)/shard_map/scatter1/pallas_call | solution.py:1574
  130.3 23.4 %last.1 = (f32[64,1024]{1,0:T(8,128)}, f32[64,1024]{1,0:T(8,128)}, f32[2,128]{1,0:T(2,128)}, f32[2,16,8,128]{3,2,1,0:T(8,128)}, f32[2,16,16,128]{3,2,1,0:T(8,128)}) custom-call(f32[2048,128]{1,0:T(8,128)} %get-tuple-element.57.near1_in, f32[1024,128]{1,0:T(8,128)} %get-tuple-element.58.given1_in, f32[2,128]{1,0:T(2,128)} %get-tuple-element.59.parts, ...), custom_call_target="tpu_custom_call" | custom-call | tf_op jit(solution)/shard_map/last/pallas_call | solution.py:1595
  153.6 2.2 %finish.1 = (f32[4,512]{1,0:T(4,128)}, f32[64,1024]{1,0:T(8,128)}, f32[128,128]{1,0:T(8,128)}, f32[1,128]{1,0:T(1,128)}, f32[1,128]{1,0:T(1,128)}, /*index=5*/f3...) custom-call(f32[64,1024]{1,0:T(8,128)} %get-tuple-element.68.from_own, f32[64,1024]{1,0:T(8,128)} %get-tuple-element.69.from_near, ...), custom_call_target="tpu_custom_call" | custom-call | tf_op jit(solution)/shard_map/finish/pallas_call | solution.py:1653
  (1 shorter events, 0.0 us)
Async XLA Ops:
  109.1 2.2 %collective-permute-start = (f32[1024,128]{1,0:T(8,128)}, f32[1024,128]{1,0:T(8,128)S(1)}, u32[]{:S(2)}, u32[]{:S(2)}) collective-permute-start(f32[1024,128]{1,0:T(8,128)} %get-tuple-element.53), channel_id=1, source_target_pairs={{0,1},{1,0},{2,3},{3,2},{4,5},{5,4},{6,7},{7,6},{8,9},{9,8},{10,11... | collective-permute-start | bytes 1572872 | tf_op jit(solution)/shard_map/ppermute | solution.py:1572
  111.3 0.8 copy-start

commit v5 on v4

--- a/solution.py
+++ b/solution.py
@@ -530,36 +530,64 @@
     live_sum = jnp.sum(live[0:1, :], axis=1, keepdims=True)
     mine = live_sum * depth
 
-    def live_total(start, size, value):
-        high, low = split(value)
-        weights = live[:, start : start + size].astype(BF16)
-        return (mm_low(weights, high) + mm_low(weights, low))[0:1]
+    def fold(count, size, body, state):
+        def several(i, carry):
+            for t in range(2):
+                carry = body(pl.multiple_of((i * 2 + t) * size, size), carry)
+            return carry
+
+        return lax.fori_loop(0, count // (2 * size), several, state)
+
+    def column_sum(value):
+        rows = [value[s : s + SUBLANES] for s in range(0, value.shape[0], SUBLANES)]
+        return tree(rows, jnp.add)
 
     def statistics(u, v, g, width):
-        for c in range(cores):
-
-            def outer(start):
-                left = quad_stacks(x1_cm[c, :, pl.ds(start, CHUNK)])
-                v[pl.ds(c * points + start, CHUNK), :] = exact_quad(left, relative_parts1)
-
-            over(points, CHUNK, outer, 2)
-
-        def inner(start):
+        per = width // LANES
+        zeros = jnp.zeros((SUBLANES, width), F32)
+
+        def first(start, carry):
             rows = pl.ds(start, CHUNK)
-            u[rows, :] = exact_quad(quad_stacks(x1_cm[core, :, rows]), direct_parts1)
-
-        over(points, CHUNK, inner, 2)
-        u_sum = live_total(0, points, u[...])
-        g_sum = jnp.sum(g[...], axis=0, keepdims=True)
+            weights = rows_to_lanes([live_col[rows, :]] * per)
+            return carry[0] + column_sum(weights * u[rows, :]), carry[1] + column_sum(g[rows, :])
+
+        u_sum, g_sum = fold(points, CHUNK, first, (zeros, zeros))
+        u_sum = jnp.sum(u_sum, axis=0, keepdims=True)
+        g_sum = jnp.sum(g_sum, axis=0, keepdims=True)
         u_mean = u_sum / live_sum
         v_mean = g_sum / mine
-        centred = u[...] - u_mean
-        spread = depth * centred * centred + 2.0 * centred * (g[...] - depth * v_mean)
-        square = live_total(0, points, spread)
-        weights = rows_to_lanes([counts[...]] * (width // LANES))
-        away = v[...] - v_mean
-        square = square + jnp.sum(weights * away * away, axis=0, keepdims=True)
+
+        def second(start, carry):
+            rows = pl.ds(start, CHUNK)
+            weights = rows_to_lanes([live_col[rows, :]] * per)
+            centred = weights * (u[rows, :] - u_mean)
+            spread = depth * centred + 2.0 * (g[rows, :] - depth * v_mean)
+            return carry + column_sum(centred * spread)
+
+        def third(start, carry):
+            rows = pl.ds(start, CHUNK)
+            away = v[rows, :] - v_mean
+            weights = rows_to_lanes([counts[rows, :]] * per)
+            return carry + column_sum(weights * away * away)
+
+        square = fold(points, CHUNK, second, zeros)
+        square = fold(both, CHUNK, third, square)
+        square = jnp.sum(square, axis=0, keepdims=True)
         return depth * u_sum + g_sum, square, u_mean, v_mean
+
+    for c in range(cores):
+
+        def outer(start):
+            left = quad_stacks(x1_cm[c, :, pl.ds(start, CHUNK)])
+            v1[pl.ds(c * points + start, CHUNK), :] = exact_quad(left, relative_parts1)
+
+        over(points, CHUNK, outer, 2)
+
+    def inner(start):
+        rows = pl.ds(start, CHUNK)
+        u1[rows, :] = exact_quad(quad_stacks(x1_cm[core, :, rows]), direct_parts1)
+
+    over(points, CHUNK, inner, 2)
 
     def send_sums(use, rows):
         for i, value in enumerate(rows):
@@ -615,7 +643,6 @@
     def fill1(start):
         rows = pl.ds(start, CHUNK)
         table1[pl.ds(SUBLANES + start, CHUNK), :] = (v1[rows, :] - v_mean1) * (slope1 * LOG2E)
-        away_all1[rows, :] += counts[rows, :] * (v1[rows, :] - (mean1 - u_mean1))
 
     over(both, CHUNK, fill1, 2)
 
@@ -625,12 +652,9 @@
         for s in range(0, CHUNK, groups1):
             here = pl.ds(lax.div(start, groups1) + s // groups1, groups1, stride=SUBLANES)
             own_rows1[here, :] = value[s : s + groups1]
-        away_own1[rows, :] = depth * live_col[rows, :] * (u1[rows, :] - mean1) + g1[rows, :]
 
     over(points, CHUNK, fill_own1, 2)
 
-    stores[2].start()
-    stores[3].start()
     loads[0].wait()
     block1, block2 = groups1 // 4, ring.shape[1]
     block_rows = block1 * SUBLANES
@@ -656,38 +680,41 @@
         lambda b: hand_over(b).start(),
     )
 
-    inverse_gain1 = 1.0 / (gain1[...] * LOG2E)
     for i in range(SUBLANES):
         here = pl.ds(i, groups1, stride=SUBLANES)
         x2[pl.ds(half + i * groups1, groups1), :] = level1[here, :]
-        offset = own_rows1[here, :] - bias1[...] * LOG2E
-        rows = slice(i * groups1, (i + 1) * groups1)
-        moment1[rows, :] = (share_rows1[here, :] * offset + moment_rows1[here, :]) * inverse_gain1
-        share1[rows, :] = share_rows1[here, :]
-    for copy in stores[4:7]:
-        copy.start()
     loads[1].wait()
     loads[2].wait()
+    direct2 = weight2[:, :width1] - weight2[:, width1:]
+    relative2 = weight2[:, width1:]
+    direct_parts2 = weight_stacks(direct2, 1)
+    relative_parts2 = weight_stacks(relative2, 1)
+    other_half = pl.multiple_of((1 - core) * points, points)
+
+    def outer2(base):
+        def chunk(start):
+            rows = pl.ds(base + start, CHUNK)
+            value = x2[rows, :]
+            high, low = split(jnp.transpose(value))
+            parts2[0:width1, rows] = high
+            parts2[width1 : 2 * width1, rows] = low
+            v2[rows, :] = exact(stacks(value, 1), relative_parts2, ((1,), (1,)))
+
+        over(points, CHUNK, chunk, 2)
+
+    def inner2(start):
+        left = stacks(x2[pl.ds(half + start, CHUNK), :], 1)
+        u2[pl.ds(start, CHUNK), :] = exact(left, direct_parts2, ((1,), (1,)))
+
+    over(points, CHUNK, inner2, 2)
+    outer2(half)
     for b in range(blocks1):
         hand_over(b).wait()
-    other_half = pl.multiple_of((1 - core) * points, points)
     for i in range(SUBLANES):
         here = pl.ds(i, groups1, stride=SUBLANES)
         x2[pl.ds(other_half + i * groups1, groups1), :] = other1[here, :]
     stores[7].start()
-
-    direct2 = weight2[:, :width1] - weight2[:, width1:]
-    relative2 = weight2[:, width1:]
-
-    direct_parts2 = weight_stacks(direct2, 1)
-    relative_parts2 = weight_stacks(relative2, 1)
-
-    def turn2(start):
-        high, low = split(jnp.transpose(x2[pl.ds(start, CHUNK), :]))
-        parts2[0:width1, pl.ds(start, CHUNK)] = high
-        parts2[width1 : 2 * width1, pl.ds(start, CHUNK)] = low
-
-    over(both, CHUNK, turn2, 4)
+    outer2(other_half)
 
     def sums_near2(start):
         columns = pl.ds(start, CHUNK)
@@ -697,43 +724,7 @@
 
     over(points, CHUNK, sums_near2, 2)
 
-    def statistics2():
-        def outer(start):
-            rows = pl.ds(start, CHUNK)
-            v2[rows, :] = exact(stacks(x2[rows, :], 1), relative_parts2, ((1,), (1,)))
-
-        over(both, CHUNK, outer, 2)
-
-        def inner(start):
-            left = stacks(x2[pl.ds(half + start, CHUNK), :], 1)
-            u2[pl.ds(start, CHUNK), :] = exact(left, direct_parts2, ((1,), (1,)))
-
-        over(points, CHUNK, inner, 2)
-        u_sum = jnp.zeros((1, width2), F32)
-        g_sum = jnp.zeros((1, width2), F32)
-        for s in range(0, points, CHUNK):
-            u_sum = u_sum + live_total(s, CHUNK, u2[s : s + CHUNK, :])
-            g_sum = g_sum + jnp.sum(g2[s : s + CHUNK, :], axis=0, keepdims=True)
-        u_mean = u_sum / live_sum
-        v_mean = g_sum / mine
-        square = jnp.zeros((1, width2), F32)
-        for s in range(0, points, CHUNK):
-            centred = u2[s : s + CHUNK, :] - u_mean
-            spread = depth * centred * centred + 2.0 * centred * (
-                g2[s : s + CHUNK, :] - depth * v_mean
-            )
-            square = square + live_total(s, CHUNK, spread)
-
-        def squares(i, carry):
-            rows = pl.ds(pl.multiple_of(i * CHUNK, CHUNK), CHUNK)
-            away = v2[rows, :] - v_mean
-            weights = rows_to_lanes([counts[rows, :]] * (width2 // LANES))
-            return carry + jnp.sum(weights * away * away, axis=0, keepdims=True)
-
-        square = lax.fori_loop(0, both // CHUNK, squares, square)
-        return depth * u_sum + g_sum, square, u_mean, v_mean
-
-    sums, square, u_mean2, v_mean2 = statistics2()
+    sums, square, u_mean2, v_mean2 = statistics(u2, v2, g2, width2)
     send_sums(1, lanes_to_rows(sums, width2) + lanes_to_rows(square, width2))
     for part, value in enumerate(split(u2[...] - u_mean2)):
         u_parts[:, part * width2 : (part + 1) * width2] = value
@@ -745,6 +736,22 @@
         )
 
     over(both, CHUNK, shared2, 2)
+
+    def away1(start):
+        rows = pl.ds(start, CHUNK)
+        away_all1[rows, :] += counts[rows, :] * (v1[rows, :] - (mean1 - u_mean1))
+
+    over(both, CHUNK, away1, 2)
+    inverse_gain1 = 1.0 / (gain1[...] * LOG2E)
+    for i in range(SUBLANES):
+        here = pl.ds(i, groups1, stride=SUBLANES)
+        rows = slice(i * groups1, (i + 1) * groups1)
+        offset = own_rows1[here, :] - bias1[...] * LOG2E
+        moment1[rows, :] = (share_rows1[here, :] * offset + moment_rows1[here, :]) * inverse_gain1
+        share1[rows, :] = share_rows1[here, :]
+        away_own1[rows, :] = depth * live_col[rows, :] * (u1[rows, :] - mean1) + g1[rows, :]
+    for copy in stores[2:7]:
+        copy.start()
     receive(1)
     count, mean2, variance2 = combine(1, numbers, width2)
     r2 = lax.rsqrt(variance2 + EPSILON)
@@ -917,6 +924,22 @@
     over(points, CHUNK, known_own, 2)
     for i in range(2):
         known1[i, cin:, :] -= known1[i, 0:cin, :]
+
+    main = jnp.zeros(grad_own2.shape, F32)
+    away_sum = jnp.zeros(grad_own2.shape, F32)
+    live_x = jnp.zeros((width1, LANES), F32)
+    for i in range(SUBLANES // 2):
+        rows = slice(i * groups2, (i + 1) * groups2)
+        here = x2[pl.ds(half + i * groups2, groups2), :]
+        weights = rows_to_lanes([live_col[rows, :]] * 2)
+        u2[rows, :] = depth * weights * (u2[rows, :] - mean2) + g2[rows, :]
+        given = rows_to_lanes(
+            [share2[pl.ds(2 * i + h, groups2, stride=SUBLANES), :] for h in range(2)]
+        )
+        g2[rows, :] = given * slope2
+        main = main + t_by(here, g2[rows, :])
+        away_sum = away_sum + t_by(here, u2[rows, :])
+        live_x = live_x + t_by(here, depth * live_col[rows, :])
     receive(2)
     sums = slot_sum(slots.at[2], total)
     grad_beta = rows_to_lanes([sums[0:1], sums[1:2]])
@@ -935,18 +958,17 @@
 
     over(both, CHUNK, extra, 2)
     late[1].start()
-    grad_own2[...] = jnp.zeros(grad_own2.shape, F32)
-
-    for i in range(SUBLANES // 2):
-        rows = slice(i * groups2, (i + 1) * groups2)
+    grad_own2[...] = main - (
+        rows_to_lanes([live_x] * 2) * beta_scale + away_sum * gamma_scale
+    )
+
+    def own(start):
+        rows = pl.ds(start, CHUNK)
         weights = rows_to_lanes([live_col[rows, :]] * 2)
-        given = rows_to_lanes(
-            [share2[pl.ds(2 * i + h, groups2, stride=SUBLANES), :] for h in range(2)]
-        )
-        away = depth * weights * (u2[rows, :] - mean2) + g2[rows, :]
-        value = given * slope2 - (depth * weights * beta_scale + away * gamma_scale)
+        value = g2[rows, :] - (depth * weights * beta_scale + u2[rows, :] * gamma_scale)
         own2[rows, :] = by(value, direct2)
-        grad_own2[...] += t_by(x2[pl.ds(half + i * groups2, groups2), :], value)
+
+    over(points, CHUNK, own, 2)
     for copy in stores + late + [pending(0), pending(1)]:
         copy.wait()
 
@@ -1083,18 +1105,28 @@
     inverse,
     share,
     moment,
+    near_out,
+    given_out,
+    parts,
     near,
     given,
-    parts,
     index,
     push,
     ring,
     load_sems,
     ring_sems,
+    store_sems,
     *sums,
 ):
     load = pltpu.make_async_copy(index_in, index, load_sems.at[0])
     load.start()
+    quarter = near.shape[0] // 4
+    stores = [pltpu.make_async_copy(given, given_out, store_sems.at[0])]
+    for i in range(4):
+        rows = pl.ds(i * quarter, quarter)
+        stores.append(
+            pltpu.make_async_copy(near.at[rows], near_out.at[rows], store_sems.at[1 + i])
+        )
 
     def prepare():
         clear(sums)
@@ -1111,15 +1143,22 @@
             grad_beta = grad_beta + jnp.sum(weighted, axis=0, keepdims=True)
             grad_gamma = grad_gamma + jnp.sum(grad * moment[rows, :], axis=0, keepdims=True)
         parts[...] = jnp.concatenate([grad_beta, grad_gamma], axis=0)
+        stores[0].start()
         load.wait()
 
     scatter_loop(1, depth, index, q_hbm, ring, ring_sems, push, sums, prepare)
 
-    def finish(start):
-        here = pl.ds(SUBLANES + start, CHUNK)
-        near[pl.ds(start, CHUNK), :] = tree([ref[here, :] for ref in sums], jnp.add)
-
-    over(near.shape[0], CHUNK, finish, 2)
+    for i in range(4):
+
+        def finish(start):
+            first = i * quarter + start
+            here = pl.ds(SUBLANES + first, CHUNK)
+            near[pl.ds(first, CHUNK), :] = tree([ref[here, :] for ref in sums], jnp.add)
+
+        over(quarter, CHUNK, finish)
+        stores[1 + i].start()
+    for copy in stores:
+        copy.wait()
 
 
 def last_kernel(
@@ -1139,7 +1178,6 @@
     grad_near2_in,
     known1_in,
     from_own,
-    from_near,
     norm1,
     whole1,
     whole2,
@@ -1345,7 +1383,7 @@
     sum1.finish()
     sum2.finish()
     swap.wait()
-    from_near[...] = arrived[...]
+    from_own[...] += arrived[...]
     sum1.back.wait()
     whole1[...] = all1[...]
     sum2.back.wait()
@@ -1354,7 +1392,6 @@
 
 def finish_kernel(
     from_own,
-    from_near,
     norm1,
     whole1,
     whole2,
@@ -1370,7 +1407,7 @@
     grad_bias2,
 ):
     pooled[...] = pooled_in[...]
-    grad_features[...] = from_own[...] + from_near[...]
+    grad_features[...] = from_own[...]
     cores, chips = whole1.shape[:2]
     cin = from_own.shape[0]
     size1 = -(-2 * cin // (cores * chips))
@@ -1575,13 +1612,16 @@
             functools.partial(scatter1_kernel, depth),
             out_shape=[shaped(both, width1), shaped(points, width1), shaped(2, width1)],
             in_specs=[ANY] * 2 + [VMEM] * 6,
-            out_specs=[VMEM] * 3,
+            out_specs=[ANY] * 2 + [VMEM],
             scratch_shapes=[
+                scratch(both, width1),
+                scratch(points, width1),
                 pltpu.SMEM((depth * points,), jnp.int32),
                 scratch(points, width1),
                 ring,
                 pltpu.SemaphoreType.DMA((1,)),
                 pltpu.SemaphoreType.DMA((3,)),
+                pltpu.SemaphoreType.DMA((5,)),
             ]
             + [scratch(both + 2 * SUBLANES, LANES)] * (SUBLANES * 2),
             compiler_params=pltpu.CompilerParams(vmem_limit_bytes=MEMORY),
@@ -1592,17 +1632,16 @@
         size2 = -(-4 * LANES // (total * SUBLANES)) * SUBLANES
         stacked1 = -(-3 * size1 // SUBLANES) * SUBLANES
         padded1 = -(-size1 // SUBLANES) * SUBLANES
-        from_own, from_near, norm1, whole1, whole2 = pl.pallas_call(
+        from_own, norm1, whole1, whole2 = pl.pallas_call(
             functools.partial(last_kernel, (cores, chips), depth),
             out_shape=[
-                shaped(cin, points),
                 shaped(cin, points),
                 shaped(2, width1),
                 shaped(cores, chips, padded1, LANES),
                 shaped(cores, chips, size2, LANES),
             ],
             in_specs=[ANY] * 2 + [VMEM] + [ANY] * 4 + [VMEM] * 3 + [ANY] * 3,
-            out_specs=[VMEM] * 5,
+            out_specs=[VMEM] * 4,
             scratch_shapes=[
                 scratch(both, width1),
                 scratch(points, width1),
@@ -1662,13 +1701,12 @@
                 shaped(1, width2),
                 shaped(1, width2),
             ],
-            in_specs=[VMEM] * 7,
+            in_specs=[VMEM] * 6,
             out_specs=[VMEM] * 8,
             compiler_params=pltpu.CompilerParams(vmem_limit_bytes=MEMORY),
             name="finish",
         )(
             from_own,
-            from_near,
             norm1,
             whole1,
             whole2,

time: 156 us -> 153 us (0.981)
  Pallas kernels: 150 us -> 147 us
    pallas_call x1, Pallas kernels: 85.7 us -> 82.8 us  [on_device(): pl.pallas_call(functools.partial(forward_kernel, (cores, total)), out_sha...]
where the time goes in v5:
time: 153 us
  Pallas kernels  147 us (96%)
  local copies, waits for them, and re-layouts  2.11 us (1%)
  waiting for transfers between devices  2.02 us (1%)
    pallas_call x1, Pallas kernels, on_device(): pl.pallas_call(functools.partial(forward_kernel, (cores, total)), out_sha...  82.8 us
    pallas_call x1, Pallas kernels, on_device(): pl.pallas_call(functools.partial(last_kernel, (cores, chips), depth), out...  23.3 us
    pallas_call x1, Pallas kernels, on_device(): pl.pallas_call(functools.partial(scatter2_kernel, depth), out_shape=[shap...  20.6 us
    pallas_call x1, Pallas kernels, on_device(): pl.pallas_call(functools.partial(scatter1_kernel, depth), out_shape=[shap...  18.2 us
  transfers between devices with their start and end apart: 1, of which 1 were waited for; matrix products, arithmetic and copies ran while one was open for 0% of the time, Pallas kernels for 0%

profile of v5, /device:TPU:0, one launch (start us, length us, event | category | flops | bytes accessed | tf_op | source)
XLA Modules:
  0.0 152.8 jit_solution(9016697975131634972)
XLA Ops:
  0.6 0.9 multiply_add_fusion
  1.6 0.6 reshape.63.index2_in.index_in
  2.2 0.7 reshape.62.index1_in.index_in
  2.9 82.8 %forward.1 = (f32[4,512]{1,0:T(4,128)}, f32[128,20,8,128]{3,2,1,0:T(8,128)}, f32[256,20,8,128]{3,2,1,0:T(8,128)}, f32[1024,128]{1,0:T(8,128)}, f32[1024,128]{1,0...) custom-call(f32[64,1024]{1,0:T(8,128)} %feat.1, ...), custom_call_target="tpu_custom_call" | custom-call | tf_op jit(solution)/shard_map/forward/pallas_call | solution.py:1472
  85.6 20.6 %scatter2.1 = (f32[1024,128]{1,0:T(8,128)}, f32[1024,128]{1,0:T(8,128)}, f32[128,256]{1,0:T(8,128)}) custom-call(s32[20480]{0:T(1024)} %reshape.63.index2_in.index_in, f32[256,20,8,128]{3,2,1,0:T(8,128)} %get-tuple-element.46.q_hbm, f32[2048,128]{1,0:T(8,128)} %get-tuple-element.47.push_in, f32[2048,128]{1,0:T(8,128)} %get-tuple-element.48.x2_in, ...), custom_call_target="tpu_custom_call" | custom-call | tf_op jit(solution)/shard_map/scatter2/pallas_call | solution.py:1590
  106.2 0.2 collective-permute-start
  106.4 2.0 %collective-permute-done.other = f32[1024,128]{1,0:T(8,128)S(1)} collective-permute-done((f32[1024,128]{1,0:T(8,128)}, f32[1024,128]{1,0:T(8,128)S(1)}, u32[]{:S(2)}, u32[]{:S(2)}) %collective-permute-start) | collective-permute-done | bytes 524320 | tf_op jit(solution)/shard_map/ppermute | solution.py:1609
  108.4 0.0 copy-start
  108.4 0.8 copy-done
  109.2 18.2 %scatter1.1 = (f32[2048,128]{1,0:T(8,128)}, f32[1024,128]{1,0:T(8,128)}, f32[2,128]{1,0:T(2,128)}) custom-call(s32[20480]{0:T(1024)} %reshape.62.index1_in.index_in, f32[128,20,8,128]{3,2,1,0:T(8,128)} %get-tuple-element.44.q_hbm, f32[1024,128]{1,0:T(8,128)} %get-tuple-element.45.own, f32[1024,128]{1,0:T(8,128)} %get-tuple-element.51.kept, ...), custom_call_target="tpu_custom_call" | custom-call | tf_op jit(solution)/shard_map/scatter1/pallas_call | solution.py:1611
  127.4 23.3 %last.1 = (f32[64,1024]{1,0:T(8,128)}, f32[2,128]{1,0:T(2,128)}, f32[2,16,8,128]{3,2,1,0:T(8,128)}, f32[2,16,16,128]{3,2,1,0:T(8,128)}) custom-call(f32[2048,128]{1,0:T(8,128)} %get-tuple-element.56.near1_in, f32[1024,128]{1,0:T(8,128)} %get-tuple-element.57.given1_in, f32[2,128]{1,0:T(2,128)} %get-tuple-element.58.parts, ...), custom_call_target="tpu_custom_call" | custom-call | tf_op jit(solution)/shard_map/last/pallas_call | solution.py:1635
  150.8 2.0 %finish.1 = (f32[4,512]{1,0:T(4,128)}, f32[64,1024]{1,0:T(8,128)}, f32[128,128]{1,0:T(8,128)}, f32[1,128]{1,0:T(1,128)}, f32[1,128]{1,0:T(1,128)}, /*index=5*/f3...) custom-call(f32[64,1024]{1,0:T(8,128)} %get-tuple-element.67.from_own, f32[2,128]{1,0:T(2,128)} %get-tuple-element.68.norm1, ...), custom_call_target="tpu_custom_call" | custom-call | tf_op jit(solution)/shard_map/finish/pallas_call | solution.py:1692
  (1 shorter events, 0.0 us)
Async XLA Ops:
  106.2 2.2 %collective-permute-start = (f32[1024,128]{1,0:T(8,128)}, f32[1024,128]{1,0:T(8,128)S(1)}, u32[]{:S(2)}, u32[]{:S(2)}) collective-permute-start(f32[1024,128]{1,0:T(8,128)} %get-tuple-element.52), channel_id=1, source_target_pairs={{0,1},{1,0},{2,3},{3,2},{4,5},{5,4},{6,7},{7,6},{8,9},{9,8},{10,11... | collective-permute-start | bytes 1572872 | tf_op jit(solution)/shard_map/ppermute | solution.py:1609
  108.4 0.8 copy-start

commit v6 on v5

--- a/solution.py
+++ b/solution.py
@@ -326,8 +326,7 @@
     feat,
     near,
     mask,
-    index1_in,
-    index2_in,
+    indices,
     lengths,
     weight1,
     gain1,
@@ -421,7 +420,11 @@
     loads = [
         pltpu.make_async_copy(source, target, load_sems.at[i])
         for i, (source, target) in enumerate(
-            ((index1_in, index1), (index2_in, index2), (weight2_in, weight2))
+            (
+                (indices.at[pl.ds(0, depth * points)], index1),
+                (indices.at[pl.ds(depth * points, depth * points)], index2),
+                (weight2_in, weight2),
+            )
         )
     ]
     for copy in loads:
@@ -1000,7 +1003,7 @@
         pull(b).wait()
         slot = lax.rem(b, slots)
 
-        def one_group(place, inner):
+        def one_group(place):
             group = b * block + place
             rows = pl.ds(pl.multiple_of(group * SUBLANES, SUBLANES), SUBLANES)
             given = push[rows, :]
@@ -1011,9 +1014,13 @@
                     j = index.at[pl.ds((k * per + i) * groups, groups)][group]
                     target = sums[i * ways + k % ways].at[pl.ds(j, SUBLANES), :]
                     pltpu.store(target, target[...] + value, mask=mine[i])
+
+        def two_groups(t, inner):
+            for u in range(2):
+                one_group(t * 2 + u)
             return inner
 
-        lax.fori_loop(0, block, one_group, 0)
+        lax.fori_loop(0, block // 2, two_groups, 0)
         return carry
 
     lax.fori_loop(0, blocks, one_block, 0)
@@ -1059,7 +1066,7 @@
     loads = [
         pltpu.make_async_copy(source, target, load_sems.at[i])
         for i, (source, target) in enumerate(
-            ((index_in, index), (push_in, push), (x2_in, x2), (weight_in, weight), (extra_in, extra))
+            ((index_in.at[pl.ds(index.shape[0], index.shape[0])], index), (push_in, push), (x2_in, x2), (weight_in, weight), (extra_in, extra))
         )
     ]
 
@@ -1118,7 +1125,8 @@
     store_sems,
     *sums,
 ):
-    load = pltpu.make_async_copy(index_in, index, load_sems.at[0])
+    first_half = index_in.at[pl.ds(0, index.shape[0])]
+    load = pltpu.make_async_copy(first_half, index, load_sems.at[0])
     load.start()
     quarter = near.shape[0] // 4
     stores = [pltpu.make_async_copy(given, given_out, store_sems.at[0])]
@@ -1465,9 +1473,9 @@
 
         def layout(subs, groups):
             place = jnp.arange(points, dtype=jnp.int32) // groups
-            return (neighbours * subs + (SUBLANES - subs * place)).reshape(-1)
-
-        index1, index2 = layout(1, groups1), layout(2, groups2)
+            return neighbours * subs + (SUBLANES - subs * place)
+
+        indices = jnp.concatenate([layout(1, groups1), layout(2, groups2)]).reshape(-1)
         block = 32
         outs = pl.pallas_call(
             functools.partial(forward_kernel, (cores, total)),
@@ -1491,7 +1499,7 @@
                 shaped(SUBLANES, width2),
                 shaped(2, 2 * cin, width1),
             ],
-            in_specs=[VMEM] * 3 + [ANY] * 2 + [SMEM] + [VMEM] * 3 + [ANY] + [VMEM] * 3,
+            in_specs=[VMEM] * 3 + [ANY] + [SMEM] + [VMEM] * 3 + [ANY] + [VMEM] * 3,
             out_specs=[VMEM] + [ANY] * 12 + [VMEM] * 5,
             scratch_shapes=[
                 scratch(2 * points, LANES),
@@ -1554,8 +1562,7 @@
             features,
             neighbours,
             mask_row,
-            index1,
-            index2,
+            indices,
             lengths,
             first_layer_weight,
             first_norm_gain[None, :],
@@ -1605,7 +1612,7 @@
             + [scratch(2 * both + 2 * SUBLANES, LANES)] * 12,
             compiler_params=pltpu.CompilerParams(vmem_limit_bytes=MEMORY),
             name="scatter2",
-        )(index2, q2, push2, x2, second_layer_weight, scales2, extra2)
+        )(indices, q2, push2, x2, second_layer_weight, scales2, extra2)
         other = lax.ppermute(sent, "points", [(0, 1), (1, 0)])
 
         near1, given1, parts = pl.pallas_call(
@@ -1626,7 +1633,7 @@
             + [scratch(both + 2 * SUBLANES, LANES)] * (SUBLANES * 2),
             compiler_params=pltpu.CompilerParams(vmem_limit_bytes=MEMORY),
             name="scatter1",
-        )(index1, q1, own2, kept, other, inverse1, share1, moment1)
+        )(indices, q1, own2, kept, other, inverse1, share1, moment1)
 
         size1 = -(-2 * cin // total)
         size2 = -(-4 * LANES // (total * SUBLANES)) * SUBLANES

time: 153 us -> 152 us (level)
  no operation moved by 1% of the time
where the time goes in v6:
time: 152 us
  Pallas kernels  147 us (97%)
  waiting for transfers between devices  2.01 us (1%)
    pallas_call x1, Pallas kernels, on_device(): pl.pallas_call(functools.partial(forward_kernel, (cores, total)), out_sha...  82.8 us
    pallas_call x1, Pallas kernels, on_device(): pl.pallas_call(functools.partial(last_kernel, (cores, chips), depth), out...  23.3 us
    pallas_call x1, Pallas kernels, on_device(): pl.pallas_call(functools.partial(scatter2_kernel, depth), out_shape=[shap...  20.3 us
    pallas_call x1, Pallas kernels, on_device(): pl.pallas_call(functools.partial(scatter1_kernel, depth), out_shape=[shap...  18.2 us
  transfers between devices with their start and end apart: 1, of which 1 were waited for; matrix products, arithmetic and copies ran while one was open for 0% of the time, Pallas kernels for 0%

profile of v6, /device:TPU:0, one launch (start us, length us, event | category | flops | bytes accessed | tf_op | source)
XLA Modules:
  0.0 152.0 jit_solution(1093267101275303347)
XLA Ops:
  0.6 0.9 broadcast_add_fusion
  1.6 0.7 copy.19
  2.3 82.8 %forward.1 = (f32[4,512]{1,0:T(4,128)}, f32[128,20,8,128]{3,2,1,0:T(8,128)}, f32[256,20,8,128]{3,2,1,0:T(8,128)}, f32[1024,128]{1,0:T(8,128)}, f32[1024,128]{1,0...) custom-call(f32[64,1024]{1,0:T(8,128)} %feat.1, ...), custom_call_target="tpu_custom_call" | custom-call | tf_op jit(solution)/shard_map/forward/pallas_call | solution.py:1480
  85.1 20.3 %scatter2.1 = (f32[1024,128]{1,0:T(8,128)}, f32[1024,128]{1,0:T(8,128)}, f32[128,256]{1,0:T(8,128)}) custom-call(s32[40960]{0:T(1024)} %bitcast.13, f32[256,20,8,128]{3,2,1,0:T(8,128)} %get-tuple-element.46.q_hbm, f32[2048,128]{1,0:T(8,128)} %get-tuple-element.47.push_in, f32[2048,128]{1,0:T(8,128)} %get-tuple-element.48.x2_in, f32[256,256]{1,0:T(8,128)} %weight_in.1, ...), custom_call_target="tpu_custom_call" | custom-call | tf_op jit(solution)/shard_map/scatter2/pallas_call | solution.py:1597
  105.4 0.2 collective-permute-start
  105.6 2.0 %collective-permute-done.other = f32[1024,128]{1,0:T(8,128)S(1)} collective-permute-done((f32[1024,128]{1,0:T(8,128)}, f32[1024,128]{1,0:T(8,128)S(1)}, u32[]{:S(2)}, u32[]{:S(2)}) %collective-permute-start) | collective-permute-done | bytes 524320 | tf_op jit(solution)/shard_map/ppermute | solution.py:1616
  107.6 0.0 copy-start
  107.6 0.8 copy-done
  108.4 18.2 %scatter1.1 = (f32[2048,128]{1,0:T(8,128)}, f32[1024,128]{1,0:T(8,128)}, f32[2,128]{1,0:T(2,128)}) custom-call(s32[40960]{0:T(1024)} %bitcast.14, f32[128,20,8,128]{3,2,1,0:T(8,128)} %get-tuple-element.44.q_hbm, f32[1024,128]{1,0:T(8,128)} %get-tuple-element.45.own, f32[1024,128]{1,0:T(8,128)} %get-tuple-element.51.kept, f32[1024,128]{1,0:T(8,128)} %copy-done, ...), custom_call_target="tpu_custom_call" | custom-call | tf_op jit(solution)/shard_map/scatter1/pallas_call | solution.py:1618
  126.6 23.3 %last.1 = (f32[64,1024]{1,0:T(8,128)}, f32[2,128]{1,0:T(2,128)}, f32[2,16,8,128]{3,2,1,0:T(8,128)}, f32[2,16,16,128]{3,2,1,0:T(8,128)}) custom-call(f32[2048,128]{1,0:T(8,128)} %get-tuple-element.56.near1_in, f32[1024,128]{1,0:T(8,128)} %get-tuple-element.57.given1_in, f32[2,128]{1,0:T(2,128)} %get-tuple-element.58.parts, ...), custom_call_target="tpu_custom_call" | custom-call | tf_op jit(solution)/shard_map/last/pallas_call | solution.py:1642
  150.0 2.0 %finish.1 = (f32[4,512]{1,0:T(4,128)}, f32[64,1024]{1,0:T(8,128)}, f32[128,128]{1,0:T(8,128)}, f32[1,128]{1,0:T(1,128)}, f32[1,128]{1,0:T(1,128)}, /*index=5*/f3...) custom-call(f32[64,1024]{1,0:T(8,128)} %get-tuple-element.67.from_own, f32[2,128]{1,0:T(2,128)} %get-tuple-element.68.norm1, ...), custom_call_target="tpu_custom_call" | custom-call | tf_op jit(solution)/shard_map/finish/pallas_call | solution.py:1699
  (2 shorter events, 0.0 us)
Async XLA Ops:
  105.4 2.2 %collective-permute-start = (f32[1024,128]{1,0:T(8,128)}, f32[1024,128]{1,0:T(8,128)S(1)}, u32[]{:S(2)}, u32[]{:S(2)}) collective-permute-start(f32[1024,128]{1,0:T(8,128)} %get-tuple-element.52), channel_id=1, source_target_pairs={{0,1},{1,0},{2,3},{3,2},{4,5},{5,4},{6,7},{7,6},{8,9},{9,8},{10,11... | collective-permute-start | bytes 1572872 | tf_op jit(solution)/shard_map/ppermute | solution.py:1616
  107.6 0.8 copy-start
